TPU v7x, 256 devices: a whole 4x4x8 slice. The times are simulated.
256 devices in a mesh: ctx: 32 (over y_hi, z, core), dp: 8 (over y_lo, x).
Axes of the slice: x: 4, y: 4 (y_hi: 2, y_lo: 2; y = y_hi * 2 + y_lo), z: 8, core: 2. Of those that a mesh axis runs over, the one named last changes fastest.
Arguments:
- inputs: bfloat16 [8, 4096, 2048], P('dp', 'ctx'), may hold values from -6 to 6
- gate_weight: bfloat16 [256, 2, 8, 256], P('ctx'), may hold values from -0.375 to 0.375
- gate_bias: float32 [2, 2048], replicated, may hold values from -4 to 4
- decay_param: float32 [2048], replicated, may hold values from 4 to 14
- conv_weight: float32 [4, 2048], replicated, may hold values from -3 to 3
- conv_bias: float32 [2048], replicated, may hold values from -3 to 3
- cotangent: bfloat16 [8, 4096, 2048], P('dp', 'ctx'), may hold values from -6 to 6
Outputs:
- grad_input: bfloat16 [8, 4096, 2048], P('dp', 'ctx')
- grad_gate_weight: float32 [256, 2, 8, 256], P('ctx')
- grad_decay: float32 [2048], replicated
- grad_gate_bias: float32 [2, 2048], replicated
- grad_conv_weight: float32 [4, 2048], replicated
- grad_conv_bias: float32 [2048], replicated
All inputs are finite; a program needn't handle non-finite values.
Results may differ from a plain program's by a relative error of at most 0.015.
Values may be sent and summed in bfloat16 or wider, within the bound.
A program may use at most 64 MiB of HBM per device.

v0:
```python
import jax
import jax.numpy as jnp
from jax import lax
from jax.sharding import PartitionSpec as P


def from_behind(x, axis, by):
    peers = lax.axis_size(axis)
    pairs = [(i, i + by) for i in range(peers) if 0 <= i + by < peers]
    return lax.ppermute(x, axis, pairs)


def prefix(value, axis, join, neutral, backward):
    count, mine = (lax.axis_size(axis), lax.axis_index(axis))
    pieces = jax.tree.map(lambda part: lax.all_gather(part, axis), value)
    if backward:
        pieces = jax.tree.map(lambda part: part[::-1], pieces)
        mine = count - 1 - mine
    subtotal = jax.tree.map(
        lambda part, zero: jnp.full_like(part, 0) + jnp.asarray(zero, part.dtype), value, neutral
    )

    def hop(position, subtotal):
        longer = join(subtotal, jax.tree.map(lambda part: part[position], pieces))
        return jax.tree.map(lambda new, old: jnp.where(position < mine, new, old), longer, subtotal)

    return lax.fori_loop(0, count - 1, hop, subtotal)


def affine(first, second):
    return (first[0] * second[0], second[0] * first[1] + second[1])


def triangles(span):
    row_ids = lax.broadcasted_iota(jnp.int32, (span, span), 0)
    col_ids = lax.broadcasted_iota(jnp.int32, (span, span), 1)
    lower_tri = (col_ids <= row_ids).astype(jnp.float32)
    return (lower_tri, lower_tri.T)


def run_sum(tri_matrix, values):
    return jnp.einsum("ts,nsw->ntw", tri_matrix, values, precision=lax.Precision.HIGHEST)


def local_chains(log_decay, decay, drive, upstream):
    seqs, rows, width = log_decay.shape
    span = min(rows, 128)
    count = rows // span
    lower_tri, upper_tri = triangles(span)
    a_carry = jnp.ones((seqs, width), jnp.float32)
    h_carry = jnp.zeros((seqs, width), jnp.float32)
    growths, shrinks, cum_parts, hid_parts = ([], [], [], [])
    number = 0
    start = number * span
    cum_log = run_sum(lower_tri, log_decay)
    growth = jnp.exp(cum_log)
    shrink_part = jnp.exp(-cum_log)
    inner_sum = growth * run_sum(lower_tri, shrink_part * drive) + growth * h_carry[:, None]
    cum_parts.append(growth * a_carry[:, None])
    hid_parts.append(inner_sum)
    growths.append(growth)
    shrinks.append(shrink_part)
    s_carry = jnp.ones((seqs, width), jnp.float32)
    c_carry = jnp.zeros((seqs, width), jnp.float32)
    suf_parts, grad_parts = ([], [])
    for number in reversed(range(count)):
        start = number * span
        growth = growths[number]
        shrink_part = shrinks[number]
        tail_part = growth[:, span - 1 : span] * shrink_part
        inner_sum = (
            shrink_part * run_sum(upper_tri, growth * upstream) + tail_part * c_carry[:, None]
        )
        suf_parts.insert(0, tail_part * s_carry[:, None])
        grad_parts.insert(0, inner_sum)
        s_carry = s_carry * growth[:, span - 1]
        c_carry = decay[:, start] * inner_sum[:, 0]
    return (cum_parts[0], hid_parts[0], suf_parts[0], grad_parts[0])


def per_device(inputs, gate_weight, gate_bias, decay_param, conv_weight, conv_bias, cotangent):
    seqs, rows, width = inputs.shape
    blocks = gate_weight.shape[2]
    block_w = gate_weight.shape[3]
    taps = conv_weight.shape[0]
    previous = from_behind(inputs[:, rows - taps + 1 :, :], "ctx", 1)
    extended = jnp.concatenate([previous, inputs], 1).astype(jnp.float32)
    mixed = conv_bias + conv_weight[0] * extended[:, 0:rows]
    for k in range(1, taps):
        mixed = mixed + conv_weight[k] * extended[:, k : k + rows]
    mixed_half = mixed.astype(jnp.bfloat16)
    mixed_full = mixed_half.astype(jnp.float32)
    x_blocks = mixed_half.reshape(seqs, rows, blocks, block_w)
    whole_weight = lax.all_gather(gate_weight, "ctx", axis=0, tiled=True)
    pre = jnp.einsum("stbi,icbj->stcbj", x_blocks, whole_weight, preferred_element_type=jnp.float32)
    gate_a = jax.nn.sigmoid(pre[:, :, 0].reshape(seqs, rows, width) + gate_bias[0])
    gate_x = jax.nn.sigmoid(pre[:, :, 1].reshape(seqs, rows, width) + gate_bias[1])
    rate = jax.nn.softplus(-decay_param)
    log_decay = -8.0 * gate_a * rate
    decay = jnp.exp(log_decay)
    square = 1.0 - decay * decay
    mult = jnp.sqrt(square)
    drive = mult * gate_x * mixed_full
    upstream = cotangent.astype(jnp.float32)
    cum_a, local_h, suffix, local_g = local_chains(log_decay, decay, drive, upstream)
    total_a = cum_a[:, rows - 1]
    local_end = local_h[:, rows - 1]
    head = decay[:, 0] * local_g[:, 0]
    ones = jnp.ones((seqs, width), jnp.float32)
    zeros = jnp.zeros((seqs, width), jnp.float32)
    state_in = prefix((total_a, local_end), "ctx", affine, (ones, zeros), False)[1]
    carry_in = prefix((total_a, head), "ctx", affine, (ones, zeros), True)[1]
    hidden = local_h + cum_a * state_in[:, None]
    hidden_prev = jnp.concatenate([state_in[:, None], hidden[:, : rows - 1]], 1)
    grad_h = local_g + suffix * carry_in[:, None]
    grad_log = (
        decay
        * grad_h
        * (hidden_prev - gate_x * mixed_full * decay / jnp.sqrt(jnp.maximum(square, 0.05)))
    )
    grad_pre_a = grad_log * (-8.0 * rate) * gate_a * (1.0 - gate_a)
    grad_pre_x = grad_h * mult * mixed_full * gate_x * (1.0 - gate_x)
    grad_pre = jnp.stack(
        [
            grad_pre_a.reshape(seqs, rows, blocks, block_w),
            grad_pre_x.reshape(seqs, rows, blocks, block_w),
        ],
        2,
    ).astype(jnp.bfloat16)
    lam_part = jnp.sum(grad_log * 8.0 * gate_a, axis=(0, 1)) * jax.nn.sigmoid(-decay_param)
    bias_part = jnp.stack([jnp.sum(grad_pre_a, axis=(0, 1)), jnp.sum(grad_pre_x, axis=(0, 1))], 0)
    back_blocks = jnp.einsum(
        "stcbj,icbj->stbi", grad_pre, whole_weight, preferred_element_type=jnp.float32
    )
    grad_mixed = grad_h * mult * gate_x + back_blocks.reshape(seqs, rows, width)
    weight_part = lax.psum_scatter(
        jnp.einsum(
            "stbi,stcbj->icbj", x_blocks, grad_pre, preferred_element_type=jnp.float32
        ).astype(jnp.bfloat16),
        "ctx",
        scatter_dimension=0,
        tiled=True,
    ).astype(jnp.float32)
    taps_part = jnp.stack(
        [jnp.sum(grad_mixed * extended[:, k : k + rows], axis=(0, 1)) for k in range(taps)], 0
    )
    shift_part = jnp.sum(grad_mixed, axis=(0, 1))
    following = from_behind(grad_mixed[:, 0 : taps - 1], "ctx", -1)
    padded = jnp.concatenate([grad_mixed, following], 1)
    back = conv_weight[0] * padded[:, taps - 1 : taps - 1 + rows]
    for k in range(1, taps):
        back = back + conv_weight[k] * padded[:, taps - 1 - k : taps - 1 - k + rows]
    grad_input = back.astype(jnp.bfloat16)
    grad_weight = lax.psum(weight_part, "dp")
    grad_decay, grad_bias, grad_taps, grad_shift = lax.psum(
        (lam_part, bias_part, taps_part, shift_part), ("ctx", "dp")
    )
    return (grad_input, grad_weight, grad_decay, grad_bias, grad_taps, grad_shift)


def solution(mesh):
    placed = (
        P("dp", "ctx", None),
        P("ctx", None, None, None),
        P(),
        P(),
        P(),
        P(),
        P("dp", "ctx", None),
    )
    return jax.shard_map(
        per_device,
        mesh=mesh,
        in_specs=placed,
        out_specs=(P("dp", "ctx", None), P("ctx", None, None, None), P(), P(), P(), P()),
        check_vma=False,
    )
```

profile of v0, /device:TPU:1, one launch (start us, length us, event | category | flops | bytes accessed | tf_op | source)
XLA Modules:
  0.0 668.4 jit_solution(1838865229373659059)
XLA Ops:
  7.2 1.5 copy.34
  9.6 4.9 collective-permute-start
  20.3 72.2 %all-gather.2.cloned.1.call-done = bf16[256,2,8,256]{3,0,1,2:T(8,128)(2,1)} async-done(((bf16[8,2,8,256]{3,0,1,2:T(8,128)(2,1)}), bf16[256,2,8,256]{3,0,1,2:T(8,128)(2,1)}) %all-gather.2.cloned.1.call-update) | async-done | bytes 2097168 | tf_op jit(solution)/shard_map/all_gather | solution.py:94
  92.5 2.0 convolution_bitcast_fusion.2
  94.6 1.4 fusion.45
  96.0 1.5 copy.36
  97.9 2.5 copy.39
  100.5 2.6 copy.40
  105.7 39.6 %all_gather.15 = f32[32,1,2048]{2,1,0:T(1,128)S(1)} all-gather(f32[1,1,2048]{2,1,0:T(1,128)S(1)} %slice.105), channel_id=1, replica_groups=mesh['ctx'=32,'dp'=8] {'ctx'}, dimensions={0}, use_global_device_ids=true | all-gather | bytes 270336 | tf_op jit(solution)/shard_map/all_gather | solution.py:15
  145.3 1.5 multiply_exponential_fusion
  146.8 1.8 fusion.2
  149.5 40.1 %all_gather.17 = f32[32,1,2048]{2,1,0:T(1,128)} all-gather(f32[1,1,2048]{2,1,0:T(1,128)S(1)} %slice.109), channel_id=1, replica_groups=mesh['ctx'=32,'dp'=8] {'ctx'}, dimensions={0}, use_global_device_ids=true | all-gather | bytes 270336 | tf_op jit(solution)/shard_map/all_gather | solution.py:15
  190.3 23.0 %while.29 = (s32[]{:T(128)}, f32[1,2048]{1,0:T(1,128)S(1)}, s32[]{:T(128)}, f32[32,1,2048]{2,1,0:T(1,128)S(1)}, f32[32,1,2048]{2,1,0:T(1,128)}, /*index=5*/s32[]{:T(128)}, s32[]{:T(128)}) while((s32[]{:T(128)}, f32[1,2048]{1,0:T(1,128)S(1)}, s32[]{:T(128)}, f32[32,1,2048]{2,1,0:T(1,128)S(1)}, f32[32,1,2048]{2,1,0:T(1,128)}, ...), condition=%wide.region_3.4_spmd.clone, body=%wide.region_2.3_spmd.clone.sunk | while | flops 8196 | bytes 32877 | solution.py:27
  213.4 2.7 slice_add_fusion
  219.0 38.9 %all_gather.16 = f32[32,1,2048]{2,1,0:T(1,128)S(1)} all-gather(f32[1,1,2048]{2,1,0:T(1,128)S(1)} %slice_multiply_fusion.1), channel_id=1, replica_groups=mesh['ctx'=32,'dp'=8] {'ctx'}, dimensions={0}, use_global_device_ids=true | all-gather | bytes 270336 | tf_op jit(solution)/shard_map/all_gather | solution.py:15
  258.7 23.7 %while.28 = (s32[]{:T(128)}, f32[1,2048]{1,0:T(1,128)S(1)}, s32[]{:T(128)}, f32[32,1,2048]{2,1,0:T(1,128)}, f32[32,1,2048]{2,1,0:T(1,128)}, /*index=5*/s32[]{:T(128)}, s32[]{:T(128)}) while((s32[]{:T(128)}, f32[1,2048]{1,0:T(1,128)S(1)}, s32[]{:T(128)}, f32[32,1,2048]{2,1,0:T(1,128)}, f32[32,1,2048]{2,1,0:T(1,128)}, ...), condition=%wide.region_1.2_spmd.clone, body=%wide.region_0.1_spmd.clone.sunk | while | flops 8196 | bytes 32877 | solution.py:27
  282.4 3.3 fusion.42
  285.8 1.7 fusion.37
  288.8 2.1 convert_bitcast_fusion
  290.9 4.5 copy.46
  295.5 2.4 convolution_bitcast_fusion.3
  299.5 2.0 multiply_reduce_fusion.3
  301.5 2.1 collective-permute-start.1
  305.5 1.2 collective-permute-done.1
  306.7 1.3 fusion.8
  308.0 97.3 %reduce-scatter.2.cloned.1.call-done = bf16[8,2,8,256]{3,2,1,0:T(8,128)(2,1)} async-done(((bf16[256,2,8,256]{3,2,1,0:T(8,128)(2,1)}), bf16[8,2,8,256]{3,2,1,0:T(8,128)(2,1)}) %reduce-scatter.2.cloned.1.call-update) | async-done | bytes 65552 | tf_op jit(solution)/shard_map/reduce_scatter | solution.py:136
  405.3 28.4 %all-reduce.5 = f32[8,2,8,256]{3,2,1,0:T(8,128)} all-reduce(bf16[8,2,8,256]{3,2,1,0:T(8,128)(2,1)} %reduce-scatter.2.cloned.1.call-done), channel_id=1, replica_groups=mesh['ctx'=32,'dp'=8] {'dp'}, use_global_device_ids=true, to_apply=%region_5.6 | all-reduce | flops 32768 | bytes 196608 | tf_op jit(solution)/shard_map/psum | solution.py:154
  433.7 222.8 %all-reduce.4.cloned.1.call-done = (f32[2048]{0:T(1024)}, f32[2,2048]{1,0:T(2,128)}, f32[4,2048]{1,0:T(4,128)}, f32[2048]{0:T(1024)}) async-done(((f32[2048]{0:T(1024)}, f32[2,2048]{1,0:T(2,128)}, f32[4,2048]{1,0:T(4,128)}, f32[2048]{0:T(1024)}), (f32[2048]{0:T(1024)}, f32[2,2048]{1,0:T(2,128)}, f32[4,2048]{1,0:T(4,128)}, f32[2048]{0:T(1024)})) %all-reduce.4.cloned.1.call-update) | async-done | bytes 65552 | tf_op jit(solution)/shard_map/psum | solution.py:155
  656.6 1.3 copy.84
  657.8 1.3 copy.85
  659.2 1.4 copy.86
  660.5 1.3 copy.87
  (130 shorter events, 65.3 us)
Async XLA Ops:
  7.2 85.4 %all-gather.2.cloned.1.call-start = ((), (), s32[]{:S(2)}) async-start(), calls=%async_computation.1 | async-start | bytes 2162688 | tf_op jit(solution)/shard_map/all_gather | solution.py:94
  8.7 396.6 %reduce-scatter.2.cloned.1.call-start = ((), (), s32[]{:S(2)}) async-start(), calls=%async_computation.2 | async-start | bytes 2162688 | tf_op jit(solution)/shard_map/reduce_scatter | solution.py:136
  9.6 7.5 %collective-permute-start = (bf16[1,3,2048]{2,1,0:T(4,128)(2,1)S(1)}, bf16[1,3,2048]{2,1,0:T(4,128)(2,1)S(1)}, u32[]{:S(2)}, u32[]{:S(2)}) collective-permute-start(bf16[1,3,2048]{2,1,0:T(4,128)(2,1)S(1)} %slice.78), channel_id=1, source_target_pairs={{0,8},{8,16},{16,24},{24,32},{32,40},{40,48},{48,56},{56,64},{64,7... | collective-permute-start | bytes 36872 | tf_op jit(solution)/shard_map/ppermute | solution.py:10
  19.4 0.8 copy-start.10
  20.3 74.3 %copy-start.5 = (bf16[16,8,8,256]{3,2,1,0:T(8,128)(2,1)}, bf16[16,8,8,256]{3,2,1,0:T(8,128)(2,1)S(1)}, u32[]{:S(2)}) copy-start(bf16[16,8,8,256]{3,2,1,0:T(8,128)(2,1)S(1)} %copy.56) | copy-start | bytes 1572868
  104.5 42.3 %copy-start = (f32[1,128,2048]{2,1,0:T(8,128)S(1)}, f32[1,128,2048]{2,1,0:T(8,128)}, u32[]{:S(2)}) copy-start(f32[1,128,2048]{2,1,0:T(8,128)} %copy.40) | copy-start | bytes 3145732
  104.5 42.3 %copy-start.11 = (bf16[1,128,2048]{2,1,0:T(8,128)(2,1)S(1)}, bf16[1,128,2048]{2,1,0:T(8,128)(2,1)}, u32[]{:S(2)}) copy-start(bf16[1,128,2048]{2,1,0:T(8,128)(2,1)} %copy-done.10) | copy-start | bytes 1572868
  104.7 1.0 copy-start.7
  148.6 1.0 copy-start.12
  213.4 2.7 copy-start.13
  217.2 1.0 copy-start.8
  282.4 3.4 copy-start.1
  282.4 3.4 copy-start.9
  282.4 3.4 copy-start.14
  285.7 1.7 copy-start.3
  287.8 1.0 copy-start.6
  295.5 361.1 %all-reduce.4.cloned.1.call-start = ((), (), s32[]{:S(2)}) async-start(), calls=%async_computation.3 | async-start | bytes 131072 | tf_op jit(solution)/shard_map/psum | solution.py:155
  297.9 1.2 copy-start.2
  297.9 1.5 copy-start.4
  299.5 4.1 copy-start.15
  301.5 5.2 collective-permute-start.1
Sparse Core Ops, SparseCore 0:
  11.1 81.3 all-gather.1
  295.6 109.6 reduce-scatter.1
  413.1 243.3 all-reduce.3
where the time goes:
time: 675 us; the launch traced here: 668 us
  waiting for transfers between devices  394 us (58%)
  blocking collectives  147 us (22%)
  other arithmetic  65 us (10%)
  local copies, waits for them, and re-layouts  30.3 us (4%)
  between operations  14.1 us (2%)
  matrix products  10 us (1%)
  starting transfers between devices  7.12 us (1%)
    psum x1, waiting for transfers between devices, per_device(): lax.psum((lam_part, bias_part, taps_part, shift_part), ('ctx', 'dp'))  223 us
    all_gather x3, blocking collectives, prefix(): pieces = jax.tree.map(lambda part: lax.all_gather(part, axis), value)  119 us
    reduce_scatter x1, waiting for transfers between devices, per_device(): lax.psum_scatter(jnp.einsum('stbi,stcbj->icbj', x_blocks, grad_pre, prefe...  97.3 us
    all_gather x1, waiting for transfers between devices, per_device(): whole_weight = lax.all_gather(gate_weight, 'ctx', axis=0, tiled=True)  72.2 us
    select_n x62, other arithmetic, hop(): jnp.where(position < mine, new, old)  45.6 us
    psum x1, blocking collectives, per_device(): grad_weight = lax.psum(weight_part, 'dp')  28.4 us
  transfers between devices with their start and end apart: 5, of which 4 were waited for; matrix products, arithmetic and copies ran while one was open for 2% of the time, Pallas kernels for 0%

commit v1 on v0

v1 whole, which is shorter than its diff:
```python
import jax
import jax.numpy as jnp
from jax import lax
from jax.experimental import pallas as pl
from jax.experimental.pallas import tpu as pltpu
from jax.sharding import PartitionSpec as P

MESH = pl.DeviceIdType.MESH
F32 = jnp.float32
BF16 = jnp.bfloat16
CHIPS = 16
REPL = 8
ROWS = 128
SPAN = 256
WIDTH = 2048
HALF = 1024
BW = 256
NB = HALF // BW
R = SPAN // 8
TILES = HALF // 128


def wait_for(ref, sem):
    pltpu.make_async_copy(ref, ref, sem).wait()


def sublane(shape):
    return lax.broadcasted_iota(jnp.int32, shape, 0)


def sigmoid(x):
    return 0.5 * jnp.tanh(0.5 * x) + 0.5


def softplus(x):
    e = jnp.exp(-jnp.abs(x))
    z = e / (2.0 + e)
    z2 = z * z
    s = jnp.full_like(z, 1.0 / 17.0)
    for n in (15, 13, 11, 9, 7, 5, 3, 1):
        s = s * z2 + 1.0 / n
    return jnp.maximum(x, 0.0) + 2.0 * z * s


def lane_tile(i):
    return slice(i * 128, (i + 1) * 128)


def block(b):
    return slice(b * BW, (b + 1) * BW)


def main_kernel(
    x_hbm, w_hbm, gb_ref, lam_ref, cw_ref, cb_ref, cot_hbm,
    gi_hbm, all_hbm,
    xb, cotb, wsh, wf, wu, wpair, W, xhalo, nat, natc, xs, cs, mb, mt, pre,
    dec, drv, qq, m1, m2, m3, oma, hp, gp, gm, tot, dsend, drecv, sin, ghs, ghr,
    wsend, frecv, own, fsum, zrecv, ssend, srecv, ssum, szrecv, G, gib,
    lsem, sib_s, sib_r, c1_s, c1_r, hal_s, hal_r, c2_s, c2_r, d_s, d_r, e_s, e_r,
    f_s, f_r, fs_s, fs_r, z_s, z_r, zs_s, zs_r, g_s, g_r,
):
    ctx = lax.axis_index("ctx")
    d = lax.axis_index("dp")
    p = ctx // 2
    c = ctx % 2
    sibling = {"ctx": 2 * p + 1 - c, "dp": d}

    def chip(j):
        return {"ctx": 2 * j + c, "dp": d}

    def peer(u):
        return {"ctx": ctx, "dp": u}

    def send(src, dst, ss, rs, dev):
        cp = pltpu.make_async_remote_copy(
            src_ref=src, dst_ref=dst, send_sem=ss, recv_sem=rs, device_id=dev, device_id_type=MESH
        )
        cp.start()
        return cp

    bar = pltpu.get_barrier_semaphore()
    pl.semaphore_signal(bar, inc=1, device_id=sibling, device_id_type=MESH)

    @pl.loop(1, CHIPS)
    def _(j):
        pl.semaphore_signal(bar, inc=1, device_id=chip((p + j) % CHIPS), device_id_type=MESH)

    @pl.loop(1, REPL)
    def _(j):
        pl.semaphore_signal(bar, inc=1, device_id=peer((d + j) % REPL), device_id_type=MESH)

    mine = pl.ds(pl.multiple_of(HALF * c, HALF), HALF)
    theirs = pl.ds(pl.multiple_of(HALF * (1 - c), HALF), HALF)
    my_rows = pl.ds(pl.multiple_of(ROWS * c, ROWS), ROWS)
    sib_rows = pl.ds(pl.multiple_of(ROWS * (1 - c), ROWS), ROWS)

    ld_w = pltpu.make_async_copy(w_hbm, wsh, lsem.at[0])
    ld_w.start()
    ld_x = pltpu.make_async_copy(x_hbm.at[0, :, mine], xb.at[my_rows], lsem.at[1])
    ld_x.start()
    ld_c = pltpu.make_async_copy(cot_hbm.at[0, :, mine], cotb.at[my_rows], lsem.at[2])
    ld_c.start()

    ld_w.wait()
    for i in range(8):
        for g in range(2):
            v = wsh[i, g].astype(F32)
            for lh in range(2):
                wf[lh, i * 16 + g * 8 : i * 16 + g * 8 + 8, :] = v[:, lane_tile(lh)]
    for h in range(2):
        for u in range(8):
            for lh in range(2):
                first = (u % 2) * 8 + 4 * h + u // 2
                wu[h, u, :, lane_tile(lh)] = wf[lh, pl.ds(first, 8, stride=16), :]

    pl.semaphore_wait(bar, 1 + (CHIPS - 1) + (REPL - 1))

    part = pl.ds(pl.multiple_of(8 * c, 8), 8)
    s_w = send(wu.at[1 - c, d], wpair.at[part], sib_s.at[0], sib_r.at[0], sibling)
    s_x = send(x_hbm.at[0, :, theirs], xb.at[my_rows], sib_s.at[1], sib_r.at[1], sibling)
    s_c = send(cot_hbm.at[0, :, theirs], cotb.at[my_rows], sib_s.at[2], sib_r.at[2], sibling)
    wpair[part, :] = wu[c, d]
    s_w.wait_recv()
    my16 = pl.ds(pl.multiple_of(16 * p, 16), 16)
    W[d, my16, :] = wpair[...].astype(BF16)

    @pl.loop(1, CHIPS)
    def _(j):
        send(W.at[d, my16], W.at[d, my16], c1_s, c1_r, chip((p + j) % CHIPS))

    ld_x.wait()
    s_x.wait_recv()
    send(xb.at[pl.ds(SPAN - 16, 16)], xhalo, hal_s, hal_r, chip((p + 1) % CHIPS))
    for k in range(TILES):
        nat[k] = xb[:, lane_tile(k)].astype(F32)

    @pl.loop(0, R)
    def _(r):
        for k in range(TILES):
            xs[3 + r, :, lane_tile(k)] = nat[k, pl.ds(r, 8, stride=R), :]

    ld_c.wait()
    s_c.wait_recv()
    for k in range(TILES):
        natc[k] = cotb[:, lane_tile(k)].astype(F32)

    @pl.loop(0, R)
    def _(r):
        for k in range(TILES):
            cs[r, :, lane_tile(k)] = natc[k, pl.ds(r, 8, stride=R), :]

    wait_for(xhalo, hal_r)
    hal = xhalo[...].astype(F32)
    hal = jnp.where(p == 0, jnp.zeros_like(hal), hal)
    sub = sublane((8, HALF))
    for k in range(3):
        rolled = pltpu.roll(xs[3 + R - 3 + k], 1, 0)
        xs[k] = jnp.where(sub == 0, jnp.broadcast_to(hal[13 + k : 14 + k], (8, HALF)), rolled)

    conv_w = cw_ref[:, mine]
    conv_b = cb_ref[:, mine]
    for b in range(NB):
        taps = [jnp.broadcast_to(conv_w[k : k + 1, block(b)], (8, BW)) for k in range(4)]
        shift = jnp.broadcast_to(conv_b[:, block(b)], (8, BW))

        @pl.loop(0, R // 2)
        def _(i):
            v = [xs[2 * i + k, :, block(b)] for k in range(5)]
            out = []
            for o in range(2):
                m = shift + taps[0] * v[o]
                for k in range(1, 4):
                    m = m + taps[k] * v[o + k]
                out.append(m)
            mb[pl.ds(pl.multiple_of(16 * i, 16), 16), block(b)] = jnp.concatenate(out, 0).astype(BF16)

        mt[b] = mb[:, block(b)].astype(F32).T.astype(BF16)

    wait_for(W.at[0, pl.ds(0, 16 * (CHIPS - 1))], c1_r)

    @pl.loop(1, REPL)
    def _(j):
        send(W.at[d], W.at[d], c2_s, c2_r.at[d], peer((d + j) % REPL))

    lam = lam_ref[:, mine]
    neg8rate = -8.0 * softplus(-lam)
    gate_b = gb_ref[:, mine]
    ends = []
    for b in range(NB):
        for u in (2 * b, 2 * b + 1):
            @pl.when(d != u)
            def _():
                wait_for(W.at[u], c2_r.at[u])

            pre[u] = jnp.dot(mb[:, block(b)], W[u], preferred_element_type=F32)
        nr = jnp.broadcast_to(neg8rate[:, block(b)], (8, BW))
        ba = jnp.broadcast_to(gate_b[0:1, block(b)], (8, BW))
        bx = jnp.broadcast_to(gate_b[1:2, block(b)], (8, BW))

        def step(i, carry):
            prod, hid, kk, logs = carry
            two = mb[pl.ds(pl.multiple_of(16 * i, 16), 16), block(b)].astype(F32)
            for o in range(2):
                r = 2 * i + o
                at = pl.ds(pl.multiple_of(8 * r, 8), 8)
                ga = sigmoid(pre[2 * b, at, :] + ba)
                gx = sigmoid(pre[2 * b + 1, at, :] + bx)
                m = two[8 * o : 8 * o + 8]
                ld = ga * nr
                a = jnp.exp(ld)
                sq = 1.0 - a * a
                mult = jnp.sqrt(sq)
                gm_ = gx * m
                drive = mult * gm_
                dec[r, :, block(b)] = a
                drv[r, :, block(b)] = drive
                qq[r, :, block(b)] = gm_ * a * lax.rsqrt(jnp.maximum(sq, 0.05))
                m1[r, :, block(b)] = a * ga
                oma[r, :, block(b)] = (1.0 - ga) * nr
                m2[r, :, block(b)] = drive * (1.0 - gx)
                m3[r, :, block(b)] = mult * gx
                hid = a * hid + drive
                prod = prod * a
                kk = kk + prod * cs[r, :, block(b)]
                logs = logs + ld
            return prod, hid, kk, logs

        zero = jnp.zeros((8, BW), F32)
        prod, hid, kk, logs = lax.fori_loop(
            0, R // 2, step, (jnp.ones((8, BW), F32), zero, zero, zero)
        )
        sb = sublane((8, BW))
        fp, fh = prod, hid
        bp, bk = prod, kk
        for s in (1, 2, 4):
            mp, mh = pltpu.roll(fp, s, 0), pltpu.roll(fh, s, 0)
            fh = jnp.where(sb >= s, fp * mh + fh, fh)
            fp = jnp.where(sb >= s, fp * mp, fp)
            mp, mk = pltpu.roll(bp, 8 - s, 0), pltpu.roll(bk, 8 - s, 0)
            bk = jnp.where(sb < 8 - s, bp * mk + bk, bk)
            bp = jnp.where(sb < 8 - s, bp * mp, bp)
            logs = logs + pltpu.roll(logs, s, 0)
        one = jnp.ones((8, BW), F32)
        ends.append((
            jnp.where(sb == 0, one, pltpu.roll(fp, 1, 0)),
            jnp.where(sb == 0, zero, pltpu.roll(fh, 1, 0)),
            jnp.where(sb == 7, one, pltpu.roll(bp, 7, 0)),
            jnp.where(sb == 7, zero, pltpu.roll(bk, 7, 0)),
        ))
        for lh in range(2):
            k = 2 * b + lh
            tot[0, k : k + 1, :] = logs[0:1, lane_tile(lh)]
            tot[1, k : k + 1, :] = fh[7:8, lane_tile(lh)]
            tot[2, k : k + 1, :] = bk[0:1, lane_tile(lh)]

    dsend[0] = jnp.concatenate([tot[0], tot[1]], 0).astype(BF16)
    dsend[1] = jnp.concatenate([tot[0], tot[2]], 0).astype(BF16)

    @pl.loop(1, CHIPS)
    def _(j):
        to = (p + j) % CHIPS
        send(dsend.at[jnp.where(to > p, 0, 1)], drecv.at[p], d_s, d_r, chip(to))

    drecv[p] = jnp.zeros((16, 128), BF16)
    wait_for(drecv.at[pl.ds(0, CHIPS - 1)], d_r)
    state = jnp.zeros((8, 128), F32)
    carry_in = jnp.zeros((8, 128), F32)
    for j in range(CHIPS):
        v = drecv[j].astype(F32)
        state = jnp.where(j < p, jnp.exp(v[:8]) * state + v[8:], state)
        v = drecv[CHIPS - 1 - j].astype(F32)
        carry_in = jnp.where(CHIPS - 1 - j > p, jnp.exp(v[:8]) * carry_in + v[8:], carry_in)
    sin[0] = state
    sin[1] = carry_in

    sums = []
    for b in range(NB):
        def wide(n):
            return jnp.concatenate(
                [jnp.broadcast_to(sin[n, 2 * b + lh : 2 * b + lh + 1, :], (8, 128)) for lh in range(2)], 1
            )

        hin = ends[b][1] + ends[b][0] * wide(0)
        kin = ends[b][3] + ends[b][2] * wide(1)

        def up(r, h):
            hp[r, :, block(b)] = h
            return dec[r, :, block(b)] * h + drv[r, :, block(b)]

        lax.fori_loop(0, R, up, hin, unroll=4)

        def down(n, carry):
            kk, st, sa, sx = carry
            i = R // 2 - 1 - n
            outs = [[None, None], [None, None]]
            for o in (1, 0):
                r = 2 * i + o
                gr = cs[r, :, block(b)] + kk
                kk = dec[r, :, block(b)] * gr
                t = (hp[r, :, block(b)] - qq[r, :, block(b)]) * m1[r, :, block(b)] * gr
                ga = t * oma[r, :, block(b)]
                gx = gr * m2[r, :, block(b)]
                gm[r, :, block(b)] = gr * m3[r, :, block(b)]
                st, sa, sx = st + t, sa + ga, sx + gx
                outs[0][o], outs[1][o] = ga, gx
            at = pl.ds(pl.multiple_of(16 * i, 16), 16)
            gp[2 * b, at, :] = jnp.concatenate(outs[0], 0).astype(BF16)
            gp[2 * b + 1, at, :] = jnp.concatenate(outs[1], 0).astype(BF16)
            return kk, st, sa, sx

        zero = jnp.zeros((8, BW), F32)
        _, st, sa, sx = lax.fori_loop(0, R // 2, down, (kin, zero, zero, zero))
        sums.append([st, sa, sx])
        for u in (2 * b, 2 * b + 1):
            grad = jnp.dot(mt[b], gp[u], preferred_element_type=F32)
            wsend[u] = grad.astype(BF16)

            @pl.when(d != u)
            def _():
                send(wsend.at[u], frecv.at[d], f_s, f_r, peer(u))

        nt = (((1,), (1,)), ((), ()))
        back = lax.dot_general(gp[2 * b], W[2 * b], nt, preferred_element_type=F32)
        back = back + lax.dot_general(gp[2 * b + 1], W[2 * b + 1], nt, preferred_element_type=F32)
        gm[0:R, :, block(b)] = gm[0:R, :, block(b)] + back.reshape(R, 8, BW)

    for k in range(3):
        ghs[k : k + 1, :] = gm[k, 0:1, :]
    send(ghs, ghr, e_s, e_r, chip((p + CHIPS - 1) % CHIPS))

    sig = 1.0 / (1.0 + jnp.exp(lam))
    for b in range(NB):
        def add(r, carry):
            g = gm[r, :, block(b)]
            return tuple(carry[k] + g * xs[r + k, :, block(b)] for k in range(4)) + (carry[4] + g,)

        zero = jnp.zeros((8, BW), F32)
        acc = lax.fori_loop(0, R, add, (zero,) * 5, unroll=4)
        st, sa, sx = sums[b]
        st = st * (8.0 * jnp.broadcast_to(sig[:, block(b)], (8, BW)))
        sb = sublane((8, BW))
        rows = zero
        for n, v in enumerate((st, sa, sx) + tuple(acc)):
            for s in (1, 2, 4):
                v = v + pltpu.roll(v, s, 0)
            rows = jnp.where(sb == n, v, rows)
        for lh in range(2):
            u = 2 * b + lh
            ssend[u] = rows[:, lane_tile(lh)]

            @pl.when(d != u)
            def _():
                send(ssend.at[u], srecv.at[d], fs_s, fs_r, peer(u))

    srecv[d] = ssend[d]
    frecv[d] = wsend[d]

    wait_for(ghr, e_r)
    halo = ghr[...]
    halo = jnp.where(p == CHIPS - 1, jnp.zeros_like(halo), halo)
    for k in range(3):
        rolled = pltpu.roll(gm[k], 7, 0)
        gm[R + k] = jnp.where(sub == 7, jnp.broadcast_to(halo[k : k + 1], (8, HALF)), rolled)

    for b in range(NB):
        taps = [jnp.broadcast_to(conv_w[k : k + 1, block(b)], (8, BW)) for k in range(4)]

        @pl.loop(0, R)
        def _(r):
            v = taps[0] * gm[r + 3, :, block(b)]
            for k in range(1, 4):
                v = v + taps[k] * gm[r + 3 - k, :, block(b)]
            for lh in range(2):
                nat[2 * b + lh, pl.ds(r, 8, stride=R), :] = v[:, lane_tile(lh)]

    for k in range(TILES):
        gib[:, lane_tile(k)] = nat[k].astype(BF16)
    s_g = send(gib.at[sib_rows], gi_hbm.at[:, mine], sib_s.at[3], sib_r.at[3], sibling)
    st_g = pltpu.make_async_copy(gib.at[my_rows], gi_hbm.at[:, mine], lsem.at[3])
    st_g.start()

    wait_for(srecv.at[pl.ds(0, REPL - 1)], fs_r)
    ssum[...] = jnp.sum(srecv[...], 0)

    @pl.loop(1, CHIPS)
    def _(j):
        send(ssum, szrecv.at[p], zs_s, zs_r, chip((p + j) % CHIPS))

    szrecv[p] = ssum[...]

    wait_for(frecv.at[pl.ds(0, REPL - 1)], f_r)

    @pl.loop(0, 16)
    def _(i):
        at = pl.ds(pl.multiple_of(16 * i, 16), 16)
        v = frecv[0, at, :].astype(F32)
        for u in range(1, REPL):
            v = v + frecv[u, at, :].astype(F32)
        fsum[i] = v.astype(BF16)

    @pl.loop(1, CHIPS)
    def _(j):
        to = (p + j) % CHIPS
        send(fsum.at[to], zrecv.at[p], z_s, z_r, chip(to))

    zrecv[p] = fsum[p]
    wait_for(szrecv.at[pl.ds(0, CHIPS - 1)], zs_r)
    small = jnp.sum(szrecv[...], 0)
    wait_for(zrecv.at[pl.ds(0, CHIPS - 1)], z_r)
    whole = zrecv[0].astype(F32)
    for j in range(1, CHIPS):
        whole = whole + zrecv[j].astype(F32)
    own[...] = whole
    G[d, c, :, 0:BW] = own[part, :]
    G[d, c, :, BW:] = small
    other = pl.ds(pl.multiple_of(8 * (1 - c), 8), 8)
    fin = tot
    for lh in range(2):
        fin[lh] = own[other, lane_tile(lh)]
    fin[2] = small
    cps = []
    for n in range(3):
        cps.append(send(fin.at[n], G.at[d, c, :, pl.ds(128 * n, 128)], sib_s.at[4 + n], sib_r.at[4 + n], sibling))
    for cp in cps:
        cp.wait_recv()

    @pl.loop(1, REPL)
    def _(j):
        send(G.at[d], G.at[d], g_s, g_r, peer((d + j) % REPL))

    wait_for(G.at[pl.ds(0, REPL - 1)], g_r)
    st_a = pltpu.make_async_copy(G, all_hbm, lsem.at[4])
    st_a.start()

    for cp in [s_w, s_x, s_c, s_g] + cps:
        cp.wait_send()
    s_g.wait_recv()
    wait_for(W.at[0, pl.ds(0, 16 * (CHIPS - 1))], c1_s)
    wait_for(xhalo, hal_s)
    wait_for(W.at[pl.ds(0, REPL - 1)], c2_s)
    wait_for(drecv.at[pl.ds(0, CHIPS - 1)], d_s)
    wait_for(ghr, e_s)
    wait_for(frecv.at[pl.ds(0, REPL - 1)], f_s)
    wait_for(srecv.at[pl.ds(0, REPL - 1)], fs_s)
    wait_for(szrecv.at[pl.ds(0, CHIPS - 1)], zs_s)
    wait_for(zrecv.at[pl.ds(0, CHIPS - 1)], z_s)
    wait_for(G.at[pl.ds(0, REPL - 1)], g_s)
    st_g.wait()
    st_a.wait()


def last_kernel(gi_in, all_ref, gi_out, gw_out, dec_out, bias_out, taps_out, shift_out, gws):
    gi_out[0] = gi_in[...]
    for h in range(2):
        for u in range(8):
            at = slice(h * HALF + 128 * u, h * HALF + 128 * (u + 1))
            v = all_ref[u, h, :, BW:]
            dec_out[:, at] = v[0:1]
            bias_out[:, at] = v[1:3]
            taps_out[:, at] = v[3:7]
            shift_out[:, at] = v[7:8]
            first = (u % 2) * 8 + 4 * h + u // 2
            for lh in range(2):
                gws[lh, pl.ds(first, 8, stride=16), :] = all_ref[u, h, :, lane_tile(lh)]
    for i in range(8):
        for g in range(2):
            for lh in range(2):
                gw_out[i, g, :, lane_tile(lh)] = gws[lh, i * 16 + g * 8 : i * 16 + g * 8 + 8, :]


def per_device(inputs, gate_weight, gate_bias, decay_param, conv_weight, conv_bias, cotangent):
    vmem = pl.BlockSpec(memory_space=pltpu.VMEM)
    anyw = pl.BlockSpec(memory_space=pl.ANY)
    dma = pltpu.SemaphoreType.DMA
    big = pltpu.VMEM((R, 8, HALF), F32)
    gi, packed = pl.pallas_call(
        main_kernel,
        name="main",
        out_shape=(
            jax.ShapeDtypeStruct((ROWS, WIDTH), BF16),
            jax.ShapeDtypeStruct((REPL, 2, 8, BW + 128), F32),
        ),
        in_specs=[anyw, anyw, vmem, vmem, vmem, vmem, anyw],
        out_specs=(anyw, anyw),
        scratch_shapes=[
            pltpu.VMEM((SPAN, HALF), BF16),
            pltpu.VMEM((SPAN, HALF), BF16),
            pltpu.VMEM((8, 2, 8, BW), BF16),
            pltpu.VMEM((2, 128, 128), F32),
            pltpu.VMEM((2, 8, 8, BW), F32),
            pltpu.VMEM((16, BW), F32),
            pltpu.VMEM((8, BW, BW), BF16),
            pltpu.VMEM((16, HALF), BF16),
            pltpu.VMEM((TILES, SPAN, 128), F32),
            pltpu.VMEM((TILES, SPAN, 128), F32),
            pltpu.VMEM((R + 3, 8, HALF), F32),
            big,
            pltpu.VMEM((SPAN, HALF), BF16),
            pltpu.VMEM((NB, BW, SPAN), BF16),
            pltpu.VMEM((8, SPAN, BW), F32),
            big, big, big, big, big, big, big, big,
            pltpu.VMEM((8, SPAN, BW), BF16),
            pltpu.VMEM((R + 3, 8, HALF), F32),
            pltpu.VMEM((3, 8, 128), F32),
            pltpu.VMEM((2, 16, 128), BF16),
            pltpu.VMEM((CHIPS, 16, 128), BF16),
            pltpu.VMEM((2, 8, 128), F32),
            pltpu.VMEM((8, HALF), F32),
            pltpu.VMEM((8, HALF), F32),
            pltpu.VMEM((8, BW, BW), BF16),
            pltpu.VMEM((8, BW, BW), BF16),
            pltpu.VMEM((16, BW), F32),
            pltpu.VMEM((CHIPS, 16, BW), BF16),
            pltpu.VMEM((CHIPS, 16, BW), BF16),
            pltpu.VMEM((8, 8, 128), F32),
            pltpu.VMEM((8, 8, 128), F32),
            pltpu.VMEM((8, 128), F32),
            pltpu.VMEM((CHIPS, 8, 128), F32),
            pltpu.VMEM((REPL, 2, 8, BW + 128), F32),
            pltpu.VMEM((SPAN, HALF), BF16),
            dma((5,)), dma((7,)), dma((7,)),
            dma, dma, dma, dma, dma, dma((REPL,)),
            dma, dma, dma, dma, dma, dma, dma, dma,
            dma, dma, dma, dma, dma, dma,
        ],
        compiler_params=pltpu.CompilerParams(
            collective_id=0, has_side_effects=True, vmem_limit_bytes=48 * 2**20
        ),
    )(
        inputs, gate_weight, gate_bias, decay_param.reshape(1, WIDTH), conv_weight,
        conv_bias.reshape(1, WIDTH), cotangent,
    )
    gi, gw, dec, bias, taps, shift = pl.pallas_call(
        last_kernel,
        name="last",
        out_shape=(
            jax.ShapeDtypeStruct((1, ROWS, WIDTH), BF16),
            jax.ShapeDtypeStruct((8, 2, 8, BW), F32),
            jax.ShapeDtypeStruct((1, WIDTH), F32),
            jax.ShapeDtypeStruct((2, WIDTH), F32),
            jax.ShapeDtypeStruct((4, WIDTH), F32),
            jax.ShapeDtypeStruct((1, WIDTH), F32),
        ),
        in_specs=[vmem, vmem],
        out_specs=(vmem,) * 6,
        scratch_shapes=[pltpu.VMEM((2, 128, 128), F32)],
    )(gi, packed)
    return gi, gw, dec.reshape(WIDTH), bias, taps, shift.reshape(WIDTH)


def solution(mesh):
    placed = (
        P("dp", "ctx", None),
        P("ctx", None, None, None),
        P(),
        P(),
        P(),
        P(),
        P("dp", "ctx", None),
    )
    return jax.shard_map(
        per_device,
        mesh=mesh,
        in_specs=placed,
        out_specs=(P("dp", "ctx", None), P("ctx", None, None, None), P(), P(), P(), P()),
        check_vma=False,
    )
```

time: 675 us -> 83.6 us (0.12)
  waiting for transfers between devices: 394 us -> 0 us
  blocking collectives: 147 us -> 0 us
  Pallas kernels: 0 us -> 75.2 us
  other arithmetic: 65 us -> 0 us
  local copies, waits for them, and re-layouts: 30.3 us -> 7.24 us
  between operations: 14.1 us -> 0.67 us
  matrix products: 10 us -> 0 us
  starting transfers between devices: 7.12 us -> 0 us
    psum x1 -> x0, waiting for transfers between devices: 223 us -> none  [per_device(): lax.psum((lam_part, bias_part, taps_part, shift_part), ('ctx', 'dp'))]
    all_gather x3 -> x0, blocking collectives: 119 us -> none  [prefix(): pieces = jax.tree.map(lambda part: lax.all_gather(part, axis), value)]
    reduce_scatter x1 -> x0, waiting for transfers between devices: 97.3 us -> none  [per_device(): lax.psum_scatter(jnp.einsum('stbi,stcbj->icbj', x_blocks, grad_pre, prefe...]
    pallas_call x0 -> x2, Pallas kernels: none -> 75.2 us  [the longest x1 73.2 us: per_device(): pl.pallas_call(main_kernel, name='main', out_shape=(jax.ShapeDtypeStruct(...]
    all_gather x1 -> x0, waiting for transfers between devices: 72.2 us -> none  [per_device(): whole_weight = lax.all_gather(gate_weight, 'ctx', axis=0, tiled=True)]
    select_n x62 -> x0, other arithmetic: 45.6 us -> none  [hop(): jnp.where(position < mine, new, old)]
    psum x1 -> x0, blocking collectives: 28.4 us -> none  [per_device(): grad_weight = lax.psum(weight_part, 'dp')]
    dot_general x6 -> x0, matrix products: 10 us -> none  [the longest x3 3.48 us: run_sum(): jnp.einsum('ts,nsw->ntw', tri_matrix, values, precision=lax.Precision.HIG...]
  transfers between devices with their start and end apart: 5 -> 0, of which waited for: 4 -> 0; matrix products, arithmetic and copies ran while one was open for 2% -> 0% of each run, Pallas kernels for 0% -> 0%
where the time goes in v1:
time: 83.6 us; the launch traced here: 83.1 us
  Pallas kernels  75.2 us (90%)
  local copies, waits for them, and re-layouts  7.24 us (9%)
    pallas_call x1, Pallas kernels, per_device(): pl.pallas_call(main_kernel, name='main', out_shape=(jax.ShapeDtypeStruct(...  73.2 us
    unnamed x18, local copies, waits for them, and re-layouts  7.24 us
    pallas_call x1, Pallas kernels, per_device(): pl.pallas_call(last_kernel, name='last', out_shape=(jax.ShapeDtypeStruct(...  1.99 us

profile of v1, /device:TPU:1, one launch (start us, length us, event | category | flops | bytes accessed | tf_op | source)
XLA Modules:
  0.0 83.1 jit_solution(8572112129613356658)
XLA Ops:
  0.6 0.0 copy-start
  0.6 1.0 %copy-done = bf16[1,128,2048]{2,1,0:T(8,128)(2,1)S(1)} copy-done((bf16[1,128,2048]{2,1,0:T(8,128)(2,1)S(1)}, bf16[1,128,2048]{2,1,0:T(8,128)(2,1)}, u32[]{:S(2)}) %copy-start) | copy-done | bytes 524312
  1.7 0.0 copy-start.1
  1.7 1.0 %copy-done.1 = bf16[1,128,2048]{2,1,0:T(8,128)(2,1)S(1)} copy-done((bf16[1,128,2048]{2,1,0:T(8,128)(2,1)S(1)}, bf16[1,128,2048]{2,1,0:T(8,128)(2,1)}, u32[]{:S(2)}) %copy-start.1) | copy-done | bytes 524312
  2.7 0.0 copy-start.4
  2.7 0.8 %copy-done.4 = bf16[8,2,8,256]{3,2,1,0:T(8,128)(2,1)S(1)} copy-done((bf16[8,2,8,256]{3,2,1,0:T(8,128)(2,1)S(1)}, bf16[8,2,8,256]{3,2,1,0:T(8,128)(2,1)}, u32[]{:S(2)}) %copy-start.4) | copy-done | bytes 65560
  3.6 0.0 copy-start.5
  3.6 0.8 copy-done.5
  4.3 0.0 copy-start.6
  4.3 0.7 copy-done.6
  5.0 0.0 copy-start.7
  5.0 0.7 copy-done.7
  5.7 0.0 copy-start.8
  5.7 0.7 copy-done.8
  6.4 73.2 %main.1 = (bf16[128,2048]{1,0:T(8,128)(2,1)S(1)}, f32[8,2,8,384]{3,2,1,0:T(8,128)S(1)}) custom-call(bf16[1,128,2048]{2,1,0:T(8,128)(2,1)S(1)} %copy-done, bf16[8,2,8,256]{3,2,1,0:T(8,128)(2,1)S(1)} %copy-done.4, f32[2,2048]{1,0:T(2,128)S(1)} %copy-done.6, f32[1,2048]{1,0:T(1,128)S(1)} %bitcast.4, f32[4,2048]{1,0:T(4,128)S(1)} %copy-done.5, ...), custom_call_target="tpu_custom_call" | custom-call | tf_op jit(solution)/shard_map/main/pallas_call | solution.py:476
  79.7 0.0 copy-start.2
  79.7 0.8 copy-done.2
  80.4 0.0 copy-start.3
  80.5 0.7 copy-done.3
  81.1 2.0 %last.1 = (bf16[1,128,2048]{2,1,0:T(8,128)(2,1)}, f32[8,2,8,256]{3,2,1,0:T(8,128)}, f32[1,2048]{1,0:T(1,128)}, f32[2,2048]{1,0:T(2,128)}, f32[4,2048]{1,0:T(4,128)}, /*index=5*/f32[1,2048]{1,0:T(1,128)}) custom-call(bf16[128,2048]{1,0:T(8,128)(2,1)} %copy-done.2, f32[8,2,8,384]{3,2,1,0:T(8,128)} %copy-done.3), custom_call_target="tpu_custom_call" | custom-call | tf_op jit(solution)/shard_map/last/pallas_call | solution.py:533
Async XLA Ops:
  0.6 1.0 %copy-start = (bf16[1,128,2048]{2,1,0:T(8,128)(2,1)S(1)}, bf16[1,128,2048]{2,1,0:T(8,128)(2,1)}, u32[]{:S(2)}) copy-start(bf16[1,128,2048]{2,1,0:T(8,128)(2,1)} %x_hbm.1) | copy-start | bytes 1572868
  1.7 1.0 %copy-start.1 = (bf16[1,128,2048]{2,1,0:T(8,128)(2,1)S(1)}, bf16[1,128,2048]{2,1,0:T(8,128)(2,1)}, u32[]{:S(2)}) copy-start(bf16[1,128,2048]{2,1,0:T(8,128)(2,1)} %cot_hbm.1) | copy-start | bytes 1572868
  2.7 0.8 %copy-start.4 = (bf16[8,2,8,256]{3,2,1,0:T(8,128)(2,1)S(1)}, bf16[8,2,8,256]{3,2,1,0:T(8,128)(2,1)}, u32[]{:S(2)}) copy-start(bf16[8,2,8,256]{3,2,1,0:T(8,128)(2,1)} %w_hbm.1) | copy-start | bytes 196612
  3.6 0.8 copy-start.5
  4.3 0.7 copy-start.6
  5.0 0.7 copy-start.7
  5.7 0.7 copy-start.8
  79.7 0.8 copy-start.2
  80.4 0.7 copy-start.3

commit v2 on v1

v2 whole, which is shorter than its diff:
```python
import jax
import jax.numpy as jnp
from jax import lax
from jax.experimental import pallas as pl
from jax.experimental.pallas import tpu as pltpu
from jax.sharding import PartitionSpec as P

MESH = pl.DeviceIdType.MESH
F32 = jnp.float32
BF16 = jnp.bfloat16
CHIPS = 16
PLANE = 16
DEPTH = 8
REPL = 8
ROWS = 128
SPAN = 256
WIDTH = 2048
HALF = 1024
BW = 256
NB = HALF // BW
R = SPAN // 8
TILES = HALF // 128
STAGES = 2


def wait_for(ref, sem):
    pltpu.make_async_copy(ref, ref, sem).wait()


def sublane(shape):
    return lax.broadcasted_iota(jnp.int32, shape, 0)


def sigmoid(x):
    return 0.5 * jnp.tanh(0.5 * x) + 0.5


def softplus(x):
    e = jnp.exp(-jnp.abs(x))
    z = e / (2.0 + e)
    z2 = z * z
    s = jnp.full_like(z, 1.0 / 17.0)
    for n in (15, 13, 11, 9, 7, 5, 3, 1):
        s = s * z2 + 1.0 / n
    return jnp.maximum(x, 0.0) + 2.0 * z * s


def lane_tile(i):
    return slice(i * 128, (i + 1) * 128)


def block(b):
    return slice(b * BW, (b + 1) * BW)


def main_kernel(
    x_hbm, w_hbm, gb_hbm, lam_hbm, cw_hbm, cb_hbm, cot_hbm,
    gi_hbm, all_hbm,
    gb_ref, lam_ref, cw_ref, cb_ref, xb, cotb, wsh, wf, wu, wpair, W, xhalo, nat, natc, xs, cs, mb, mt, pre,
    dec, drv, qq, m1, m2, m3, oma, hp, gp, gm, dsend, drecv, sin, ghs, ghr,
    wsend, frecv, own, fsum, zrecv, ssend, srecv, ssum, szrecv, fin, G, gib,
    lsem, sib_s, sib_r, c1_s, c1_r, hal_s, hal_r, c2_s, c2_r, d_s, d_r, e_s, e_r,
    f_s, f_r, fs_s, fs_r, z_s, z_r, zs_s, zs_r, g_s, g_r,
):
    ctx = lax.axis_index("ctx")
    d = lax.axis_index("dp")
    p = ctx // 2
    c = ctx % 2
    z = p % DEPTH
    y = 2 * (p // DEPTH) + d // 4
    x = d % 4
    spot = 4 * y + x
    sibling = {"ctx": 2 * p + 1 - c, "dp": d}

    def chip(j):
        return {"ctx": 2 * j + c, "dp": d}

    def deep(j):
        return {"ctx": 2 * (p - z + j) + c, "dp": d}

    def peer(u):
        return {"ctx": ctx, "dp": u}

    def plane(j):
        to_x, to_y = (x + j % 4) % 4, (y + j // 4) % 4
        to_d = 4 * (to_y % 2) + to_x
        return {"ctx": 2 * (DEPTH * (to_y // 2) + z) + c, "dp": to_d}, to_y // 2, to_d

    def rows_of(h):
        return pl.ds(pl.multiple_of(128 * h, 128), 128)

    def lanes_of(u):
        return pl.ds(pl.multiple_of(128 * (u % 2), 128), 128)

    def send(src, dst, ss, rs, dev):
        cp = pltpu.make_async_remote_copy(
            src_ref=src, dst_ref=dst, send_sem=ss, recv_sem=rs, device_id=dev, device_id_type=MESH
        )
        cp.start()
        return cp

    bar = pltpu.get_barrier_semaphore()
    pl.semaphore_signal(bar, inc=1, device_id=sibling, device_id_type=MESH)

    @pl.loop(1, CHIPS)
    def _(j):
        pl.semaphore_signal(bar, inc=1, device_id=chip((p + j) % CHIPS), device_id_type=MESH)

    @pl.loop(1, PLANE)
    def _(j):
        @pl.when(j != PLANE // 2)
        def _():
            pl.semaphore_signal(bar, inc=1, device_id=plane(j)[0], device_id_type=MESH)

    mine = pl.ds(pl.multiple_of(HALF * c, HALF), HALF)
    theirs = pl.ds(pl.multiple_of(HALF * (1 - c), HALF), HALF)
    my_rows = pl.ds(pl.multiple_of(ROWS * c, ROWS), ROWS)
    sib_rows = pl.ds(pl.multiple_of(ROWS * (1 - c), ROWS), ROWS)

    ld_w = pltpu.make_async_copy(w_hbm, wsh, lsem.at[0])
    ld_w.start()
    ld_x = pltpu.make_async_copy(x_hbm.at[0, :, mine], xb.at[my_rows], lsem.at[1])
    ld_x.start()
    ld_c = pltpu.make_async_copy(cot_hbm.at[0, :, mine], cotb.at[my_rows], lsem.at[2])
    ld_c.start()
    lds = []
    for n, (src, dst) in enumerate(
        ((gb_hbm, gb_ref), (lam_hbm, lam_ref), (cw_hbm, cw_ref), (cb_hbm, cb_ref))
    ):
        lds.append(pltpu.make_async_copy(src.at[:, mine], dst, lsem.at[5 + n]))
        lds[-1].start()
    pending = []

    ld_w.wait()
    for i in range(8):
        for g in range(2):
            v = wsh[i, g].astype(F32)
            for lh in range(2):
                wf[lh, i * 16 + g * 8 : i * 16 + g * 8 + 8, :] = v[:, lane_tile(lh)]
    for h in range(2):
        for u in range(REPL):
            for st in range(STAGES):
                first = ((u // 2) % 2) * 8 + 4 * h + 2 * st + u // 4
                wu[h, u, st] = wf[u % 2, pl.ds(first, 8, stride=16), :]

    pl.semaphore_wait(bar, 1 + (CHIPS - 1) + (PLANE - 2))

    part = pl.ds(pl.multiple_of(8 * c, 8), 8)
    s_w = send(wu.at[1 - c, d], wpair.at[:, part], sib_s.at[0], sib_r.at[0], sibling)
    s_x = send(x_hbm.at[0, :, theirs], xb.at[my_rows], sib_s.at[1], sib_r.at[1], sibling)
    s_c = send(cot_hbm.at[0, :, theirs], cotb.at[my_rows], sib_s.at[2], sib_r.at[2], sibling)
    wpair[:, part, :] = wu[c, d]
    s_w.wait_recv()
    my16 = pl.ds(pl.multiple_of(16 * p, 16), 16)
    mine_w = W.at[d // 2, :, my16, lanes_of(d)]
    mine_w[...] = wpair[...].astype(BF16)

    @pl.loop(1, DEPTH)
    def _(j):
        send(mine_w, mine_w, c1_s, c1_r, deep((z + j) % DEPTH))

    seven = wsend.at[0, :, pl.ds(0, 16 * (DEPTH - 1)), pl.ds(0, 128)]
    pending.append((seven, c1_s))

    ld_x.wait()
    s_x.wait_recv()
    send(xb.at[pl.ds(SPAN - 16, 16)], xhalo, hal_s, hal_r, chip((p + 1) % CHIPS))
    pending.append((xhalo, hal_s))
    for k in range(TILES):
        nat[k] = xb[:, lane_tile(k)].astype(F32)

    @pl.loop(0, R)
    def _(r):
        for k in range(TILES):
            xs[3 + r, :, lane_tile(k)] = nat[k, pl.ds(r, 8, stride=R), :]

    wait_for(seven, c1_r)
    fifteen = frecv.at[0, pl.ds(0, PLANE - 1)]
    for st in range(STAGES):
        @pl.loop(1, PLANE)
        def _(j):
            mine_s = W.at[d // 2, st, rows_of(y // 2), lanes_of(d)]
            send(mine_s, mine_s, c2_s.at[st], c2_r.at[st], plane(j)[0])

        pending.append((fifteen, c2_s.at[st]))

    ld_c.wait()
    s_c.wait_recv()
    for k in range(TILES):
        natc[k] = cotb[:, lane_tile(k)].astype(F32)

    @pl.loop(0, R)
    def _(r):
        for k in range(TILES):
            cs[r, :, lane_tile(k)] = natc[k, pl.ds(r, 8, stride=R), :]

    wait_for(xhalo, hal_r)
    hal = xhalo[...].astype(F32)
    hal = jnp.where(p == 0, jnp.zeros_like(hal), hal)
    sub = sublane((8, HALF))
    for k in range(3):
        rolled = pltpu.roll(xs[3 + R - 3 + k], 1, 0)
        xs[k] = jnp.where(sub == 0, jnp.broadcast_to(hal[13 + k : 14 + k], (8, HALF)), rolled)

    for ld in lds:
        ld.wait()
    conv_w = cw_ref[...]
    conv_b = cb_ref[...]
    for b in range(NB):
        taps = [jnp.broadcast_to(conv_w[k : k + 1, block(b)], (8, BW)) for k in range(4)]
        shift = jnp.broadcast_to(conv_b[:, block(b)], (8, BW))

        @pl.loop(0, R // 2)
        def _(i):
            v = [xs[2 * i + k, :, block(b)] for k in range(5)]
            out = []
            for o in range(2):
                m = shift + taps[0] * v[o]
                for k in range(1, 4):
                    m = m + taps[k] * v[o + k]
                out.append(m)
            mb[pl.ds(pl.multiple_of(16 * i, 16), 16), block(b)] = jnp.concatenate(out, 0).astype(BF16)

        mt[b] = mb[:, block(b)].astype(F32).T.astype(BF16)

    lam = lam_ref[...]
    neg8rate = -8.0 * softplus(-lam)
    gate_b = gb_ref[...]
    ends = []

    def gates(b):
        st, k = b // 2, 2 * (b % 2)
        for g in range(2):
            pre[2 * b + g] = jnp.dot(mb[:, block(b)], W[k + g, st], preferred_element_type=F32)
        nr = jnp.broadcast_to(neg8rate[:, block(b)], (8, BW))
        ba = jnp.broadcast_to(gate_b[0:1, block(b)], (8, BW))
        bx = jnp.broadcast_to(gate_b[1:2, block(b)], (8, BW))

        def step(i, carry):
            prod, hid, kk, logs = carry
            two = mb[pl.ds(pl.multiple_of(16 * i, 16), 16), block(b)].astype(F32)
            for o in range(2):
                r = 2 * i + o
                at = pl.ds(pl.multiple_of(8 * r, 8), 8)
                ga = sigmoid(pre[2 * b, at, :] + ba)
                gx = sigmoid(pre[2 * b + 1, at, :] + bx)
                m = two[8 * o : 8 * o + 8]
                ld = ga * nr
                a = jnp.exp(ld)
                sq = 1.0 - a * a
                mult = jnp.sqrt(sq)
                gm_ = gx * m
                drive = mult * gm_
                dec[r, :, block(b)] = a
                drv[r, :, block(b)] = drive
                qq[r, :, block(b)] = gm_ * a * lax.rsqrt(jnp.maximum(sq, 0.05))
                m1[r, :, block(b)] = a * ga
                oma[r, :, block(b)] = (1.0 - ga) * nr
                m2[r, :, block(b)] = drive * (1.0 - gx)
                m3[r, :, block(b)] = mult * gx
                hid = a * hid + drive
                prod = prod * a
                kk = kk + prod * cs[r, :, block(b)]
                logs = logs + ld
            return prod, hid, kk, logs

        zero = jnp.zeros((8, BW), F32)
        prod, hid, kk, logs = lax.fori_loop(
            0, R // 2, step, (jnp.ones((8, BW), F32), zero, zero, zero)
        )
        sb = sublane((8, BW))
        fp, fh = prod, hid
        bp, bk = prod, kk
        for s in (1, 2, 4):
            mp, mh = pltpu.roll(fp, s, 0), pltpu.roll(fh, s, 0)
            fh = jnp.where(sb >= s, fp * mh + fh, fh)
            fp = jnp.where(sb >= s, fp * mp, fp)
            mp, mk = pltpu.roll(bp, 8 - s, 0), pltpu.roll(bk, 8 - s, 0)
            bk = jnp.where(sb < 8 - s, bp * mk + bk, bk)
            bp = jnp.where(sb < 8 - s, bp * mp, bp)
            logs = logs + pltpu.roll(logs, s, 0)
        one = jnp.ones((8, BW), F32)
        ends.append((
            jnp.where(sb == 0, one, pltpu.roll(fp, 1, 0)),
            jnp.where(sb == 0, zero, pltpu.roll(fh, 1, 0)),
            jnp.where(sb == 7, one, pltpu.roll(bp, 7, 0)),
            jnp.where(sb == 7, zero, pltpu.roll(bk, 7, 0)),
        ))
        for lh in range(2):
            k = 2 * (b % 2) + lh
            dsend[st, 0, k : k + 1, :] = logs[0:1, lane_tile(lh)]
            dsend[st, 1, k : k + 1, :] = logs[0:1, lane_tile(lh)]
            dsend[st, 0, 4 + k : 5 + k, :] = fh[7:8, lane_tile(lh)]
            dsend[st, 1, 4 + k : 5 + k, :] = bk[0:1, lane_tile(lh)]

    for st in range(STAGES):
        wait_for(fifteen, c2_r.at[st])
        for b in (2 * st, 2 * st + 1):
            gates(b)

        @pl.loop(1, CHIPS)
        def _(j):
            to = (p + j) % CHIPS
            send(dsend.at[st, jnp.where(to > p, 0, 1)], drecv.at[st, p], d_s.at[st], d_r.at[st], chip(to))

        pending.append((drecv.at[st, pl.ds(0, CHIPS - 1)], d_s.at[st]))
        drecv[st, p] = jnp.zeros((8, 128), F32)

    sums = []

    def grads(b):
        st, k = b // 2, 2 * (b % 2)

        def wide(n):
            return jnp.concatenate(
                [jnp.broadcast_to(sin[st, n, k + lh : k + lh + 1, :], (8, 128)) for lh in range(2)], 1
            )

        hin = ends[b][1] + ends[b][0] * wide(0)
        kin = ends[b][3] + ends[b][2] * wide(1)

        def up(r, h):
            hp[r, :, block(b)] = h
            return dec[r, :, block(b)] * h + drv[r, :, block(b)]

        lax.fori_loop(0, R, up, hin, unroll=4)

        def down(n, carry):
            kk, t_sum, a_sum, x_sum = carry
            i = R // 2 - 1 - n
            outs = [[None, None], [None, None]]
            for o in (1, 0):
                r = 2 * i + o
                gr = cs[r, :, block(b)] + kk
                kk = dec[r, :, block(b)] * gr
                t = (hp[r, :, block(b)] - qq[r, :, block(b)]) * m1[r, :, block(b)] * gr
                ga = t * oma[r, :, block(b)]
                gx = gr * m2[r, :, block(b)]
                gm[r, :, block(b)] = gr * m3[r, :, block(b)]
                t_sum, a_sum, x_sum = t_sum + t, a_sum + ga, x_sum + gx
                outs[0][o], outs[1][o] = ga, gx
            at = pl.ds(pl.multiple_of(16 * i, 16), 16)
            gp[2 * b, at, :] = jnp.concatenate(outs[0], 0).astype(BF16)
            gp[2 * b + 1, at, :] = jnp.concatenate(outs[1], 0).astype(BF16)
            return kk, t_sum, a_sum, x_sum

        zero = jnp.zeros((8, BW), F32)
        _, t_sum, a_sum, x_sum = lax.fori_loop(0, R // 2, down, (kin, zero, zero, zero))
        sums.append([t_sum, a_sum, x_sum])
        for g in range(2):
            wsend[k + g, st] = jnp.dot(mt[b], gp[2 * b + g], preferred_element_type=F32).astype(BF16)

    def through(b):
        st, k = b // 2, 2 * (b % 2)
        nt = (((1,), (1,)), ((), ()))
        back = lax.dot_general(gp[2 * b], W[k, st], nt, preferred_element_type=F32)
        back = back + lax.dot_general(gp[2 * b + 1], W[k + 1, st], nt, preferred_element_type=F32)
        gm[0:R, :, block(b)] = gm[0:R, :, block(b)] + back.reshape(R, 8, BW)

    for st in range(STAGES):
        wait_for(drecv.at[st, pl.ds(0, CHIPS - 1)], d_r.at[st])
        state = jnp.zeros((4, 128), F32)
        carry_in = jnp.zeros((4, 128), F32)
        for j in range(CHIPS):
            v = drecv[st, j]
            state = jnp.where(j < p, jnp.exp(v[:4]) * state + v[4:], state)
            v = drecv[st, CHIPS - 1 - j]
            carry_in = jnp.where(CHIPS - 1 - j > p, jnp.exp(v[:4]) * carry_in + v[4:], carry_in)
        sin[st, 0] = state
        sin[st, 1] = carry_in
        for b in (2 * st, 2 * st + 1):
            grads(b)

        @pl.loop(1, PLANE)
        def _(j):
            dev, to_h, to_d = plane(j)
            send(
                wsend.at[to_d // 2, st, rows_of(to_h), lanes_of(to_d)],
                frecv.at[st, spot], f_s.at[st], f_r.at[st], dev,
            )

        pending.append((fifteen, f_s.at[st]))
        frecv[st, spot] = wsend[d // 2, st, rows_of(y // 2), lanes_of(d)]
        for b in (2 * st, 2 * st + 1):
            through(b)

    for k in range(3):
        ghs[k : k + 1, :] = gm[k, 0:1, :]
    send(ghs, ghr, e_s, e_r, chip((p + CHIPS - 1) % CHIPS))
    pending.append((ghr, e_s))

    sig = 1.0 / (1.0 + jnp.exp(lam))
    for b in range(NB):
        def add(r, carry):
            g = gm[r, :, block(b)]
            return tuple(carry[k] + g * xs[r + k, :, block(b)] for k in range(4)) + (carry[4] + g,)

        zero = jnp.zeros((8, BW), F32)
        acc = lax.fori_loop(0, R, add, (zero,) * 5, unroll=4)
        t_sum, a_sum, x_sum = sums[b]
        t_sum = t_sum * (8.0 * jnp.broadcast_to(sig[:, block(b)], (8, BW)))
        sb = sublane((8, BW))
        rows = zero
        for n, v in enumerate((t_sum, a_sum, x_sum) + tuple(acc)):
            for s in (1, 2, 4):
                v = v + pltpu.roll(v, s, 0)
            rows = jnp.where(sb == n, v, rows)
        for lh in range(2):
            ssend[2 * b + lh] = rows[:, lane_tile(lh)]

    @pl.loop(1, PLANE)
    def _(j):
        dev, _, to_d = plane(j)
        send(ssend.at[to_d], srecv.at[spot], fs_s, fs_r, dev)

    pending.append((srecv.at[pl.ds(0, PLANE - 1)], fs_s))
    srecv[spot] = ssend[d]

    def fold(st):
        wait_for(fifteen, f_r.at[st])

        @pl.loop(0, DEPTH)
        def _(i):
            at = pl.ds(pl.multiple_of(16 * i, 16), 16)
            v = frecv[st, 0, at, :].astype(F32)
            for u in range(1, PLANE):
                v = v + frecv[st, u, at, :].astype(F32)
            fsum[st, i] = v.astype(BF16)

        @pl.loop(1, DEPTH)
        def _(j):
            to = (z + j) % DEPTH
            send(fsum.at[st, to], zrecv.at[st, z], z_s.at[st], z_r.at[st], deep(to))

        pending.append((zrecv.at[st, pl.ds(0, DEPTH - 1)], z_s.at[st]))
        zrecv[st, z] = fsum[st, z]

    fold(0)
    wait_for(ghr, e_r)
    halo = ghr[...]
    halo = jnp.where(p == CHIPS - 1, jnp.zeros_like(halo), halo)
    for k in range(3):
        rolled = pltpu.roll(gm[k], 7, 0)
        gm[R + k] = jnp.where(sub == 7, jnp.broadcast_to(halo[k : k + 1], (8, HALF)), rolled)

    for b in range(NB):
        taps = [jnp.broadcast_to(conv_w[k : k + 1, block(b)], (8, BW)) for k in range(4)]

        @pl.loop(0, R)
        def _(r):
            v = taps[0] * gm[r + 3, :, block(b)]
            for k in range(1, 4):
                v = v + taps[k] * gm[r + 3 - k, :, block(b)]
            for lh in range(2):
                nat[2 * b + lh, pl.ds(r, 8, stride=R), :] = v[:, lane_tile(lh)]

    for k in range(TILES):
        gib[:, lane_tile(k)] = nat[k].astype(BF16)
    s_g = send(gib.at[sib_rows], gi_hbm.at[:, mine], sib_s.at[3], sib_r.at[3], sibling)
    st_g = pltpu.make_async_copy(gib.at[my_rows], gi_hbm.at[:, mine], lsem.at[3])
    st_g.start()
    pending.append((gib.at[my_rows], lsem.at[3]))

    wait_for(srecv.at[pl.ds(0, PLANE - 1)], fs_r)
    ssum[...] = jnp.sum(srecv[...], 0)

    @pl.loop(1, DEPTH)
    def _(j):
        send(ssum, szrecv.at[z], zs_s, zs_r, deep((z + j) % DEPTH))

    pending.append((szrecv.at[pl.ds(0, DEPTH - 1)], zs_s))
    szrecv[z] = ssum[...]
    fold(1)
    wait_for(szrecv.at[pl.ds(0, DEPTH - 1)], zs_r)
    small = jnp.sum(szrecv[...], 0)
    for st in range(STAGES):
        wait_for(zrecv.at[st, pl.ds(0, DEPTH - 1)], z_r.at[st])
    other = pl.ds(pl.multiple_of(8 * (1 - c), 8), 8)
    for st in range(STAGES):
        whole = zrecv[st, 0].astype(F32)
        for j in range(1, DEPTH):
            whole = whole + zrecv[st, j].astype(F32)
        own[...] = whole
        G[d, c, :, lane_tile(st)] = own[part, :]
        fin[:, lane_tile(st)] = own[other, :]
    G[d, c, :, lane_tile(STAGES)] = small
    fin[:, lane_tile(STAGES)] = small
    s_f = send(fin, G.at[d, c], sib_s.at[4], sib_r.at[4], sibling)
    s_f.wait_recv()

    @pl.loop(1, REPL)
    def _(j):
        send(G.at[d], G.at[d], g_s, g_r, peer((d + j) % REPL))

    pending.append((G.at[pl.ds(0, REPL - 1)], g_s))
    wait_for(G.at[pl.ds(0, REPL - 1)], g_r)
    st_a = pltpu.make_async_copy(G, all_hbm, lsem.at[4])
    st_a.start()

    for cp in [s_w, s_x, s_c, s_g, s_f]:
        cp.wait_send()
    s_g.wait_recv()
    for ref, sem in pending:
        wait_for(ref, sem)
    st_a.wait()


def last_kernel(gi_in, all_ref, gi_out, gw_out, dec_out, bias_out, taps_out, shift_out, gws, sem):
    copy = pltpu.make_async_copy(gi_in, gi_out.at[0], sem)
    copy.start()
    for h in range(2):
        for u in range(8):
            at = slice(h * HALF + 128 * u, h * HALF + 128 * (u + 1))
            v = all_ref[u, h, :, BW:]
            dec_out[:, at] = v[0:1]
            bias_out[:, at] = v[1:3]
            taps_out[:, at] = v[3:7]
            shift_out[:, at] = v[7:8]
            for st in range(STAGES):
                first = ((u // 2) % 2) * 8 + 4 * h + 2 * st + u // 4
                gws[u % 2, pl.ds(first, 8, stride=16), :] = all_ref[u, h, :, lane_tile(st)]
    for i in range(8):
        for g in range(2):
            for lh in range(2):
                gw_out[i, g, :, lane_tile(lh)] = gws[lh, i * 16 + g * 8 : i * 16 + g * 8 + 8, :]
    copy.wait()


def per_device(inputs, gate_weight, gate_bias, decay_param, conv_weight, conv_bias, cotangent):
    vmem = pl.BlockSpec(memory_space=pltpu.VMEM)
    hbm = pl.BlockSpec(memory_space=pltpu.HBM)
    dma = pltpu.SemaphoreType.DMA
    big = pltpu.VMEM((R, 8, HALF), F32)
    gi, packed = pl.pallas_call(
        main_kernel,
        name="main",
        out_shape=(
            jax.ShapeDtypeStruct((ROWS, WIDTH), BF16),
            jax.ShapeDtypeStruct((REPL, 2, 8, BW + 128), F32),
        ),
        in_specs=[hbm] * 7,
        out_specs=(hbm, hbm),
        scratch_shapes=[
            pltpu.VMEM((2, HALF), F32),
            pltpu.VMEM((1, HALF), F32),
            pltpu.VMEM((4, HALF), F32),
            pltpu.VMEM((1, HALF), F32),
            pltpu.VMEM((SPAN, HALF), BF16),
            pltpu.VMEM((SPAN, HALF), BF16),
            pltpu.VMEM((8, 2, 8, BW), BF16),
            pltpu.VMEM((2, 128, 128), F32),
            pltpu.VMEM((2, REPL, STAGES, 8, 128), F32),
            pltpu.VMEM((STAGES, 16, 128), F32),
            pltpu.VMEM((4, STAGES, BW, BW), BF16),
            pltpu.VMEM((16, HALF), BF16),
            pltpu.VMEM((TILES, SPAN, 128), F32),
            pltpu.VMEM((TILES, SPAN, 128), F32),
            pltpu.VMEM((R + 3, 8, HALF), F32),
            big,
            pltpu.VMEM((SPAN, HALF), BF16),
            pltpu.VMEM((NB, BW, SPAN), BF16),
            pltpu.VMEM((8, SPAN, BW), F32),
            big, big, big, big, big, big, big, big,
            pltpu.VMEM((8, SPAN, BW), BF16),
            pltpu.VMEM((R + 3, 8, HALF), F32),
            pltpu.VMEM((STAGES, 2, 8, 128), F32),
            pltpu.VMEM((STAGES, CHIPS, 8, 128), F32),
            pltpu.VMEM((STAGES, 2, 4, 128), F32),
            pltpu.VMEM((8, HALF), F32),
            pltpu.VMEM((8, HALF), F32),
            pltpu.VMEM((4, STAGES, BW, BW), BF16),
            pltpu.VMEM((STAGES, PLANE, 128, 128), BF16),
            pltpu.VMEM((16, 128), F32),
            pltpu.VMEM((STAGES, DEPTH, 16, 128), BF16),
            pltpu.VMEM((STAGES, DEPTH, 16, 128), BF16),
            pltpu.VMEM((8, 8, 128), F32),
            pltpu.VMEM((PLANE, 8, 128), F32),
            pltpu.VMEM((8, 128), F32),
            pltpu.VMEM((DEPTH, 8, 128), F32),
            pltpu.VMEM((8, BW + 128), F32),
            pltpu.VMEM((REPL, 2, 8, BW + 128), F32),
            pltpu.VMEM((SPAN, HALF), BF16),
            dma((9,)), dma((7,)), dma((7,)),
            dma, dma, dma, dma, dma((STAGES,)), dma((STAGES,)),
            dma((STAGES,)), dma((STAGES,)), dma, dma, dma((STAGES,)), dma((STAGES,)), dma, dma,
            dma((STAGES,)), dma((STAGES,)), dma, dma, dma, dma,
        ],
        compiler_params=pltpu.CompilerParams(
            collective_id=0, has_side_effects=True, vmem_limit_bytes=60 * 2**20
        ),
    )(
        inputs, gate_weight, gate_bias, decay_param.reshape(1, WIDTH), conv_weight,
        conv_bias.reshape(1, WIDTH), cotangent,
    )
    gi, gw, dec, bias, taps, shift = pl.pallas_call(
        last_kernel,
        name="last",
        out_shape=(
            jax.ShapeDtypeStruct((1, ROWS, WIDTH), BF16),
            jax.ShapeDtypeStruct((8, 2, 8, BW), F32),
            jax.ShapeDtypeStruct((1, WIDTH), F32),
            jax.ShapeDtypeStruct((2, WIDTH), F32),
            jax.ShapeDtypeStruct((4, WIDTH), F32),
            jax.ShapeDtypeStruct((1, WIDTH), F32),
        ),
        in_specs=[hbm, vmem],
        out_specs=(hbm,) + (vmem,) * 5,
        scratch_shapes=[pltpu.VMEM((2, 128, 128), F32), dma],
        compiler_params=pltpu.CompilerParams(vmem_limit_bytes=60 * 2**20),
    )(gi, packed)
    return gi, gw, dec.reshape(WIDTH), bias, taps, shift.reshape(WIDTH)


def solution(mesh):
    placed = (
        P("dp", "ctx", None),
        P("ctx", None, None, None),
        P(),
        P(),
        P(),
        P(),
        P("dp", "ctx", None),
    )
    return jax.shard_map(
        per_device,
        mesh=mesh,
        in_specs=placed,
        out_specs=(P("dp", "ctx", None), P("ctx", None, None, None), P(), P(), P(), P()),
        check_vma=False,
    )
```

time: 83.6 us -> 83.2 us (level)
  Pallas kernels: 75.2 us -> 82.5 us
  local copies, waits for them, and re-layouts: 7.24 us -> 0 us
    pallas_call x1, Pallas kernels: 1.99 us -> 18.6 us  [per_device(): pl.pallas_call(last_kernel, name='last', out_shape=(jax.ShapeDtypeStruct(...]
    pallas_call x1, Pallas kernels: 73.2 us -> 63.9 us  [per_device(): pl.pallas_call(main_kernel, name='main', out_shape=(jax.ShapeDtypeStruct(...]
    unnamed x18 -> x0, local copies, waits for them, and re-layouts: 7.24 us -> none
where the time goes in v2:
time: 83.2 us; the launch traced here: 83.1 us
  Pallas kernels  82.5 us (99%)
    pallas_call x1, Pallas kernels, per_device(): pl.pallas_call(main_kernel, name='main', out_shape=(jax.ShapeDtypeStruct(...  63.9 us
    pallas_call x1, Pallas kernels, per_device(): pl.pallas_call(last_kernel, name='last', out_shape=(jax.ShapeDtypeStruct(...  18.6 us

profile of v2, /device:TPU:1, one launch (start us, length us, event | category | flops | bytes accessed | tf_op | source)
XLA Modules:
  0.0 83.1 jit_solution(7662030210925627551)
XLA Ops:
  0.6 63.9 %main.1 = (bf16[128,2048]{1,0:T(8,128)(2,1)}, f32[8,2,8,384]{3,2,1,0:T(8,128)}) custom-call(bf16[1,128,2048]{2,1,0:T(8,128)(2,1)} %x_hbm.1, bf16[8,2,8,256]{3,2,1,0:T(8,128)(2,1)} %w_hbm.1, f32[2,2048]{1,0:T(2,128)} %gb_hbm.1, f32[1,2048]{1,0:T(1,128)} %bitcast.4, f32[4,2048]{1,0:T(4,128)} %cw_hbm.1, f32[1,2048]{1,0:T(1,128)} %bitcast.5, ...), custom_call_target="tpu_custom_call" | custom-call | tf_op jit(solution)/shard_map/main/pallas_call | solution.py:534
  64.5 18.6 %last.1 = (bf16[1,128,2048]{2,1,0:T(8,128)(2,1)}, f32[8,2,8,256]{3,2,1,0:T(8,128)}, f32[1,2048]{1,0:T(1,128)}, f32[2,2048]{1,0:T(2,128)}, f32[4,2048]{1,0:T(4,128)}, /*index=5*/f32[1,2048]{1,0:T(1,128)}) custom-call(bf16[128,2048]{1,0:T(8,128)(2,1)} %get-tuple-element.14.gi_in, f32[8,2,8,384]{3,2,1,0:T(8,128)} %get-tuple-element.15.all_ref), custom_call_target="tpu_custom_call" | custom-call | tf_op jit(solution)/shard_map/last/pallas_call | solution.py:595

commit v3 on v2

--- a/solution.py
+++ b/solution.py
@@ -505,9 +505,15 @@
     st_a.wait()
 
 
-def last_kernel(gi_in, all_ref, gi_out, gw_out, dec_out, bias_out, taps_out, shift_out, gws, sem):
-    copy = pltpu.make_async_copy(gi_in, gi_out.at[0], sem)
-    copy.start()
+def last_kernel(gi_in, all_ref, gi_out, gw_out, dec_out, bias_out, taps_out, shift_out, gws, via, l_sem, s_sem):
+    parts = [pl.ds(k * (ROWS // 4), ROWS // 4) for k in range(4)]
+    loads = [pltpu.make_async_copy(gi_in.at[at], via.at[at], l_sem.at[k]) for k, at in enumerate(parts)]
+    stores = [pltpu.make_async_copy(via.at[at], gi_out.at[0, at], s_sem.at[k]) for k, at in enumerate(parts)]
+    for cp in loads:
+        cp.start()
+    for k in range(4):
+        loads[k].wait()
+        stores[k].start()
     for h in range(2):
         for u in range(8):
             at = slice(h * HALF + 128 * u, h * HALF + 128 * (u + 1))
@@ -523,7 +529,8 @@
         for g in range(2):
             for lh in range(2):
                 gw_out[i, g, :, lane_tile(lh)] = gws[lh, i * 16 + g * 8 : i * 16 + g * 8 + 8, :]
-    copy.wait()
+    for cp in stores:
+        cp.wait()
 
 
 def per_device(inputs, gate_weight, gate_bias, decay_param, conv_weight, conv_bias, cotangent):
@@ -605,7 +612,7 @@
         ),
         in_specs=[hbm, vmem],
         out_specs=(hbm,) + (vmem,) * 5,
-        scratch_shapes=[pltpu.VMEM((2, 128, 128), F32), dma],
+        scratch_shapes=[pltpu.VMEM((2, 128, 128), F32), pltpu.VMEM((ROWS, WIDTH), BF16), dma((4,)), dma((4,))],
         compiler_params=pltpu.CompilerParams(vmem_limit_bytes=60 * 2**20),
     )(gi, packed)
     return gi, gw, dec.reshape(WIDTH), bias, taps, shift.reshape(WIDTH)

time: 83.2 us -> 68.1 us (0.82)
  Pallas kernels: 82.5 us -> 67.3 us
    pallas_call x1, Pallas kernels: 18.6 us -> 3.42 us  [per_device(): pl.pallas_call(last_kernel, name='last', out_shape=(jax.ShapeDtypeStruct(...]
where the time goes in v3:
time: 68.1 us; the launch traced here: 67.9 us
  Pallas kernels  67.3 us (99%)
    pallas_call x1, Pallas kernels, per_device(): pl.pallas_call(main_kernel, name='main', out_shape=(jax.ShapeDtypeStruct(...  63.9 us
    pallas_call x1, Pallas kernels, per_device(): pl.pallas_call(last_kernel, name='last', out_shape=(jax.ShapeDtypeStruct(...  3.42 us

profile of v3, /device:TPU:1, one launch (start us, length us, event | category | flops | bytes accessed | tf_op | source)
XLA Modules:
  0.0 67.9 jit_solution(12655123001481265864)
XLA Ops:
  0.6 63.9 %main.1 = (bf16[128,2048]{1,0:T(8,128)(2,1)}, f32[8,2,8,384]{3,2,1,0:T(8,128)}) custom-call(bf16[1,128,2048]{2,1,0:T(8,128)(2,1)} %x_hbm.1, bf16[8,2,8,256]{3,2,1,0:T(8,128)(2,1)} %w_hbm.1, f32[2,2048]{1,0:T(2,128)} %gb_hbm.1, f32[1,2048]{1,0:T(1,128)} %bitcast.4, f32[4,2048]{1,0:T(4,128)} %cw_hbm.1, f32[1,2048]{1,0:T(1,128)} %bitcast.5, ...), custom_call_target="tpu_custom_call" | custom-call | tf_op jit(solution)/shard_map/main/pallas_call | solution.py:541
  64.5 3.4 %last.1 = (bf16[1,128,2048]{2,1,0:T(8,128)(2,1)}, f32[8,2,8,256]{3,2,1,0:T(8,128)}, f32[1,2048]{1,0:T(1,128)}, f32[2,2048]{1,0:T(2,128)}, f32[4,2048]{1,0:T(4,128)}, /*index=5*/f32[1,2048]{1,0:T(1,128)}) custom-call(bf16[128,2048]{1,0:T(8,128)(2,1)} %get-tuple-element.14.gi_in, f32[8,2,8,384]{3,2,1,0:T(8,128)} %get-tuple-element.15.all_ref), custom_call_target="tpu_custom_call" | custom-call | tf_op jit(solution)/shard_map/last/pallas_call | solution.py:602

commit v4 on v3

--- a/solution.py
+++ b/solution.py
@@ -59,7 +59,7 @@
     gb_ref, lam_ref, cw_ref, cb_ref, xb, cotb, wsh, wf, wu, wpair, W, xhalo, nat, natc, xs, cs, mb, mt, pre,
     dec, drv, qq, m1, m2, m3, oma, hp, gp, gm, dsend, drecv, sin, ghs, ghr,
     wsend, frecv, own, fsum, zrecv, ssend, srecv, ssum, szrecv, fin, G, gib,
-    lsem, sib_s, sib_r, c1_s, c1_r, hal_s, hal_r, c2_s, c2_r, d_s, d_r, e_s, e_r,
+    lsem, sib_s, sib_r, c1_s, c1_r, hal_s, hal_r, za_s, za_r, c2_s, c2_r, d_s, d_r, e_s, e_r,
     f_s, f_r, fs_s, fs_r, z_s, z_r, zs_s, zs_r, g_s, g_r,
 ):
     ctx = lax.axis_index("ctx")
@@ -111,6 +111,11 @@
         @pl.when(j != PLANE // 2)
         def _():
             pl.semaphore_signal(bar, inc=1, device_id=plane(j)[0], device_id_type=MESH)
+
+    @pl.loop(1, REPL)
+    def _(j):
+        dev = {"ctx": 2 * p + 1 - c, "dp": (d + j) % REPL}
+        pl.semaphore_signal(bar, inc=1, device_id=dev, device_id_type=MESH)
 
     mine = pl.ds(pl.multiple_of(HALF * c, HALF), HALF)
     theirs = pl.ds(pl.multiple_of(HALF * (1 - c), HALF), HALF)
@@ -141,26 +146,40 @@
         for u in range(REPL):
             for st in range(STAGES):
                 first = ((u // 2) % 2) * 8 + 4 * h + 2 * st + u // 4
-                wu[h, u, st] = wf[u % 2, pl.ds(first, 8, stride=16), :]
-
-    pl.semaphore_wait(bar, 1 + (CHIPS - 1) + (PLANE - 2))
+                wu[h, st, u] = wf[u % 2, pl.ds(first, 8, stride=16), :]
+
+    pl.semaphore_wait(bar, 1 + (CHIPS - 1) + (PLANE - 2) + (REPL - 1))
 
     part = pl.ds(pl.multiple_of(8 * c, 8), 8)
-    s_w = send(wu.at[1 - c, d], wpair.at[:, part], sib_s.at[0], sib_r.at[0], sibling)
+    s_w = send(wu.at[1 - c, 0, d], wpair.at[0, part], sib_s.at[0], sib_r.at[0], sibling)
+    s_v = send(wu.at[1 - c, 1], wpair.at[pl.ds(1, REPL), part], sib_s.at[5], sib_r.at[5], sibling)
     s_x = send(x_hbm.at[0, :, theirs], xb.at[my_rows], sib_s.at[1], sib_r.at[1], sibling)
     s_c = send(cot_hbm.at[0, :, theirs], cotb.at[my_rows], sib_s.at[2], sib_r.at[2], sibling)
-    wpair[:, part, :] = wu[c, d]
+    my16 = pl.ds(pl.multiple_of(16 * p, 16), 16)
+    wpair[0, part, :] = wu[c, 0, d]
     s_w.wait_recv()
-    my16 = pl.ds(pl.multiple_of(16 * p, 16), 16)
-    mine_w = W.at[d // 2, :, my16, lanes_of(d)]
-    mine_w[...] = wpair[...].astype(BF16)
+    mine_w = W.at[0, d // 2, my16, lanes_of(d)]
+    mine_w[...] = wpair[0].astype(BF16)
 
     @pl.loop(1, DEPTH)
     def _(j):
         send(mine_w, mine_w, c1_s, c1_r, deep((z + j) % DEPTH))
 
-    seven = wsend.at[0, :, pl.ds(0, 16 * (DEPTH - 1)), pl.ds(0, 128)]
+    seven = wsend.at[0, 0, pl.ds(0, 16 * (DEPTH - 1)), pl.ds(0, 128)]
     pending.append((seven, c1_s))
+    wpair[1:, part, :] = wu[c, 1]
+    s_v.wait_recv()
+    for u in range(REPL):
+        W[1, u // 2, my16, lane_tile(u % 2)] = wpair[1 + u].astype(BF16)
+    across = (p + DEPTH) % CHIPS
+    rows_a = W.at[1, :, my16]
+    rows_b = W.at[1, :, pl.ds(pl.multiple_of(16 * across, 16), 16)]
+    send(rows_a, rows_a, za_s.at[0], za_r.at[0], chip(across))
+    pending.append((rows_a, za_s.at[0]))
+
+    @pl.loop(1, DEPTH)
+    def _(j):
+        send(rows_a, rows_a, za_s.at[1], za_r.at[1], deep((z + j) % DEPTH))
 
     ld_x.wait()
     s_x.wait_recv()
@@ -174,15 +193,23 @@
         for k in range(TILES):
             xs[3 + r, :, lane_tile(k)] = nat[k, pl.ds(r, 8, stride=R), :]
 
+    wait_for(rows_b, za_r.at[0])
+
+    @pl.loop(1, DEPTH)
+    def _(j):
+        send(rows_b, rows_b, za_s.at[1], za_r.at[1], deep((z + j) % DEPTH))
+
+    fourteen = wsend.at[1, :, pl.ds(0, 16 * 2 * (DEPTH - 1))]
+    pending.append((fourteen, za_s.at[1]))
     wait_for(seven, c1_r)
     fifteen = frecv.at[0, pl.ds(0, PLANE - 1)]
-    for st in range(STAGES):
-        @pl.loop(1, PLANE)
-        def _(j):
-            mine_s = W.at[d // 2, st, rows_of(y // 2), lanes_of(d)]
-            send(mine_s, mine_s, c2_s.at[st], c2_r.at[st], plane(j)[0])
-
-        pending.append((fifteen, c2_s.at[st]))
+    mine_s = W.at[0, d // 2, rows_of(y // 2), lanes_of(d)]
+
+    @pl.loop(1, PLANE)
+    def _(j):
+        send(mine_s, mine_s, c2_s, c2_r, plane(j)[0])
+
+    pending.append((fifteen, c2_s))
 
     ld_c.wait()
     s_c.wait_recv()
@@ -231,7 +258,7 @@
     def gates(b):
         st, k = b // 2, 2 * (b % 2)
         for g in range(2):
-            pre[2 * b + g] = jnp.dot(mb[:, block(b)], W[k + g, st], preferred_element_type=F32)
+            pre[2 * b + g] = jnp.dot(mb[:, block(b)], W[st, k + g], preferred_element_type=F32)
         nr = jnp.broadcast_to(neg8rate[:, block(b)], (8, BW))
         ba = jnp.broadcast_to(gate_b[0:1, block(b)], (8, BW))
         bx = jnp.broadcast_to(gate_b[1:2, block(b)], (8, BW))
@@ -294,7 +321,7 @@
             dsend[st, 1, 4 + k : 5 + k, :] = bk[0:1, lane_tile(lh)]
 
     for st in range(STAGES):
-        wait_for(fifteen, c2_r.at[st])
+        wait_for(*((fifteen, c2_r) if st == 0 else (fourteen, za_r.at[1])))
         for b in (2 * st, 2 * st + 1):
             gates(b)
 
@@ -348,13 +375,13 @@
         _, t_sum, a_sum, x_sum = lax.fori_loop(0, R // 2, down, (kin, zero, zero, zero))
         sums.append([t_sum, a_sum, x_sum])
         for g in range(2):
-            wsend[k + g, st] = jnp.dot(mt[b], gp[2 * b + g], preferred_element_type=F32).astype(BF16)
+            wsend[st, k + g] = jnp.dot(mt[b], gp[2 * b + g], preferred_element_type=F32).astype(BF16)
 
     def through(b):
         st, k = b // 2, 2 * (b % 2)
         nt = (((1,), (1,)), ((), ()))
-        back = lax.dot_general(gp[2 * b], W[k, st], nt, preferred_element_type=F32)
-        back = back + lax.dot_general(gp[2 * b + 1], W[k + 1, st], nt, preferred_element_type=F32)
+        back = lax.dot_general(gp[2 * b], W[st, k], nt, preferred_element_type=F32)
+        back = back + lax.dot_general(gp[2 * b + 1], W[st, k + 1], nt, preferred_element_type=F32)
         gm[0:R, :, block(b)] = gm[0:R, :, block(b)] + back.reshape(R, 8, BW)
 
     for st in range(STAGES):
@@ -375,12 +402,12 @@
         def _(j):
             dev, to_h, to_d = plane(j)
             send(
-                wsend.at[to_d // 2, st, rows_of(to_h), lanes_of(to_d)],
+                wsend.at[st, to_d // 2, rows_of(to_h), lanes_of(to_d)],
                 frecv.at[st, spot], f_s.at[st], f_r.at[st], dev,
             )
 
         pending.append((fifteen, f_s.at[st]))
-        frecv[st, spot] = wsend[d // 2, st, rows_of(y // 2), lanes_of(d)]
+        frecv[st, spot] = wsend[st, d // 2, rows_of(y // 2), lanes_of(d)]
         for b in (2 * st, 2 * st + 1):
             through(b)
 
@@ -471,33 +498,37 @@
     pending.append((szrecv.at[pl.ds(0, DEPTH - 1)], zs_s))
     szrecv[z] = ssum[...]
     fold(1)
-    wait_for(szrecv.at[pl.ds(0, DEPTH - 1)], zs_r)
-    small = jnp.sum(szrecv[...], 0)
-    for st in range(STAGES):
+
+    def spread(n, tile):
+        G[d, c, :, lane_tile(n)] = tile(c)[...]
+
+        @pl.loop(1, 2 * REPL)
+        def _(j):
+            to_c = (c + j // REPL) % 2
+            dev = {"ctx": 2 * p + to_c, "dp": (d + j) % REPL}
+            send(tile(to_c), G.at[d, c, :, lane_tile(n)], g_s.at[n], g_r.at[n], dev)
+
+        pending.append((srecv.at[pl.ds(0, 2 * REPL - 1)], g_s.at[n]))
+
+    def finish(st):
         wait_for(zrecv.at[st, pl.ds(0, DEPTH - 1)], z_r.at[st])
-    other = pl.ds(pl.multiple_of(8 * (1 - c), 8), 8)
-    for st in range(STAGES):
         whole = zrecv[st, 0].astype(F32)
         for j in range(1, DEPTH):
             whole = whole + zrecv[st, j].astype(F32)
-        own[...] = whole
-        G[d, c, :, lane_tile(st)] = own[part, :]
-        fin[:, lane_tile(st)] = own[other, :]
-    G[d, c, :, lane_tile(STAGES)] = small
-    fin[:, lane_tile(STAGES)] = small
-    s_f = send(fin, G.at[d, c], sib_s.at[4], sib_r.at[4], sibling)
-    s_f.wait_recv()
-
-    @pl.loop(1, REPL)
-    def _(j):
-        send(G.at[d], G.at[d], g_s, g_r, peer((d + j) % REPL))
-
-    pending.append((G.at[pl.ds(0, REPL - 1)], g_s))
-    wait_for(G.at[pl.ds(0, REPL - 1)], g_r)
+        own[st] = whole
+        spread(st, lambda core: own.at[st, pl.ds(pl.multiple_of(8 * core, 8), 8)])
+
+    finish(0)
+    wait_for(szrecv.at[pl.ds(0, DEPTH - 1)], zs_r)
+    fin[...] = jnp.sum(szrecv[...], 0)
+    spread(STAGES, lambda core: fin)
+    finish(1)
+    for n in range(STAGES + 1):
+        wait_for(srecv.at[pl.ds(0, 2 * REPL - 1)], g_r.at[n])
     st_a = pltpu.make_async_copy(G, all_hbm, lsem.at[4])
     st_a.start()
 
-    for cp in [s_w, s_x, s_c, s_g, s_f]:
+    for cp in [s_w, s_v, s_x, s_c, s_g]:
         cp.wait_send()
     s_g.wait_recv()
     for ref, sem in pending:
@@ -505,36 +536,46 @@
     st_a.wait()
 
 
-def last_kernel(gi_in, all_ref, gi_out, gw_out, dec_out, bias_out, taps_out, shift_out, gws, via, l_sem, s_sem):
+def last_kernel(
+    gi_in, all_in, gi_out, gw_out, dec_out, bias_out, taps_out, shift_out,
+    all_ref, gws, gw, dec, bias, taps, shift, via, l_sem, s_sem,
+):
+    get = pltpu.make_async_copy(all_in, all_ref, l_sem.at[4])
+    get.start()
     parts = [pl.ds(k * (ROWS // 4), ROWS // 4) for k in range(4)]
     loads = [pltpu.make_async_copy(gi_in.at[at], via.at[at], l_sem.at[k]) for k, at in enumerate(parts)]
     stores = [pltpu.make_async_copy(via.at[at], gi_out.at[0, at], s_sem.at[k]) for k, at in enumerate(parts)]
     for cp in loads:
         cp.start()
-    for k in range(4):
-        loads[k].wait()
-        stores[k].start()
+    get.wait()
     for h in range(2):
         for u in range(8):
             at = slice(h * HALF + 128 * u, h * HALF + 128 * (u + 1))
             v = all_ref[u, h, :, BW:]
-            dec_out[:, at] = v[0:1]
-            bias_out[:, at] = v[1:3]
-            taps_out[:, at] = v[3:7]
-            shift_out[:, at] = v[7:8]
+            dec[:, at] = v[0:1]
+            bias[:, at] = v[1:3]
+            taps[:, at] = v[3:7]
+            shift[:, at] = v[7:8]
             for st in range(STAGES):
                 first = ((u // 2) % 2) * 8 + 4 * h + 2 * st + u // 4
                 gws[u % 2, pl.ds(first, 8, stride=16), :] = all_ref[u, h, :, lane_tile(st)]
+    for n, (src, dst) in enumerate(((dec, dec_out), (bias, bias_out), (taps, taps_out), (shift, shift_out))):
+        stores.append(pltpu.make_async_copy(src, dst, s_sem.at[4 + n]))
+        stores[-1].start()
+    for k in range(4):
+        loads[k].wait()
+        stores[k].start()
     for i in range(8):
         for g in range(2):
             for lh in range(2):
-                gw_out[i, g, :, lane_tile(lh)] = gws[lh, i * 16 + g * 8 : i * 16 + g * 8 + 8, :]
+                gw[i, g, :, lane_tile(lh)] = gws[lh, i * 16 + g * 8 : i * 16 + g * 8 + 8, :]
+    stores.append(pltpu.make_async_copy(gw, gw_out, s_sem.at[8]))
+    stores[-1].start()
     for cp in stores:
         cp.wait()
 
 
 def per_device(inputs, gate_weight, gate_bias, decay_param, conv_weight, conv_bias, cotangent):
-    vmem = pl.BlockSpec(memory_space=pltpu.VMEM)
     hbm = pl.BlockSpec(memory_space=pltpu.HBM)
     dma = pltpu.SemaphoreType.DMA
     big = pltpu.VMEM((R, 8, HALF), F32)
@@ -556,9 +597,9 @@
             pltpu.VMEM((SPAN, HALF), BF16),
             pltpu.VMEM((8, 2, 8, BW), BF16),
             pltpu.VMEM((2, 128, 128), F32),
-            pltpu.VMEM((2, REPL, STAGES, 8, 128), F32),
-            pltpu.VMEM((STAGES, 16, 128), F32),
-            pltpu.VMEM((4, STAGES, BW, BW), BF16),
+            pltpu.VMEM((2, STAGES, REPL, 8, 128), F32),
+            pltpu.VMEM((1 + REPL, 16, 128), F32),
+            pltpu.VMEM((STAGES, 4, BW, BW), BF16),
             pltpu.VMEM((16, HALF), BF16),
             pltpu.VMEM((TILES, SPAN, 128), F32),
             pltpu.VMEM((TILES, SPAN, 128), F32),
@@ -575,22 +616,22 @@
             pltpu.VMEM((STAGES, 2, 4, 128), F32),
             pltpu.VMEM((8, HALF), F32),
             pltpu.VMEM((8, HALF), F32),
-            pltpu.VMEM((4, STAGES, BW, BW), BF16),
+            pltpu.VMEM((STAGES, 4, BW, BW), BF16),
             pltpu.VMEM((STAGES, PLANE, 128, 128), BF16),
-            pltpu.VMEM((16, 128), F32),
+            pltpu.VMEM((STAGES, 16, 128), F32),
             pltpu.VMEM((STAGES, DEPTH, 16, 128), BF16),
             pltpu.VMEM((STAGES, DEPTH, 16, 128), BF16),
             pltpu.VMEM((8, 8, 128), F32),
             pltpu.VMEM((PLANE, 8, 128), F32),
             pltpu.VMEM((8, 128), F32),
             pltpu.VMEM((DEPTH, 8, 128), F32),
-            pltpu.VMEM((8, BW + 128), F32),
+            pltpu.VMEM((8, 128), F32),
             pltpu.VMEM((REPL, 2, 8, BW + 128), F32),
             pltpu.VMEM((SPAN, HALF), BF16),
             dma((9,)), dma((7,)), dma((7,)),
-            dma, dma, dma, dma, dma((STAGES,)), dma((STAGES,)),
+            dma, dma, dma, dma, dma((2,)), dma((2,)), dma, dma,
             dma((STAGES,)), dma((STAGES,)), dma, dma, dma((STAGES,)), dma((STAGES,)), dma, dma,
-            dma((STAGES,)), dma((STAGES,)), dma, dma, dma, dma,
+            dma((STAGES,)), dma((STAGES,)), dma, dma, dma((STAGES + 1,)), dma((STAGES + 1,)),
         ],
         compiler_params=pltpu.CompilerParams(
             collective_id=0, has_side_effects=True, vmem_limit_bytes=60 * 2**20
@@ -610,9 +651,20 @@
             jax.ShapeDtypeStruct((4, WIDTH), F32),
             jax.ShapeDtypeStruct((1, WIDTH), F32),
         ),
-        in_specs=[hbm, vmem],
-        out_specs=(hbm,) + (vmem,) * 5,
-        scratch_shapes=[pltpu.VMEM((2, 128, 128), F32), pltpu.VMEM((ROWS, WIDTH), BF16), dma((4,)), dma((4,))],
+        in_specs=[hbm] * 2,
+        out_specs=(hbm,) * 6,
+        scratch_shapes=[
+            pltpu.VMEM((REPL, 2, 8, BW + 128), F32),
+            pltpu.VMEM((2, 128, 128), F32),
+            pltpu.VMEM((8, 2, 8, BW), F32),
+            pltpu.VMEM((1, WIDTH), F32),
+            pltpu.VMEM((2, WIDTH), F32),
+            pltpu.VMEM((4, WIDTH), F32),
+            pltpu.VMEM((1, WIDTH), F32),
+            pltpu.VMEM((ROWS, WIDTH), BF16),
+            dma((5,)),
+            dma((9,)),
+        ],
         compiler_params=pltpu.CompilerParams(vmem_limit_bytes=60 * 2**20),
     )(gi, packed)
     return gi, gw, dec.reshape(WIDTH), bias, taps, shift.reshape(WIDTH)

time: 68.1 us -> 62.5 us (0.918)
  Pallas kernels: 67.3 us -> 61.7 us
    pallas_call x1, Pallas kernels: 63.9 us -> 59.7 us  [per_device(): pl.pallas_call(main_kernel, name='main', out_shape=(jax.ShapeDtypeStruct(...]
    pallas_call x1, Pallas kernels: 3.42 us -> 2.02 us  [per_device(): pl.pallas_call(last_kernel, name='last', out_shape=(jax.ShapeDtypeStruct(...]
where the time goes in v4:
time: 62.5 us; the launch traced here: 62.4 us
  Pallas kernels  61.7 us (99%)
  between operations  0.64 us (1%)
    pallas_call x1, Pallas kernels, per_device(): pl.pallas_call(main_kernel, name='main', out_shape=(jax.ShapeDtypeStruct(...  59.7 us
    pallas_call x1, Pallas kernels, per_device(): pl.pallas_call(last_kernel, name='last', out_shape=(jax.ShapeDtypeStruct(...  2.02 us

profile of v4, /device:TPU:1, one launch (start us, length us, event | category | flops | bytes accessed | tf_op | source)
XLA Modules:
  0.0 62.4 jit_solution(10660194834367220139)
XLA Ops:
  0.6 59.7 %main.1 = (bf16[128,2048]{1,0:T(8,128)(2,1)}, f32[8,2,8,384]{3,2,1,0:T(8,128)}) custom-call(bf16[1,128,2048]{2,1,0:T(8,128)(2,1)} %x_hbm.1, bf16[8,2,8,256]{3,2,1,0:T(8,128)(2,1)} %w_hbm.1, f32[2,2048]{1,0:T(2,128)} %gb_hbm.1, f32[1,2048]{1,0:T(1,128)} %bitcast.4, f32[4,2048]{1,0:T(4,128)} %cw_hbm.1, f32[1,2048]{1,0:T(1,128)} %bitcast.5, ...), custom_call_target="tpu_custom_call" | custom-call | tf_op jit(solution)/shard_map/main/pallas_call | solution.py:582
  60.3 2.0 %last.1 = (bf16[1,128,2048]{2,1,0:T(8,128)(2,1)}, f32[8,2,8,256]{3,2,1,0:T(8,128)}, f32[1,2048]{1,0:T(1,128)}, f32[2,2048]{1,0:T(2,128)}, f32[4,2048]{1,0:T(4,128)}, /*index=5*/f32[1,2048]{1,0:T(1,128)}) custom-call(bf16[128,2048]{1,0:T(8,128)(2,1)} %get-tuple-element.14.gi_in, f32[8,2,8,384]{3,2,1,0:T(8,128)} %get-tuple-element.15.all_in), custom_call_target="tpu_custom_call" | custom-call | tf_op jit(solution)/shard_map/last/pallas_call | solution.py:643

commit v5 on v4

--- a/solution.py
+++ b/solution.py
@@ -55,12 +55,12 @@
 
 def main_kernel(
     x_hbm, w_hbm, gb_hbm, lam_hbm, cw_hbm, cb_hbm, cot_hbm,
-    gi_hbm, all_hbm,
+    gi_hbm, all_hbm, small_hbm,
     gb_ref, lam_ref, cw_ref, cb_ref, xb, cotb, wsh, wf, wu, wpair, W, xhalo, nat, natc, xs, cs, mb, mt, pre,
     dec, drv, qq, m1, m2, m3, oma, hp, gp, gm, dsend, drecv, sin, ghs, ghr,
-    wsend, frecv, own, fsum, zrecv, ssend, srecv, ssum, szrecv, fin, G, gib,
+    wsend, frecv, brecv, bsum, bz, own, fsum, zrecv, ssend, srecv, ssum, szrecv, fin, tiles, G, gib,
     lsem, sib_s, sib_r, c1_s, c1_r, hal_s, hal_r, za_s, za_r, c2_s, c2_r, d_s, d_r, e_s, e_r,
-    f_s, f_r, fs_s, fs_r, z_s, z_r, zs_s, zs_r, g_s, g_r,
+    f_s, f_r, b_s, b_r, fs_s, fs_r, z_s, z_r, g_s, g_r,
 ):
     ctx = lax.axis_index("ctx")
     d = lax.axis_index("dp")
@@ -88,6 +88,9 @@
 
     def rows_of(h):
         return pl.ds(pl.multiple_of(128 * h, 128), 128)
+
+    def rows16(j):
+        return pl.ds(pl.multiple_of(16 * j, 16), 16)
 
     def lanes_of(u):
         return pl.ds(pl.multiple_of(128 * (u % 2), 128), 128)
@@ -136,6 +139,10 @@
         lds[-1].start()
     pending = []
 
+    def later(ref, sem):
+        pending.append(lambda: wait_for(ref, sem))
+
+
     ld_w.wait()
     for i in range(8):
         for g in range(2):
@@ -165,8 +172,8 @@
     def _(j):
         send(mine_w, mine_w, c1_s, c1_r, deep((z + j) % DEPTH))
 
-    seven = wsend.at[0, 0, pl.ds(0, 16 * (DEPTH - 1)), pl.ds(0, 128)]
-    pending.append((seven, c1_s))
+    seven = W.at[0, 0, pl.ds(0, 16 * (DEPTH - 1)), pl.ds(0, 128)]
+    later(seven, c1_s)
     wpair[1:, part, :] = wu[c, 1]
     s_v.wait_recv()
     for u in range(REPL):
@@ -175,16 +182,34 @@
     rows_a = W.at[1, :, my16]
     rows_b = W.at[1, :, pl.ds(pl.multiple_of(16 * across, 16), 16)]
     send(rows_a, rows_a, za_s.at[0], za_r.at[0], chip(across))
-    pending.append((rows_a, za_s.at[0]))
-
-    @pl.loop(1, DEPTH)
-    def _(j):
-        send(rows_a, rows_a, za_s.at[1], za_r.at[1], deep((z + j) % DEPTH))
+    later(rows_a, za_s.at[0])
+
+    def at_depth(side, by):
+        q = (p - z if side == 0 else across - z) + (z + by + DEPTH) % DEPTH
+        return pl.ds(pl.multiple_of(16 * q, 16), 16)
+
+    def near(side):
+        rows = W.at[1, :, at_depth(side, 0)]
+        for by in (1, -1):
+            send(rows, rows, za_s.at[1], za_r.at[1], deep((z + by + DEPTH) % DEPTH))
+        for by in (2, -2):
+            arrive = za_r.at[2 + 2 * side + (0 if by > 0 else 1)]
+            send(rows, rows, za_s.at[1], arrive, deep((z + by + DEPTH) % DEPTH))
+
+    def onward(side):
+        for way, by in ((0, 1), (1, -1)):
+            rows = W.at[1, :, at_depth(side, -2 * by)]
+            wait_for(rows, za_r.at[2 + 2 * side + way])
+            send(rows, rows, za_s.at[1], za_r.at[1], deep((z + by + DEPTH) % DEPTH))
+            half = W.at[1, pl.ds(2 * way, 2), at_depth(side, -2 * by)]
+            send(half, half, za_s.at[1], za_r.at[1], deep((z + 2 * by + DEPTH) % DEPTH))
+
+    near(0)
 
     ld_x.wait()
     s_x.wait_recv()
     send(xb.at[pl.ds(SPAN - 16, 16)], xhalo, hal_s, hal_r, chip((p + 1) % CHIPS))
-    pending.append((xhalo, hal_s))
+    later(xhalo, hal_s)
     for k in range(TILES):
         nat[k] = xb[:, lane_tile(k)].astype(F32)
 
@@ -195,12 +220,9 @@
 
     wait_for(rows_b, za_r.at[0])
 
-    @pl.loop(1, DEPTH)
-    def _(j):
-        send(rows_b, rows_b, za_s.at[1], za_r.at[1], deep((z + j) % DEPTH))
-
-    fourteen = wsend.at[1, :, pl.ds(0, 16 * 2 * (DEPTH - 1))]
-    pending.append((fourteen, za_s.at[1]))
+    near(1)
+    later(W.at[1, :, pl.ds(0, 16 * 14)], za_s.at[1])
+    ten = W.at[1, :, pl.ds(0, 16 * 10)]
     wait_for(seven, c1_r)
     fifteen = frecv.at[0, pl.ds(0, PLANE - 1)]
     mine_s = W.at[0, d // 2, rows_of(y // 2), lanes_of(d)]
@@ -209,8 +231,9 @@
     def _(j):
         send(mine_s, mine_s, c2_s, c2_r, plane(j)[0])
 
-    pending.append((fifteen, c2_s))
-
+    later(fifteen, c2_s)
+    onward(0)
+    onward(1)
     ld_c.wait()
     s_c.wait_recv()
     for k in range(TILES):
@@ -321,7 +344,7 @@
             dsend[st, 1, 4 + k : 5 + k, :] = bk[0:1, lane_tile(lh)]
 
     for st in range(STAGES):
-        wait_for(*((fifteen, c2_r) if st == 0 else (fourteen, za_r.at[1])))
+        wait_for(*((fifteen, c2_r) if st == 0 else (ten, za_r.at[1])))
         for b in (2 * st, 2 * st + 1):
             gates(b)
 
@@ -330,7 +353,7 @@
             to = (p + j) % CHIPS
             send(dsend.at[st, jnp.where(to > p, 0, 1)], drecv.at[st, p], d_s.at[st], d_r.at[st], chip(to))
 
-        pending.append((drecv.at[st, pl.ds(0, CHIPS - 1)], d_s.at[st]))
+        later(drecv.at[st, pl.ds(0, CHIPS - 1)], d_s.at[st])
         drecv[st, p] = jnp.zeros((8, 128), F32)
 
     sums = []
@@ -375,7 +398,9 @@
         _, t_sum, a_sum, x_sum = lax.fori_loop(0, R // 2, down, (kin, zero, zero, zero))
         sums.append([t_sum, a_sum, x_sum])
         for g in range(2):
-            wsend[st, k + g] = jnp.dot(mt[b], gp[2 * b + g], preferred_element_type=F32).astype(BF16)
+            grad = jnp.dot(mt[b], gp[2 * b + g], preferred_element_type=F32).astype(BF16)
+            for h in range(2):
+                wsend[st, k + g, h] = grad[128 * h : 128 * (h + 1)]
 
     def through(b):
         st, k = b // 2, 2 * (b % 2)
@@ -401,20 +426,40 @@
         @pl.loop(1, PLANE)
         def _(j):
             dev, to_h, to_d = plane(j)
-            send(
-                wsend.at[st, to_d // 2, rows_of(to_h), lanes_of(to_d)],
-                frecv.at[st, spot], f_s.at[st], f_r.at[st], dev,
-            )
-
-        pending.append((fifteen, f_s.at[st]))
-        frecv[st, spot] = wsend[st, d // 2, rows_of(y // 2), lanes_of(d)]
+
+            def go():
+                send(
+                    wsend.at[st, to_d // 2, to_h, :, lanes_of(to_d)],
+                    frecv.at[st, spot], f_s.at[st], f_r.at[st], dev,
+                )
+
+            if st == 0:
+                pl.when(to_d < 4)(go)
+            else:
+                go()
+
+        if st == 0:
+            @pl.when(y % 2 == 0)
+            def _():
+                frecv[st, spot] = wsend[st, d // 2, y // 2, :, lanes_of(d)]
+
+            @pl.loop(1, DEPTH)
+            def _(j):
+                to = (z + j) % DEPTH
+                send(wsend.at[0, pl.ds(2, 2), :, rows16(to)], brecv.at[z], b_s.at[0], b_r.at[0], deep(to))
+
+            later(brecv.at[pl.ds(0, DEPTH - 1)], b_s.at[0])
+            brecv[z] = wsend[0, 2:4, :, rows16(z)]
+        else:
+            later(fifteen, f_s.at[st])
+            frecv[st, spot] = wsend[st, d // 2, y // 2, :, lanes_of(d)]
         for b in (2 * st, 2 * st + 1):
             through(b)
 
     for k in range(3):
         ghs[k : k + 1, :] = gm[k, 0:1, :]
     send(ghs, ghr, e_s, e_r, chip((p + CHIPS - 1) % CHIPS))
-    pending.append((ghr, e_s))
+    later(ghr, e_s)
 
     sig = 1.0 / (1.0 + jnp.exp(lam))
     for b in range(NB):
@@ -435,20 +480,20 @@
         for lh in range(2):
             ssend[2 * b + lh] = rows[:, lane_tile(lh)]
 
-    @pl.loop(1, PLANE)
-    def _(j):
-        dev, _, to_d = plane(j)
-        send(ssend.at[to_d], srecv.at[spot], fs_s, fs_r, dev)
-
-    pending.append((srecv.at[pl.ds(0, PLANE - 1)], fs_s))
-    srecv[spot] = ssend[d]
+    @pl.loop(1, DEPTH)
+    def _(j):
+        to = (z + j) % DEPTH
+        send(ssend.at[to], srecv.at[z], fs_s.at[0], fs_r.at[0], deep(to))
+
+    later(srecv.at[pl.ds(0, DEPTH - 1)], fs_s.at[0])
+    srecv[z] = ssend[z]
 
     def fold(st):
         wait_for(fifteen, f_r.at[st])
 
         @pl.loop(0, DEPTH)
         def _(i):
-            at = pl.ds(pl.multiple_of(16 * i, 16), 16)
+            at = rows16(i)
             v = frecv[st, 0, at, :].astype(F32)
             for u in range(1, PLANE):
                 v = v + frecv[st, u, at, :].astype(F32)
@@ -459,10 +504,8 @@
             to = (z + j) % DEPTH
             send(fsum.at[st, to], zrecv.at[st, z], z_s.at[st], z_r.at[st], deep(to))
 
-        pending.append((zrecv.at[st, pl.ds(0, DEPTH - 1)], z_s.at[st]))
         zrecv[st, z] = fsum[st, z]
 
-    fold(0)
     wait_for(ghr, e_r)
     halo = ghr[...]
     halo = jnp.where(p == CHIPS - 1, jnp.zeros_like(halo), halo)
@@ -486,18 +529,67 @@
     s_g = send(gib.at[sib_rows], gi_hbm.at[:, mine], sib_s.at[3], sib_r.at[3], sibling)
     st_g = pltpu.make_async_copy(gib.at[my_rows], gi_hbm.at[:, mine], lsem.at[3])
     st_g.start()
-    pending.append((gib.at[my_rows], lsem.at[3]))
-
-    wait_for(srecv.at[pl.ds(0, PLANE - 1)], fs_r)
+    later(gib.at[my_rows], lsem.at[3])
+
+    wait_for(srecv.at[pl.ds(0, DEPTH - 1)], fs_r.at[0])
     ssum[...] = jnp.sum(srecv[...], 0)
 
+    @pl.loop(1, PLANE)
+    def _(j):
+        send(ssum, szrecv.at[spot], fs_s.at[1], fs_r.at[1], plane(j)[0])
+
+    later(szrecv.at[pl.ds(0, PLANE - 1)], fs_s.at[1])
+    szrecv[spot] = ssum[...]
+
+    pl.when(y % 2 == 0)(lambda: fold(0))
+    wait_for(brecv.at[pl.ds(0, DEPTH - 1)], b_r.at[0])
+    for k in range(2):
+        for h in range(2):
+            v = brecv[0, k, h].astype(F32)
+            for j in range(1, DEPTH):
+                v = v + brecv[j, k, h].astype(F32)
+            for lh in range(2):
+                bsum[h, 2 * k + lh] = v[:, lane_tile(lh)].astype(BF16)
+
+    @pl.loop(1, PLANE)
+    def _(j):
+        dev, to_h, to_d = plane(j)
+
+        @pl.when(to_d >= 4)
+        def _():
+            send(bsum.at[to_h, to_d % 4], bz.at[spot], b_s.at[1], b_r.at[1], dev)
+
+    @pl.when(y % 2 == 1)
+    def _():
+        bz[spot] = bsum[y // 2, x]
+
+    wait_for(szrecv.at[pl.ds(0, PLANE - 1)], fs_r.at[1])
+    fin[...] = jnp.sum(szrecv[...], 0)
+
     @pl.loop(1, DEPTH)
     def _(j):
-        send(ssum, szrecv.at[z], zs_s, zs_r, deep((z + j) % DEPTH))
-
-    pending.append((szrecv.at[pl.ds(0, DEPTH - 1)], zs_s))
-    szrecv[z] = ssum[...]
+        send(fin, tiles.at[c, z], fs_s.at[2], fs_r.at[2], deep((z + j) % DEPTH))
+
+    later(tiles.at[0, pl.ds(0, DEPTH - 1)], fs_s.at[2])
+    tiles[c, z] = fin[...]
     fold(1)
+    later(zrecv.at[1, pl.ds(0, DEPTH - 1)], z_s.at[1])
+
+    @pl.when(y % 2 == 0)
+    def _():
+        wait_for(zrecv.at[0, pl.ds(0, DEPTH - 1)], z_s.at[0])
+        wait_for(zrecv.at[0, pl.ds(0, DEPTH - 1)], z_r.at[0])
+        wait_for(frecv.at[0, pl.ds(0, 7)], f_s.at[0])
+        wait_for(bz.at[pl.ds(0, 8)], b_s.at[1])
+
+    @pl.when(y % 2 == 1)
+    def _():
+        wait_for(bz.at[pl.ds(0, PLANE - 1)], b_r.at[1])
+        wait_for(frecv.at[0, pl.ds(0, 8)], f_s.at[0])
+        wait_for(bz.at[pl.ds(0, 7)], b_s.at[1])
+
+
+    srecv15 = szrecv.at[pl.ds(0, 2 * REPL - 1)]
 
     def spread(n, tile):
         G[d, c, :, lane_tile(n)] = tile(c)[...]
@@ -508,50 +600,61 @@
             dev = {"ctx": 2 * p + to_c, "dp": (d + j) % REPL}
             send(tile(to_c), G.at[d, c, :, lane_tile(n)], g_s.at[n], g_r.at[n], dev)
 
-        pending.append((srecv.at[pl.ds(0, 2 * REPL - 1)], g_s.at[n]))
+        later(srecv15, g_s.at[n])
+
+    def total(st, parts, count):
+        whole = parts(0).astype(F32)
+        for j in range(1, count):
+            whole = whole + parts(j).astype(F32)
+        own[st] = whole
 
     def finish(st):
-        wait_for(zrecv.at[st, pl.ds(0, DEPTH - 1)], z_r.at[st])
-        whole = zrecv[st, 0].astype(F32)
-        for j in range(1, DEPTH):
-            whole = whole + zrecv[st, j].astype(F32)
-        own[st] = whole
         spread(st, lambda core: own.at[st, pl.ds(pl.multiple_of(8 * core, 8), 8)])
 
+    pl.when(y % 2 == 0)(lambda: total(0, lambda j: zrecv[0, j], DEPTH))
+    pl.when(y % 2 == 1)(lambda: total(0, lambda j: bz[j], PLANE))
     finish(0)
-    wait_for(szrecv.at[pl.ds(0, DEPTH - 1)], zs_r)
-    fin[...] = jnp.sum(szrecv[...], 0)
-    spread(STAGES, lambda core: fin)
+    wait_for(tiles.at[0, pl.ds(0, DEPTH - 1)], fs_r.at[2])
+    s_t = send(tiles.at[c], tiles.at[c], sib_s.at[4], sib_r.at[4], sibling)
+    wait_for(zrecv.at[1, pl.ds(0, DEPTH - 1)], z_r.at[1])
+    total(1, lambda j: zrecv[1, j], DEPTH)
     finish(1)
-    for n in range(STAGES + 1):
-        wait_for(srecv.at[pl.ds(0, 2 * REPL - 1)], g_r.at[n])
+    s_t.wait_recv()
+    st_t = pltpu.make_async_copy(tiles, small_hbm, lsem.at[9])
+    st_t.start()
+    for n in range(STAGES):
+        wait_for(srecv15, g_r.at[n])
     st_a = pltpu.make_async_copy(G, all_hbm, lsem.at[4])
     st_a.start()
 
-    for cp in [s_w, s_v, s_x, s_c, s_g]:
+    for cp in [s_w, s_v, s_x, s_c, s_g, s_t]:
         cp.wait_send()
     s_g.wait_recv()
-    for ref, sem in pending:
-        wait_for(ref, sem)
+    for finish_one in pending:
+        finish_one()
     st_a.wait()
+    st_t.wait()
 
 
 def last_kernel(
-    gi_in, all_in, gi_out, gw_out, dec_out, bias_out, taps_out, shift_out,
-    all_ref, gws, gw, dec, bias, taps, shift, via, l_sem, s_sem,
+    gi_in, all_in, small_in, gi_out, gw_out, dec_out, bias_out, taps_out, shift_out,
+    all_ref, small_ref, gws, gw, dec, bias, taps, shift, via, l_sem, s_sem,
 ):
     get = pltpu.make_async_copy(all_in, all_ref, l_sem.at[4])
     get.start()
+    get_small = pltpu.make_async_copy(small_in, small_ref, l_sem.at[5])
+    get_small.start()
     parts = [pl.ds(k * (ROWS // 4), ROWS // 4) for k in range(4)]
     loads = [pltpu.make_async_copy(gi_in.at[at], via.at[at], l_sem.at[k]) for k, at in enumerate(parts)]
     stores = [pltpu.make_async_copy(via.at[at], gi_out.at[0, at], s_sem.at[k]) for k, at in enumerate(parts)]
     for cp in loads:
         cp.start()
     get.wait()
+    get_small.wait()
     for h in range(2):
         for u in range(8):
             at = slice(h * HALF + 128 * u, h * HALF + 128 * (u + 1))
-            v = all_ref[u, h, :, BW:]
+            v = small_ref[h, u]
             dec[:, at] = v[0:1]
             bias[:, at] = v[1:3]
             taps[:, at] = v[3:7]
@@ -579,15 +682,16 @@
     hbm = pl.BlockSpec(memory_space=pltpu.HBM)
     dma = pltpu.SemaphoreType.DMA
     big = pltpu.VMEM((R, 8, HALF), F32)
-    gi, packed = pl.pallas_call(
+    gi, packed, small = pl.pallas_call(
         main_kernel,
         name="main",
         out_shape=(
             jax.ShapeDtypeStruct((ROWS, WIDTH), BF16),
-            jax.ShapeDtypeStruct((REPL, 2, 8, BW + 128), F32),
+            jax.ShapeDtypeStruct((REPL, 2, 8, BW), F32),
+            jax.ShapeDtypeStruct((2, DEPTH, 8, 128), F32),
         ),
         in_specs=[hbm] * 7,
-        out_specs=(hbm, hbm),
+        out_specs=(hbm,) * 3,
         scratch_shapes=[
             pltpu.VMEM((2, HALF), F32),
             pltpu.VMEM((1, HALF), F32),
@@ -616,22 +720,27 @@
             pltpu.VMEM((STAGES, 2, 4, 128), F32),
             pltpu.VMEM((8, HALF), F32),
             pltpu.VMEM((8, HALF), F32),
-            pltpu.VMEM((STAGES, 4, BW, BW), BF16),
+            pltpu.VMEM((STAGES, 4, 2, 128, BW), BF16),
             pltpu.VMEM((STAGES, PLANE, 128, 128), BF16),
+            pltpu.VMEM((DEPTH, 2, 2, 16, BW), BF16),
+            pltpu.VMEM((2, 4, 16, 128), BF16),
+            pltpu.VMEM((PLANE, 16, 128), BF16),
             pltpu.VMEM((STAGES, 16, 128), F32),
             pltpu.VMEM((STAGES, DEPTH, 16, 128), BF16),
             pltpu.VMEM((STAGES, DEPTH, 16, 128), BF16),
             pltpu.VMEM((8, 8, 128), F32),
+            pltpu.VMEM((DEPTH, 8, 128), F32),
+            pltpu.VMEM((8, 128), F32),
             pltpu.VMEM((PLANE, 8, 128), F32),
             pltpu.VMEM((8, 128), F32),
-            pltpu.VMEM((DEPTH, 8, 128), F32),
-            pltpu.VMEM((8, 128), F32),
-            pltpu.VMEM((REPL, 2, 8, BW + 128), F32),
+            pltpu.VMEM((2, DEPTH, 8, 128), F32),
+            pltpu.VMEM((REPL, 2, 8, BW), F32),
             pltpu.VMEM((SPAN, HALF), BF16),
-            dma((9,)), dma((7,)), dma((7,)),
-            dma, dma, dma, dma, dma((2,)), dma((2,)), dma, dma,
-            dma((STAGES,)), dma((STAGES,)), dma, dma, dma((STAGES,)), dma((STAGES,)), dma, dma,
-            dma((STAGES,)), dma((STAGES,)), dma, dma, dma((STAGES + 1,)), dma((STAGES + 1,)),
+            dma((10,)), dma((7,)), dma((7,)),
+            dma, dma, dma, dma, dma((2,)), dma((6,)), dma, dma,
+            dma((STAGES,)), dma((STAGES,)), dma, dma, dma((STAGES,)), dma((STAGES,)),
+            dma((2,)), dma((2,)), dma((3,)), dma((3,)),
+            dma((STAGES,)), dma((STAGES,)), dma((STAGES,)), dma((STAGES,)),
         ],
         compiler_params=pltpu.CompilerParams(
             collective_id=0, has_side_effects=True, vmem_limit_bytes=60 * 2**20
@@ -651,10 +760,11 @@
             jax.ShapeDtypeStruct((4, WIDTH), F32),
             jax.ShapeDtypeStruct((1, WIDTH), F32),
         ),
-        in_specs=[hbm] * 2,
+        in_specs=[hbm] * 3,
         out_specs=(hbm,) * 6,
         scratch_shapes=[
-            pltpu.VMEM((REPL, 2, 8, BW + 128), F32),
+            pltpu.VMEM((REPL, 2, 8, BW), F32),
+            pltpu.VMEM((2, DEPTH, 8, 128), F32),
             pltpu.VMEM((2, 128, 128), F32),
             pltpu.VMEM((8, 2, 8, BW), F32),
             pltpu.VMEM((1, WIDTH), F32),
@@ -662,11 +772,11 @@
             pltpu.VMEM((4, WIDTH), F32),
             pltpu.VMEM((1, WIDTH), F32),
             pltpu.VMEM((ROWS, WIDTH), BF16),
-            dma((5,)),
+            dma((6,)),
             dma((9,)),
         ],
         compiler_params=pltpu.CompilerParams(vmem_limit_bytes=60 * 2**20),
-    )(gi, packed)
+    )(gi, packed, small)
     return gi, gw, dec.reshape(WIDTH), bias, taps, shift.reshape(WIDTH)
 
 

time: 62.5 us -> 65.3 us (1.045)
  Pallas kernels: 61.7 us -> 64.5 us
    pallas_call x1, Pallas kernels: 59.7 us -> 62.5 us  [per_device(): pl.pallas_call(main_kernel, name='main', out_shape=(jax.ShapeDtypeStruct(...]
where the time goes in v5:
time: 65.3 us; the launch traced here: 65.2 us
  Pallas kernels  64.5 us (99%)
    pallas_call x1, Pallas kernels, per_device(): pl.pallas_call(main_kernel, name='main', out_shape=(jax.ShapeDtypeStruct(...  62.5 us
    pallas_call x1, Pallas kernels, per_device(): pl.pallas_call(last_kernel, name='last', out_shape=(jax.ShapeDtypeStruct(...  2.03 us

profile of v5, /device:TPU:1, one launch (start us, length us, event | category | flops | bytes accessed | tf_op | source)
XLA Modules:
  0.0 65.2 jit_solution(8865971740406750778)
XLA Ops:
  0.6 62.5 %main.1 = (bf16[128,2048]{1,0:T(8,128)(2,1)}, f32[8,2,8,256]{3,2,1,0:T(8,128)}, f32[2,8,8,128]{3,2,1,0:T(8,128)}) custom-call(bf16[1,128,2048]{2,1,0:T(8,128)(2,1)} %x_hbm.1, bf16[8,2,8,256]{3,2,1,0:T(8,128)(2,1)} %w_hbm.1, f32[2,2048]{1,0:T(2,128)} %gb_hbm.1, f32[1,2048]{1,0:T(1,128)} %bitcast.4, f32[4,2048]{1,0:T(4,128)} %cw_hbm.1, f32[1,2048]{1,0:T(1,128)} %bitcast.5, ...), custom_call_target="tpu_custom_call" | custom-call | tf_op jit(solution)/shard_map/main/pallas_call | solution.py:685
  63.1 2.0 %last.1 = (bf16[1,128,2048]{2,1,0:T(8,128)(2,1)}, f32[8,2,8,256]{3,2,1,0:T(8,128)}, f32[1,2048]{1,0:T(1,128)}, f32[2,2048]{1,0:T(2,128)}, f32[4,2048]{1,0:T(4,128)}, /*index=5*/f32[1,2048]{1,0:T(1,128)}) custom-call(bf16[128,2048]{1,0:T(8,128)(2,1)} %get-tuple-element.15.gi_in, f32[8,2,8,256]{3,2,1,0:T(8,128)} %get-tuple-element.16.all_in, ...), custom_call_target="tpu_custom_call" | custom-call | tf_op jit(solution)/shard_map/last/pallas_call | solution.py:752

commit v6 on v5

--- a/solution.py
+++ b/solution.py
@@ -56,9 +56,9 @@
 def main_kernel(
     x_hbm, w_hbm, gb_hbm, lam_hbm, cw_hbm, cb_hbm, cot_hbm,
     gi_hbm, all_hbm, small_hbm,
-    gb_ref, lam_ref, cw_ref, cb_ref, xb, cotb, wsh, wf, wu, wpair, W, xhalo, nat, natc, xs, cs, mb, mt, pre,
+    gb_ref, lam_ref, cw_ref, cb_ref, xb, cotb, wsh, wf, wu, wpair, W0, W1, xhalo, nat, natc, xs, cs, mb, mt, pre,
     dec, drv, qq, m1, m2, m3, oma, hp, gp, gm, dsend, drecv, sin, ghs, ghr,
-    wsend, frecv, brecv, bsum, bz, own, fsum, zrecv, ssend, srecv, ssum, szrecv, fin, tiles, G, gib,
+    wsend, wz, frecv, brecv, bsum, bz, own, fsum, zrecv, ssend, srecv, ssum, szrecv, fin, tiles, G, gib,
     lsem, sib_s, sib_r, c1_s, c1_r, hal_s, hal_r, za_s, za_r, c2_s, c2_r, d_s, d_r, e_s, e_r,
     f_s, f_r, b_s, b_r, fs_s, fs_r, z_s, z_r, g_s, g_r,
 ):
@@ -86,14 +86,8 @@
         to_d = 4 * (to_y % 2) + to_x
         return {"ctx": 2 * (DEPTH * (to_y // 2) + z) + c, "dp": to_d}, to_y // 2, to_d
 
-    def rows_of(h):
-        return pl.ds(pl.multiple_of(128 * h, 128), 128)
-
     def rows16(j):
         return pl.ds(pl.multiple_of(16 * j, 16), 16)
-
-    def lanes_of(u):
-        return pl.ds(pl.multiple_of(128 * (u % 2), 128), 128)
 
     def send(src, dst, ss, rs, dev):
         cp = pltpu.make_async_remote_copy(
@@ -162,34 +156,31 @@
     s_v = send(wu.at[1 - c, 1], wpair.at[pl.ds(1, REPL), part], sib_s.at[5], sib_r.at[5], sibling)
     s_x = send(x_hbm.at[0, :, theirs], xb.at[my_rows], sib_s.at[1], sib_r.at[1], sibling)
     s_c = send(cot_hbm.at[0, :, theirs], cotb.at[my_rows], sib_s.at[2], sib_r.at[2], sibling)
-    my16 = pl.ds(pl.multiple_of(16 * p, 16), 16)
     wpair[0, part, :] = wu[c, 0, d]
     s_w.wait_recv()
-    mine_w = W.at[0, d // 2, my16, lanes_of(d)]
+    mine_w = W0.at[d, y // 2, rows16(z)]
     mine_w[...] = wpair[0].astype(BF16)
 
     @pl.loop(1, DEPTH)
     def _(j):
         send(mine_w, mine_w, c1_s, c1_r, deep((z + j) % DEPTH))
 
-    seven = W.at[0, 0, pl.ds(0, 16 * (DEPTH - 1)), pl.ds(0, 128)]
+    seven = W1.at[0, pl.ds(0, DEPTH - 1)]
     later(seven, c1_s)
     wpair[1:, part, :] = wu[c, 1]
     s_v.wait_recv()
     for u in range(REPL):
-        W[1, u // 2, my16, lane_tile(u % 2)] = wpair[1 + u].astype(BF16)
+        W1[p, u] = wpair[1 + u].astype(BF16)
     across = (p + DEPTH) % CHIPS
-    rows_a = W.at[1, :, my16]
-    rows_b = W.at[1, :, pl.ds(pl.multiple_of(16 * across, 16), 16)]
+    rows_a, rows_b = W1.at[p], W1.at[across]
     send(rows_a, rows_a, za_s.at[0], za_r.at[0], chip(across))
     later(rows_a, za_s.at[0])
 
     def at_depth(side, by):
-        q = (p - z if side == 0 else across - z) + (z + by + DEPTH) % DEPTH
-        return pl.ds(pl.multiple_of(16 * q, 16), 16)
+        return (p - z if side == 0 else across - z) + (z + by + DEPTH) % DEPTH
 
     def near(side):
-        rows = W.at[1, :, at_depth(side, 0)]
+        rows = W1.at[at_depth(side, 0)]
         for by in (1, -1):
             send(rows, rows, za_s.at[1], za_r.at[1], deep((z + by + DEPTH) % DEPTH))
         for by in (2, -2):
@@ -198,10 +189,10 @@
 
     def onward(side):
         for way, by in ((0, 1), (1, -1)):
-            rows = W.at[1, :, at_depth(side, -2 * by)]
+            rows = W1.at[at_depth(side, -2 * by)]
             wait_for(rows, za_r.at[2 + 2 * side + way])
             send(rows, rows, za_s.at[1], za_r.at[1], deep((z + by + DEPTH) % DEPTH))
-            half = W.at[1, pl.ds(2 * way, 2), at_depth(side, -2 * by)]
+            half = W1.at[at_depth(side, -2 * by), pl.ds(4 * way, 4)]
             send(half, half, za_s.at[1], za_r.at[1], deep((z + 2 * by + DEPTH) % DEPTH))
 
     near(0)
@@ -221,11 +212,11 @@
     wait_for(rows_b, za_r.at[0])
 
     near(1)
-    later(W.at[1, :, pl.ds(0, 16 * 14)], za_s.at[1])
-    ten = W.at[1, :, pl.ds(0, 16 * 10)]
+    later(W1.at[pl.ds(0, 14)], za_s.at[1])
+    ten = W1.at[pl.ds(0, 10)]
     wait_for(seven, c1_r)
     fifteen = frecv.at[0, pl.ds(0, PLANE - 1)]
-    mine_s = W.at[0, d // 2, rows_of(y // 2), lanes_of(d)]
+    mine_s = W0.at[d, y // 2]
 
     @pl.loop(1, PLANE)
     def _(j):
@@ -278,10 +269,15 @@
     gate_b = gb_ref[...]
     ends = []
 
+    def weights(b, g):
+        u = 4 * (b % 2) + 2 * g
+        two = (W0[u + lh] if b < 2 else W1[:, u + lh] for lh in range(2))
+        return jnp.concatenate([v.reshape(BW, 128) for v in two], 1)
+
     def gates(b):
-        st, k = b // 2, 2 * (b % 2)
+        st = b // 2
         for g in range(2):
-            pre[2 * b + g] = jnp.dot(mb[:, block(b)], W[st, k + g], preferred_element_type=F32)
+            pre[2 * b + g] = jnp.dot(mb[:, block(b)], weights(b, g), preferred_element_type=F32)
         nr = jnp.broadcast_to(neg8rate[:, block(b)], (8, BW))
         ba = jnp.broadcast_to(gate_b[0:1, block(b)], (8, BW))
         bx = jnp.broadcast_to(gate_b[1:2, block(b)], (8, BW))
@@ -399,14 +395,18 @@
         sums.append([t_sum, a_sum, x_sum])
         for g in range(2):
             grad = jnp.dot(mt[b], gp[2 * b + g], preferred_element_type=F32).astype(BF16)
-            for h in range(2):
-                wsend[st, k + g, h] = grad[128 * h : 128 * (h + 1)]
+            for lh in range(2):
+                for h in range(2):
+                    if b == 1:
+                        for j in range(DEPTH):
+                            wz[j, h, 2 * g + lh] = grad[128 * h + 16 * j : 128 * h + 16 * j + 16, lane_tile(lh)]
+                    else:
+                        wsend[st, 2 * (k + g) + lh, h] = grad[128 * h : 128 * (h + 1), lane_tile(lh)]
 
     def through(b):
-        st, k = b // 2, 2 * (b % 2)
         nt = (((1,), (1,)), ((), ()))
-        back = lax.dot_general(gp[2 * b], W[st, k], nt, preferred_element_type=F32)
-        back = back + lax.dot_general(gp[2 * b + 1], W[st, k + 1], nt, preferred_element_type=F32)
+        back = lax.dot_general(gp[2 * b], weights(b, 0), nt, preferred_element_type=F32)
+        back = back + lax.dot_general(gp[2 * b + 1], weights(b, 1), nt, preferred_element_type=F32)
         gm[0:R, :, block(b)] = gm[0:R, :, block(b)] + back.reshape(R, 8, BW)
 
     for st in range(STAGES):
@@ -429,7 +429,7 @@
 
             def go():
                 send(
-                    wsend.at[st, to_d // 2, to_h, :, lanes_of(to_d)],
+                    wsend.at[st, to_d, to_h],
                     frecv.at[st, spot], f_s.at[st], f_r.at[st], dev,
                 )
 
@@ -441,18 +441,18 @@
         if st == 0:
             @pl.when(y % 2 == 0)
             def _():
-                frecv[st, spot] = wsend[st, d // 2, y // 2, :, lanes_of(d)]
+                frecv[st, spot] = wsend[st, d, y // 2]
 
             @pl.loop(1, DEPTH)
             def _(j):
                 to = (z + j) % DEPTH
-                send(wsend.at[0, pl.ds(2, 2), :, rows16(to)], brecv.at[z], b_s.at[0], b_r.at[0], deep(to))
+                send(wz.at[to], brecv.at[z], b_s.at[0], b_r.at[0], deep(to))
 
             later(brecv.at[pl.ds(0, DEPTH - 1)], b_s.at[0])
-            brecv[z] = wsend[0, 2:4, :, rows16(z)]
+            brecv[z] = wz[z]
         else:
             later(fifteen, f_s.at[st])
-            frecv[st, spot] = wsend[st, d // 2, y // 2, :, lanes_of(d)]
+            frecv[st, spot] = wsend[st, d, y // 2]
         for b in (2 * st, 2 * st + 1):
             through(b)
 
@@ -506,6 +506,37 @@
 
         zrecv[st, z] = fsum[st, z]
 
+    pl.when(y % 2 == 0)(lambda: fold(0))
+    wait_for(brecv.at[pl.ds(0, DEPTH - 1)], b_r.at[0])
+    for h in range(2):
+        for t in range(4):
+            v = brecv[0, h, t].astype(F32)
+            for j in range(1, DEPTH):
+                v = v + brecv[j, h, t].astype(F32)
+            bsum[h, t] = v.astype(BF16)
+
+    @pl.loop(1, PLANE)
+    def _(j):
+        dev, to_h, to_d = plane(j)
+
+        @pl.when(to_d >= 4)
+        def _():
+            send(bsum.at[to_h, to_d % 4], bz.at[spot], b_s.at[1], b_r.at[1], dev)
+
+    @pl.when(y % 2 == 1)
+    def _():
+        bz[spot] = bsum[y // 2, x]
+
+    wait_for(srecv.at[pl.ds(0, DEPTH - 1)], fs_r.at[0])
+    ssum[...] = jnp.sum(srecv[...], 0)
+
+    @pl.loop(1, PLANE)
+    def _(j):
+        send(ssum, szrecv.at[spot], fs_s.at[1], fs_r.at[1], plane(j)[0])
+
+    later(szrecv.at[pl.ds(0, PLANE - 1)], fs_s.at[1])
+    szrecv[spot] = ssum[...]
+
     wait_for(ghr, e_r)
     halo = ghr[...]
     halo = jnp.where(p == CHIPS - 1, jnp.zeros_like(halo), halo)
@@ -530,48 +561,6 @@
     st_g = pltpu.make_async_copy(gib.at[my_rows], gi_hbm.at[:, mine], lsem.at[3])
     st_g.start()
     later(gib.at[my_rows], lsem.at[3])
-
-    wait_for(srecv.at[pl.ds(0, DEPTH - 1)], fs_r.at[0])
-    ssum[...] = jnp.sum(srecv[...], 0)
-
-    @pl.loop(1, PLANE)
-    def _(j):
-        send(ssum, szrecv.at[spot], fs_s.at[1], fs_r.at[1], plane(j)[0])
-
-    later(szrecv.at[pl.ds(0, PLANE - 1)], fs_s.at[1])
-    szrecv[spot] = ssum[...]
-
-    pl.when(y % 2 == 0)(lambda: fold(0))
-    wait_for(brecv.at[pl.ds(0, DEPTH - 1)], b_r.at[0])
-    for k in range(2):
-        for h in range(2):
-            v = brecv[0, k, h].astype(F32)
-            for j in range(1, DEPTH):
-                v = v + brecv[j, k, h].astype(F32)
-            for lh in range(2):
-                bsum[h, 2 * k + lh] = v[:, lane_tile(lh)].astype(BF16)
-
-    @pl.loop(1, PLANE)
-    def _(j):
-        dev, to_h, to_d = plane(j)
-
-        @pl.when(to_d >= 4)
-        def _():
-            send(bsum.at[to_h, to_d % 4], bz.at[spot], b_s.at[1], b_r.at[1], dev)
-
-    @pl.when(y % 2 == 1)
-    def _():
-        bz[spot] = bsum[y // 2, x]
-
-    wait_for(szrecv.at[pl.ds(0, PLANE - 1)], fs_r.at[1])
-    fin[...] = jnp.sum(szrecv[...], 0)
-
-    @pl.loop(1, DEPTH)
-    def _(j):
-        send(fin, tiles.at[c, z], fs_s.at[2], fs_r.at[2], deep((z + j) % DEPTH))
-
-    later(tiles.at[0, pl.ds(0, DEPTH - 1)], fs_s.at[2])
-    tiles[c, z] = fin[...]
     fold(1)
     later(zrecv.at[1, pl.ds(0, DEPTH - 1)], z_s.at[1])
 
@@ -614,11 +603,20 @@
     pl.when(y % 2 == 0)(lambda: total(0, lambda j: zrecv[0, j], DEPTH))
     pl.when(y % 2 == 1)(lambda: total(0, lambda j: bz[j], PLANE))
     finish(0)
-    wait_for(tiles.at[0, pl.ds(0, DEPTH - 1)], fs_r.at[2])
-    s_t = send(tiles.at[c], tiles.at[c], sib_s.at[4], sib_r.at[4], sibling)
+    wait_for(szrecv.at[pl.ds(0, PLANE - 1)], fs_r.at[1])
+    fin[...] = jnp.sum(szrecv[...], 0)
+
+    @pl.loop(1, DEPTH)
+    def _(j):
+        send(fin, tiles.at[c, z], fs_s.at[2], fs_r.at[2], deep((z + j) % DEPTH))
+
+    later(tiles.at[0, pl.ds(0, DEPTH - 1)], fs_s.at[2])
+    tiles[c, z] = fin[...]
     wait_for(zrecv.at[1, pl.ds(0, DEPTH - 1)], z_r.at[1])
     total(1, lambda j: zrecv[1, j], DEPTH)
     finish(1)
+    wait_for(tiles.at[0, pl.ds(0, DEPTH - 1)], fs_r.at[2])
+    s_t = send(tiles.at[c], tiles.at[c], sib_s.at[4], sib_r.at[4], sibling)
     s_t.wait_recv()
     st_t = pltpu.make_async_copy(tiles, small_hbm, lsem.at[9])
     st_t.start()
@@ -703,7 +701,8 @@
             pltpu.VMEM((2, 128, 128), F32),
             pltpu.VMEM((2, STAGES, REPL, 8, 128), F32),
             pltpu.VMEM((1 + REPL, 16, 128), F32),
-            pltpu.VMEM((STAGES, 4, BW, BW), BF16),
+            pltpu.VMEM((REPL, 2, 128, 128), BF16),
+            pltpu.VMEM((CHIPS, REPL, 16, 128), BF16),
             pltpu.VMEM((16, HALF), BF16),
             pltpu.VMEM((TILES, SPAN, 128), F32),
             pltpu.VMEM((TILES, SPAN, 128), F32),
@@ -720,9 +719,10 @@
             pltpu.VMEM((STAGES, 2, 4, 128), F32),
             pltpu.VMEM((8, HALF), F32),
             pltpu.VMEM((8, HALF), F32),
-            pltpu.VMEM((STAGES, 4, 2, 128, BW), BF16),
+            pltpu.VMEM((STAGES, REPL, 2, 128, 128), BF16),
+            pltpu.VMEM((DEPTH, 2, 4, 16, 128), BF16),
             pltpu.VMEM((STAGES, PLANE, 128, 128), BF16),
-            pltpu.VMEM((DEPTH, 2, 2, 16, BW), BF16),
+            pltpu.VMEM((DEPTH, 2, 4, 16, 128), BF16),
             pltpu.VMEM((2, 4, 16, 128), BF16),
             pltpu.VMEM((PLANE, 16, 128), BF16),
             pltpu.VMEM((STAGES, 16, 128), F32),

time: 65.3 us -> 63.1 us (0.966)
  Pallas kernels: 64.5 us -> 62.3 us
    pallas_call x1, Pallas kernels: 62.5 us -> 60.3 us  [per_device(): pl.pallas_call(main_kernel, name='main', out_shape=(jax.ShapeDtypeStruct(...]
where the time goes in v6:
time: 63.1 us; the launch traced here: 63 us
  Pallas kernels  62.3 us (99%)
  between operations  0.64 us (1%)
    pallas_call x1, Pallas kernels, per_device(): pl.pallas_call(main_kernel, name='main', out_shape=(jax.ShapeDtypeStruct(...  60.3 us
    pallas_call x1, Pallas kernels, per_device(): pl.pallas_call(last_kernel, name='last', out_shape=(jax.ShapeDtypeStruct(...  2.03 us

profile of v6, /device:TPU:1, one launch (start us, length us, event | category | flops | bytes accessed | tf_op | source)
XLA Modules:
  0.0 63.0 jit_solution(14954933255163590001)
XLA Ops:
  0.6 60.3 %main.1 = (bf16[128,2048]{1,0:T(8,128)(2,1)}, f32[8,2,8,256]{3,2,1,0:T(8,128)}, f32[2,8,8,128]{3,2,1,0:T(8,128)}) custom-call(bf16[1,128,2048]{2,1,0:T(8,128)(2,1)} %x_hbm.1, bf16[8,2,8,256]{3,2,1,0:T(8,128)(2,1)} %w_hbm.1, f32[2,2048]{1,0:T(2,128)} %gb_hbm.1, f32[1,2048]{1,0:T(1,128)} %bitcast.4, f32[4,2048]{1,0:T(4,128)} %cw_hbm.1, f32[1,2048]{1,0:T(1,128)} %bitcast.5, ...), custom_call_target="tpu_custom_call" | custom-call | tf_op jit(solution)/shard_map/main/pallas_call | solution.py:683
  61.0 2.0 %last.1 = (bf16[1,128,2048]{2,1,0:T(8,128)(2,1)}, f32[8,2,8,256]{3,2,1,0:T(8,128)}, f32[1,2048]{1,0:T(1,128)}, f32[2,2048]{1,0:T(2,128)}, f32[4,2048]{1,0:T(4,128)}, /*index=5*/f32[1,2048]{1,0:T(1,128)}) custom-call(bf16[128,2048]{1,0:T(8,128)(2,1)} %get-tuple-element.15.gi_in, f32[8,2,8,256]{3,2,1,0:T(8,128)} %get-tuple-element.16.all_in, ...), custom_call_target="tpu_custom_call" | custom-call | tf_op jit(solution)/shard_map/last/pallas_call | solution.py:752

commit v7 on v6

--- a/solution.py
+++ b/solution.py
@@ -58,17 +58,18 @@
     gi_hbm, all_hbm, small_hbm,
     gb_ref, lam_ref, cw_ref, cb_ref, xb, cotb, wsh, wf, wu, wpair, W0, W1, xhalo, nat, natc, xs, cs, mb, mt, pre,
     dec, drv, qq, m1, m2, m3, oma, hp, gp, gm, dsend, drecv, sin, ghs, ghr,
-    wsend, wz, frecv, brecv, bsum, bz, own, fsum, zrecv, ssend, srecv, ssum, szrecv, fin, tiles, G, gib,
+    wsend, wz, frecv, brecv, bsum, bz, own, fsum, zrecv, ssend, srecv, ssum, szrecv, fin, tiles, gib,
     lsem, sib_s, sib_r, c1_s, c1_r, hal_s, hal_r, za_s, za_r, c2_s, c2_r, d_s, d_r, e_s, e_r,
     f_s, f_r, b_s, b_r, fs_s, fs_r, z_s, z_r, g_s, g_r,
 ):
     ctx = lax.axis_index("ctx")
     d = lax.axis_index("dp")
-    p = ctx // 2
-    c = ctx % 2
-    z = p % DEPTH
-    y = 2 * (p // DEPTH) + d // 4
-    x = d % 4
+    div, rem = lax.div, lax.rem
+    p, c = div(ctx, 2), rem(ctx, 2)
+    z = rem(p, DEPTH)
+    y = 2 * div(p, DEPTH) + div(d, 4)
+    x = rem(d, 4)
+    y_hi, y_odd = div(y, 2), rem(y, 2)
     spot = 4 * y + x
     sibling = {"ctx": 2 * p + 1 - c, "dp": d}
 
@@ -82,9 +83,9 @@
         return {"ctx": ctx, "dp": u}
 
     def plane(j):
-        to_x, to_y = (x + j % 4) % 4, (y + j // 4) % 4
-        to_d = 4 * (to_y % 2) + to_x
-        return {"ctx": 2 * (DEPTH * (to_y // 2) + z) + c, "dp": to_d}, to_y // 2, to_d
+        to_x, to_y = rem(x + rem(j, 4), 4), rem(y + div(j, 4), 4)
+        to_h, to_d = div(to_y, 2), 4 * rem(to_y, 2) + to_x
+        return {"ctx": 2 * (DEPTH * to_h + z) + c, "dp": to_d}, to_h, to_d
 
     def rows16(j):
         return pl.ds(pl.multiple_of(16 * j, 16), 16)
@@ -101,7 +102,7 @@
 
     @pl.loop(1, CHIPS)
     def _(j):
-        pl.semaphore_signal(bar, inc=1, device_id=chip((p + j) % CHIPS), device_id_type=MESH)
+        pl.semaphore_signal(bar, inc=1, device_id=chip(rem(p + j, CHIPS)), device_id_type=MESH)
 
     @pl.loop(1, PLANE)
     def _(j):
@@ -111,7 +112,7 @@
 
     @pl.loop(1, REPL)
     def _(j):
-        dev = {"ctx": 2 * p + 1 - c, "dp": (d + j) % REPL}
+        dev = {"ctx": 2 * p + 1 - c, "dp": rem(d + j, REPL)}
         pl.semaphore_signal(bar, inc=1, device_id=dev, device_id_type=MESH)
 
     mine = pl.ds(pl.multiple_of(HALF * c, HALF), HALF)
@@ -154,52 +155,52 @@
     part = pl.ds(pl.multiple_of(8 * c, 8), 8)
     s_w = send(wu.at[1 - c, 0, d], wpair.at[0, part], sib_s.at[0], sib_r.at[0], sibling)
     s_v = send(wu.at[1 - c, 1], wpair.at[pl.ds(1, REPL), part], sib_s.at[5], sib_r.at[5], sibling)
+    wpair[0, part, :] = wu[c, 0, d]
+    s_w.wait_recv()
+    mine_w = W0.at[d, y_hi, rows16(z)]
+    mine_w[...] = wpair[0].astype(BF16)
+
+    @pl.loop(1, DEPTH)
+    def _(j):
+        send(mine_w, mine_w, c1_s, c1_r, deep(rem(z + j, DEPTH)))
+
     s_x = send(x_hbm.at[0, :, theirs], xb.at[my_rows], sib_s.at[1], sib_r.at[1], sibling)
     s_c = send(cot_hbm.at[0, :, theirs], cotb.at[my_rows], sib_s.at[2], sib_r.at[2], sibling)
-    wpair[0, part, :] = wu[c, 0, d]
-    s_w.wait_recv()
-    mine_w = W0.at[d, y // 2, rows16(z)]
-    mine_w[...] = wpair[0].astype(BF16)
-
-    @pl.loop(1, DEPTH)
-    def _(j):
-        send(mine_w, mine_w, c1_s, c1_r, deep((z + j) % DEPTH))
-
     seven = W1.at[0, pl.ds(0, DEPTH - 1)]
     later(seven, c1_s)
     wpair[1:, part, :] = wu[c, 1]
     s_v.wait_recv()
     for u in range(REPL):
         W1[p, u] = wpair[1 + u].astype(BF16)
-    across = (p + DEPTH) % CHIPS
+    across = rem(p + DEPTH, CHIPS)
     rows_a, rows_b = W1.at[p], W1.at[across]
     send(rows_a, rows_a, za_s.at[0], za_r.at[0], chip(across))
     later(rows_a, za_s.at[0])
 
     def at_depth(side, by):
-        return (p - z if side == 0 else across - z) + (z + by + DEPTH) % DEPTH
+        return (p - z if side == 0 else across - z) + rem(z + by + DEPTH, DEPTH)
 
     def near(side):
         rows = W1.at[at_depth(side, 0)]
         for by in (1, -1):
-            send(rows, rows, za_s.at[1], za_r.at[1], deep((z + by + DEPTH) % DEPTH))
+            send(rows, rows, za_s.at[1], za_r.at[1], deep(rem(z + by + DEPTH, DEPTH)))
         for by in (2, -2):
             arrive = za_r.at[2 + 2 * side + (0 if by > 0 else 1)]
-            send(rows, rows, za_s.at[1], arrive, deep((z + by + DEPTH) % DEPTH))
+            send(rows, rows, za_s.at[1], arrive, deep(rem(z + by + DEPTH, DEPTH)))
 
     def onward(side):
         for way, by in ((0, 1), (1, -1)):
             rows = W1.at[at_depth(side, -2 * by)]
             wait_for(rows, za_r.at[2 + 2 * side + way])
-            send(rows, rows, za_s.at[1], za_r.at[1], deep((z + by + DEPTH) % DEPTH))
+            send(rows, rows, za_s.at[1], za_r.at[1], deep(rem(z + by + DEPTH, DEPTH)))
             half = W1.at[at_depth(side, -2 * by), pl.ds(4 * way, 4)]
-            send(half, half, za_s.at[1], za_r.at[1], deep((z + 2 * by + DEPTH) % DEPTH))
+            send(half, half, za_s.at[1], za_r.at[1], deep(rem(z + 2 * by + DEPTH, DEPTH)))
 
     near(0)
 
     ld_x.wait()
     s_x.wait_recv()
-    send(xb.at[pl.ds(SPAN - 16, 16)], xhalo, hal_s, hal_r, chip((p + 1) % CHIPS))
+    send(xb.at[pl.ds(SPAN - 16, 16)], xhalo, hal_s, hal_r, chip(rem(p + 1, CHIPS)))
     later(xhalo, hal_s)
     for k in range(TILES):
         nat[k] = xb[:, lane_tile(k)].astype(F32)
@@ -216,7 +217,7 @@
     ten = W1.at[pl.ds(0, 10)]
     wait_for(seven, c1_r)
     fifteen = frecv.at[0, pl.ds(0, PLANE - 1)]
-    mine_s = W0.at[d, y // 2]
+    mine_s = W0.at[d, y_hi]
 
     @pl.loop(1, PLANE)
     def _(j):
@@ -312,7 +313,7 @@
 
         zero = jnp.zeros((8, BW), F32)
         prod, hid, kk, logs = lax.fori_loop(
-            0, R // 2, step, (jnp.ones((8, BW), F32), zero, zero, zero)
+            0, R // 2, step, (jnp.ones((8, BW), F32), zero, zero, zero), unroll=2
         )
         sb = sublane((8, BW))
         fp, fh = prod, hid
@@ -346,7 +347,7 @@
 
         @pl.loop(1, CHIPS)
         def _(j):
-            to = (p + j) % CHIPS
+            to = rem(p + j, CHIPS)
             send(dsend.at[st, jnp.where(to > p, 0, 1)], drecv.at[st, p], d_s.at[st], d_r.at[st], chip(to))
 
         later(drecv.at[st, pl.ds(0, CHIPS - 1)], d_s.at[st])
@@ -391,7 +392,7 @@
             return kk, t_sum, a_sum, x_sum
 
         zero = jnp.zeros((8, BW), F32)
-        _, t_sum, a_sum, x_sum = lax.fori_loop(0, R // 2, down, (kin, zero, zero, zero))
+        _, t_sum, a_sum, x_sum = lax.fori_loop(0, R // 2, down, (kin, zero, zero, zero), unroll=4)
         sums.append([t_sum, a_sum, x_sum])
         for g in range(2):
             grad = jnp.dot(mt[b], gp[2 * b + g], preferred_element_type=F32).astype(BF16)
@@ -439,26 +440,26 @@
                 go()
 
         if st == 0:
-            @pl.when(y % 2 == 0)
+            @pl.when(y_odd == 0)
             def _():
-                frecv[st, spot] = wsend[st, d, y // 2]
+                frecv[st, spot] = wsend[st, d, y_hi]
 
             @pl.loop(1, DEPTH)
             def _(j):
-                to = (z + j) % DEPTH
+                to = rem(z + j, DEPTH)
                 send(wz.at[to], brecv.at[z], b_s.at[0], b_r.at[0], deep(to))
 
             later(brecv.at[pl.ds(0, DEPTH - 1)], b_s.at[0])
             brecv[z] = wz[z]
         else:
             later(fifteen, f_s.at[st])
-            frecv[st, spot] = wsend[st, d, y // 2]
+            frecv[st, spot] = wsend[st, d, y_hi]
         for b in (2 * st, 2 * st + 1):
             through(b)
 
     for k in range(3):
         ghs[k : k + 1, :] = gm[k, 0:1, :]
-    send(ghs, ghr, e_s, e_r, chip((p + CHIPS - 1) % CHIPS))
+    send(ghs, ghr, e_s, e_r, chip(rem(p + CHIPS - 1, CHIPS)))
     later(ghr, e_s)
 
     sig = 1.0 / (1.0 + jnp.exp(lam))
@@ -482,7 +483,7 @@
 
     @pl.loop(1, DEPTH)
     def _(j):
-        to = (z + j) % DEPTH
+        to = rem(z + j, DEPTH)
         send(ssend.at[to], srecv.at[z], fs_s.at[0], fs_r.at[0], deep(to))
 
     later(srecv.at[pl.ds(0, DEPTH - 1)], fs_s.at[0])
@@ -501,12 +502,36 @@
 
         @pl.loop(1, DEPTH)
         def _(j):
-            to = (z + j) % DEPTH
+            to = rem(z + j, DEPTH)
             send(fsum.at[st, to], zrecv.at[st, z], z_s.at[st], z_r.at[st], deep(to))
 
         zrecv[st, z] = fsum[st, z]
 
-    pl.when(y % 2 == 0)(lambda: fold(0))
+    pl.when(y_odd == 0)(lambda: fold(0))
+    wait_for(ghr, e_r)
+    halo = ghr[...]
+    halo = jnp.where(p == CHIPS - 1, jnp.zeros_like(halo), halo)
+    for k in range(3):
+        rolled = pltpu.roll(gm[k], 7, 0)
+        gm[R + k] = jnp.where(sub == 7, jnp.broadcast_to(halo[k : k + 1], (8, HALF)), rolled)
+
+    for b in range(NB):
+        taps = [jnp.broadcast_to(conv_w[k : k + 1, block(b)], (8, BW)) for k in range(4)]
+
+        @pl.loop(0, R)
+        def _(r):
+            v = taps[0] * gm[r + 3, :, block(b)]
+            for k in range(1, 4):
+                v = v + taps[k] * gm[r + 3 - k, :, block(b)]
+            for lh in range(2):
+                nat[2 * b + lh, pl.ds(r, 8, stride=R), :] = v[:, lane_tile(lh)]
+
+    for k in range(TILES):
+        gib[:, lane_tile(k)] = nat[k].astype(BF16)
+    s_g = send(gib.at[sib_rows], gi_hbm.at[:, mine], sib_s.at[3], sib_r.at[3], sibling)
+    st_g = pltpu.make_async_copy(gib.at[my_rows], gi_hbm.at[:, mine], lsem.at[3])
+    st_g.start()
+    later(gib.at[my_rows], lsem.at[3])
     wait_for(brecv.at[pl.ds(0, DEPTH - 1)], b_r.at[0])
     for h in range(2):
         for t in range(4):
@@ -521,11 +546,11 @@
 
         @pl.when(to_d >= 4)
         def _():
-            send(bsum.at[to_h, to_d % 4], bz.at[spot], b_s.at[1], b_r.at[1], dev)
-
-    @pl.when(y % 2 == 1)
+            send(bsum.at[to_h, rem(to_d, 4)], bz.at[spot], b_s.at[1], b_r.at[1], dev)
+
+    @pl.when(y_odd == 1)
     def _():
-        bz[spot] = bsum[y // 2, x]
+        bz[spot] = bsum[y_hi, x]
 
     wait_for(srecv.at[pl.ds(0, DEPTH - 1)], fs_r.at[0])
     ssum[...] = jnp.sum(srecv[...], 0)
@@ -537,41 +562,17 @@
     later(szrecv.at[pl.ds(0, PLANE - 1)], fs_s.at[1])
     szrecv[spot] = ssum[...]
 
-    wait_for(ghr, e_r)
-    halo = ghr[...]
-    halo = jnp.where(p == CHIPS - 1, jnp.zeros_like(halo), halo)
-    for k in range(3):
-        rolled = pltpu.roll(gm[k], 7, 0)
-        gm[R + k] = jnp.where(sub == 7, jnp.broadcast_to(halo[k : k + 1], (8, HALF)), rolled)
-
-    for b in range(NB):
-        taps = [jnp.broadcast_to(conv_w[k : k + 1, block(b)], (8, BW)) for k in range(4)]
-
-        @pl.loop(0, R)
-        def _(r):
-            v = taps[0] * gm[r + 3, :, block(b)]
-            for k in range(1, 4):
-                v = v + taps[k] * gm[r + 3 - k, :, block(b)]
-            for lh in range(2):
-                nat[2 * b + lh, pl.ds(r, 8, stride=R), :] = v[:, lane_tile(lh)]
-
-    for k in range(TILES):
-        gib[:, lane_tile(k)] = nat[k].astype(BF16)
-    s_g = send(gib.at[sib_rows], gi_hbm.at[:, mine], sib_s.at[3], sib_r.at[3], sibling)
-    st_g = pltpu.make_async_copy(gib.at[my_rows], gi_hbm.at[:, mine], lsem.at[3])
-    st_g.start()
-    later(gib.at[my_rows], lsem.at[3])
     fold(1)
     later(zrecv.at[1, pl.ds(0, DEPTH - 1)], z_s.at[1])
 
-    @pl.when(y % 2 == 0)
+    @pl.when(y_odd == 0)
     def _():
         wait_for(zrecv.at[0, pl.ds(0, DEPTH - 1)], z_s.at[0])
         wait_for(zrecv.at[0, pl.ds(0, DEPTH - 1)], z_r.at[0])
         wait_for(frecv.at[0, pl.ds(0, 7)], f_s.at[0])
         wait_for(bz.at[pl.ds(0, 8)], b_s.at[1])
 
-    @pl.when(y % 2 == 1)
+    @pl.when(y_odd == 1)
     def _():
         wait_for(bz.at[pl.ds(0, PLANE - 1)], b_r.at[1])
         wait_for(frecv.at[0, pl.ds(0, 8)], f_s.at[0])
@@ -580,14 +581,18 @@
 
     srecv15 = szrecv.at[pl.ds(0, 2 * REPL - 1)]
 
+    kept = []
+
     def spread(n, tile):
-        G[d, c, :, lane_tile(n)] = tile(c)[...]
+        keep = pltpu.make_async_copy(tile(c), all_hbm.at[d, c, :, lane_tile(n)], lsem.at[9 + n])
+        keep.start()
+        kept.append(keep)
 
         @pl.loop(1, 2 * REPL)
         def _(j):
-            to_c = (c + j // REPL) % 2
-            dev = {"ctx": 2 * p + to_c, "dp": (d + j) % REPL}
-            send(tile(to_c), G.at[d, c, :, lane_tile(n)], g_s.at[n], g_r.at[n], dev)
+            to_c = rem(c + div(j, REPL), 2)
+            dev = {"ctx": 2 * p + to_c, "dp": rem(d + j, REPL)}
+            send(tile(to_c), all_hbm.at[d, c, :, lane_tile(n)], g_s.at[n], g_r.at[n], dev)
 
         later(srecv15, g_s.at[n])
 
@@ -600,15 +605,15 @@
     def finish(st):
         spread(st, lambda core: own.at[st, pl.ds(pl.multiple_of(8 * core, 8), 8)])
 
-    pl.when(y % 2 == 0)(lambda: total(0, lambda j: zrecv[0, j], DEPTH))
-    pl.when(y % 2 == 1)(lambda: total(0, lambda j: bz[j], PLANE))
+    pl.when(y_odd == 0)(lambda: total(0, lambda j: zrecv[0, j], DEPTH))
+    pl.when(y_odd == 1)(lambda: total(0, lambda j: bz[j], PLANE))
     finish(0)
     wait_for(szrecv.at[pl.ds(0, PLANE - 1)], fs_r.at[1])
     fin[...] = jnp.sum(szrecv[...], 0)
 
     @pl.loop(1, DEPTH)
     def _(j):
-        send(fin, tiles.at[c, z], fs_s.at[2], fs_r.at[2], deep((z + j) % DEPTH))
+        send(fin, tiles.at[c, z], fs_s.at[2], fs_r.at[2], deep(rem(z + j, DEPTH)))
 
     later(tiles.at[0, pl.ds(0, DEPTH - 1)], fs_s.at[2])
     tiles[c, z] = fin[...]
@@ -616,22 +621,20 @@
     total(1, lambda j: zrecv[1, j], DEPTH)
     finish(1)
     wait_for(tiles.at[0, pl.ds(0, DEPTH - 1)], fs_r.at[2])
-    s_t = send(tiles.at[c], tiles.at[c], sib_s.at[4], sib_r.at[4], sibling)
-    s_t.wait_recv()
-    st_t = pltpu.make_async_copy(tiles, small_hbm, lsem.at[9])
-    st_t.start()
+    s_t = send(tiles.at[c], small_hbm.at[c], sib_s.at[4], sib_r.at[4], sibling)
+    kept.append(pltpu.make_async_copy(tiles.at[c], small_hbm.at[c], lsem.at[4]))
+    kept[-1].start()
     for n in range(STAGES):
         wait_for(srecv15, g_r.at[n])
-    st_a = pltpu.make_async_copy(G, all_hbm, lsem.at[4])
-    st_a.start()
+    s_t.wait_recv()
 
     for cp in [s_w, s_v, s_x, s_c, s_g, s_t]:
         cp.wait_send()
     s_g.wait_recv()
     for finish_one in pending:
         finish_one()
-    st_a.wait()
-    st_t.wait()
+    for cp in kept:
+        cp.wait()
 
 
 def last_kernel(
@@ -734,9 +737,8 @@
             pltpu.VMEM((PLANE, 8, 128), F32),
             pltpu.VMEM((8, 128), F32),
             pltpu.VMEM((2, DEPTH, 8, 128), F32),
-            pltpu.VMEM((REPL, 2, 8, BW), F32),
             pltpu.VMEM((SPAN, HALF), BF16),
-            dma((10,)), dma((7,)), dma((7,)),
+            dma((11,)), dma((7,)), dma((7,)),
             dma, dma, dma, dma, dma((2,)), dma((6,)), dma, dma,
             dma((STAGES,)), dma((STAGES,)), dma, dma, dma((STAGES,)), dma((STAGES,)),
             dma((2,)), dma((2,)), dma((3,)), dma((3,)),

time: 63.1 us -> 63.7 us (level)
  Pallas kernels: 62.3 us -> 63 us
where the time goes in v7:
time: 63.7 us; the launch traced here: 63.6 us
  Pallas kernels  63 us (99%)
  between operations  0.64 us (1%)
    pallas_call x1, Pallas kernels, per_device(): pl.pallas_call(main_kernel, name='main', out_shape=(jax.ShapeDtypeStruct(...  60.9 us
    pallas_call x1, Pallas kernels, per_device(): pl.pallas_call(last_kernel, name='last', out_shape=(jax.ShapeDtypeStruct(...  2.03 us

profile of v7, /device:TPU:1, one launch (start us, length us, event | category | flops | bytes accessed | tf_op | source)
XLA Modules:
  0.0 63.6 jit_solution(11441578919384109637)
XLA Ops:
  0.6 60.9 %main.1 = (bf16[128,2048]{1,0:T(8,128)(2,1)}, f32[8,2,8,256]{3,2,1,0:T(8,128)}, f32[2,8,8,128]{3,2,1,0:T(8,128)}) custom-call(bf16[1,128,2048]{2,1,0:T(8,128)(2,1)} %x_hbm.1, bf16[8,2,8,256]{3,2,1,0:T(8,128)(2,1)} %w_hbm.1, f32[2,2048]{1,0:T(2,128)} %gb_hbm.1, f32[1,2048]{1,0:T(1,128)} %bitcast.4, f32[4,2048]{1,0:T(4,128)} %cw_hbm.1, f32[1,2048]{1,0:T(1,128)} %bitcast.5, ...), custom_call_target="tpu_custom_call" | custom-call | tf_op jit(solution)/shard_map/main/pallas_call | solution.py:686
  61.6 2.0 %last.1 = (bf16[1,128,2048]{2,1,0:T(8,128)(2,1)}, f32[8,2,8,256]{3,2,1,0:T(8,128)}, f32[1,2048]{1,0:T(1,128)}, f32[2,2048]{1,0:T(2,128)}, f32[4,2048]{1,0:T(4,128)}, /*index=5*/f32[1,2048]{1,0:T(1,128)}) custom-call(bf16[128,2048]{1,0:T(8,128)(2,1)} %get-tuple-element.15.gi_in, f32[8,2,8,256]{3,2,1,0:T(8,128)} %get-tuple-element.16.all_in, ...), custom_call_target="tpu_custom_call" | custom-call | tf_op jit(solution)/shard_map/last/pallas_call | solution.py:754

commit v8 on v7

--- a/solution.py
+++ b/solution.py
@@ -58,7 +58,7 @@
     gi_hbm, all_hbm, small_hbm,
     gb_ref, lam_ref, cw_ref, cb_ref, xb, cotb, wsh, wf, wu, wpair, W0, W1, xhalo, nat, natc, xs, cs, mb, mt, pre,
     dec, drv, qq, m1, m2, m3, oma, hp, gp, gm, dsend, drecv, sin, ghs, ghr,
-    wsend, wz, frecv, brecv, bsum, bz, own, fsum, zrecv, ssend, srecv, ssum, szrecv, fin, tiles, gib,
+    wsend, wz, frecv, brecv, bsum, bz, own, fsum, zrecv, ssend, srecv, ssum, szrecv, fin, gib,
     lsem, sib_s, sib_r, c1_s, c1_r, hal_s, hal_r, za_s, za_r, c2_s, c2_r, d_s, d_r, e_s, e_r,
     f_s, f_r, b_s, b_r, fs_s, fs_r, z_s, z_r, g_s, g_r,
 ):
@@ -410,60 +410,9 @@
         back = back + lax.dot_general(gp[2 * b + 1], weights(b, 1), nt, preferred_element_type=F32)
         gm[0:R, :, block(b)] = gm[0:R, :, block(b)] + back.reshape(R, 8, BW)
 
-    for st in range(STAGES):
-        wait_for(drecv.at[st, pl.ds(0, CHIPS - 1)], d_r.at[st])
-        state = jnp.zeros((4, 128), F32)
-        carry_in = jnp.zeros((4, 128), F32)
-        for j in range(CHIPS):
-            v = drecv[st, j]
-            state = jnp.where(j < p, jnp.exp(v[:4]) * state + v[4:], state)
-            v = drecv[st, CHIPS - 1 - j]
-            carry_in = jnp.where(CHIPS - 1 - j > p, jnp.exp(v[:4]) * carry_in + v[4:], carry_in)
-        sin[st, 0] = state
-        sin[st, 1] = carry_in
-        for b in (2 * st, 2 * st + 1):
-            grads(b)
-
-        @pl.loop(1, PLANE)
-        def _(j):
-            dev, to_h, to_d = plane(j)
-
-            def go():
-                send(
-                    wsend.at[st, to_d, to_h],
-                    frecv.at[st, spot], f_s.at[st], f_r.at[st], dev,
-                )
-
-            if st == 0:
-                pl.when(to_d < 4)(go)
-            else:
-                go()
-
-        if st == 0:
-            @pl.when(y_odd == 0)
-            def _():
-                frecv[st, spot] = wsend[st, d, y_hi]
-
-            @pl.loop(1, DEPTH)
-            def _(j):
-                to = rem(z + j, DEPTH)
-                send(wz.at[to], brecv.at[z], b_s.at[0], b_r.at[0], deep(to))
-
-            later(brecv.at[pl.ds(0, DEPTH - 1)], b_s.at[0])
-            brecv[z] = wz[z]
-        else:
-            later(fifteen, f_s.at[st])
-            frecv[st, spot] = wsend[st, d, y_hi]
-        for b in (2 * st, 2 * st + 1):
-            through(b)
-
-    for k in range(3):
-        ghs[k : k + 1, :] = gm[k, 0:1, :]
-    send(ghs, ghr, e_s, e_r, chip(rem(p + CHIPS - 1, CHIPS)))
-    later(ghr, e_s)
-
     sig = 1.0 / (1.0 + jnp.exp(lam))
-    for b in range(NB):
+
+    def small_sums(b):
         def add(r, carry):
             g = gm[r, :, block(b)]
             return tuple(carry[k] + g * xs[r + k, :, block(b)] for k in range(4)) + (carry[4] + g,)
@@ -481,13 +430,61 @@
         for lh in range(2):
             ssend[2 * b + lh] = rows[:, lane_tile(lh)]
 
-    @pl.loop(1, DEPTH)
+    for st in range(STAGES):
+        wait_for(drecv.at[st, pl.ds(0, CHIPS - 1)], d_r.at[st])
+        state = jnp.zeros((4, 128), F32)
+        carry_in = jnp.zeros((4, 128), F32)
+        for j in range(CHIPS):
+            v = drecv[st, j]
+            state = jnp.where(j < p, jnp.exp(v[:4]) * state + v[4:], state)
+            v = drecv[st, CHIPS - 1 - j]
+            carry_in = jnp.where(CHIPS - 1 - j > p, jnp.exp(v[:4]) * carry_in + v[4:], carry_in)
+        sin[st, 0] = state
+        sin[st, 1] = carry_in
+        def to_plane(low):
+            @pl.loop(1, PLANE)
+            def _(j):
+                dev, to_h, to_d = plane(j)
+
+                @pl.when(to_d < 4 if low else to_d >= 4)
+                def _():
+                    send(
+                        wsend.at[st, to_d, to_h], frecv.at[st, spot], f_s.at[st], f_r.at[st], dev
+                    )
+
+        grads(2 * st)
+        to_plane(True)
+        grads(2 * st + 1)
+        if st == 0:
+            @pl.when(y_odd == 0)
+            def _():
+                frecv[0, spot] = wsend[0, d, y_hi]
+
+            @pl.loop(1, DEPTH)
+            def _(j):
+                to = rem(z + j, DEPTH)
+                send(wz.at[to], brecv.at[z], b_s.at[0], b_r.at[0], deep(to))
+
+            later(brecv.at[pl.ds(0, DEPTH - 1)], b_s.at[0])
+            brecv[z] = wz[z]
+        for b in (2 * st, 2 * st + 1):
+            through(b)
+            small_sums(b)
+
+    @pl.loop(1, PLANE)
     def _(j):
-        to = rem(z + j, DEPTH)
-        send(ssend.at[to], srecv.at[z], fs_s.at[0], fs_r.at[0], deep(to))
-
-    later(srecv.at[pl.ds(0, DEPTH - 1)], fs_s.at[0])
-    srecv[z] = ssend[z]
+        dev, _, to_d = plane(j)
+        send(ssend.at[to_d], srecv.at[spot], fs_s.at[0], fs_r.at[0], dev)
+
+    later(srecv.at[pl.ds(0, PLANE - 1)], fs_s.at[0])
+    for k in range(3):
+        ghs[k : k + 1, :] = gm[k, 0:1, :]
+    send(ghs, ghr, e_s, e_r, chip(rem(p + CHIPS - 1, CHIPS)))
+    later(ghr, e_s)
+    to_plane(False)
+    later(fifteen, f_s.at[1])
+    frecv[1, spot] = wsend[1, d, y_hi]
+    srecv[spot] = ssend[d]
 
     def fold(st):
         wait_for(fifteen, f_r.at[st])
@@ -552,15 +549,15 @@
     def _():
         bz[spot] = bsum[y_hi, x]
 
-    wait_for(srecv.at[pl.ds(0, DEPTH - 1)], fs_r.at[0])
+    wait_for(srecv.at[pl.ds(0, PLANE - 1)], fs_r.at[0])
     ssum[...] = jnp.sum(srecv[...], 0)
 
-    @pl.loop(1, PLANE)
+    @pl.loop(1, DEPTH)
     def _(j):
-        send(ssum, szrecv.at[spot], fs_s.at[1], fs_r.at[1], plane(j)[0])
-
-    later(szrecv.at[pl.ds(0, PLANE - 1)], fs_s.at[1])
-    szrecv[spot] = ssum[...]
+        send(ssum, szrecv.at[z], fs_s.at[1], fs_r.at[1], deep(rem(z + j, DEPTH)))
+
+    later(szrecv.at[pl.ds(0, DEPTH - 1)], fs_s.at[1])
+    szrecv[z] = ssum[...]
 
     fold(1)
     later(zrecv.at[1, pl.ds(0, DEPTH - 1)], z_s.at[1])
@@ -579,12 +576,11 @@
         wait_for(bz.at[pl.ds(0, 7)], b_s.at[1])
 
 
-    srecv15 = szrecv.at[pl.ds(0, 2 * REPL - 1)]
-
+    srecv15 = srecv.at[pl.ds(0, 2 * REPL - 1)]
     kept = []
 
-    def spread(n, tile):
-        keep = pltpu.make_async_copy(tile(c), all_hbm.at[d, c, :, lane_tile(n)], lsem.at[9 + n])
+    def spread(n, tile, out):
+        keep = pltpu.make_async_copy(tile(c), out, lsem.at[9 + n])
         keep.start()
         kept.append(keep)
 
@@ -592,7 +588,7 @@
         def _(j):
             to_c = rem(c + div(j, REPL), 2)
             dev = {"ctx": 2 * p + to_c, "dp": rem(d + j, REPL)}
-            send(tile(to_c), all_hbm.at[d, c, :, lane_tile(n)], g_s.at[n], g_r.at[n], dev)
+            send(tile(to_c), out, g_s.at[n], g_r.at[n], dev)
 
         later(srecv15, g_s.at[n])
 
@@ -603,32 +599,22 @@
         own[st] = whole
 
     def finish(st):
-        spread(st, lambda core: own.at[st, pl.ds(pl.multiple_of(8 * core, 8), 8)])
+        rows = lambda core: own.at[st, pl.ds(pl.multiple_of(8 * core, 8), 8)]
+        spread(st, rows, all_hbm.at[d, c, :, lane_tile(st)])
 
     pl.when(y_odd == 0)(lambda: total(0, lambda j: zrecv[0, j], DEPTH))
     pl.when(y_odd == 1)(lambda: total(0, lambda j: bz[j], PLANE))
     finish(0)
-    wait_for(szrecv.at[pl.ds(0, PLANE - 1)], fs_r.at[1])
+    wait_for(szrecv.at[pl.ds(0, DEPTH - 1)], fs_r.at[1])
     fin[...] = jnp.sum(szrecv[...], 0)
-
-    @pl.loop(1, DEPTH)
-    def _(j):
-        send(fin, tiles.at[c, z], fs_s.at[2], fs_r.at[2], deep(rem(z + j, DEPTH)))
-
-    later(tiles.at[0, pl.ds(0, DEPTH - 1)], fs_s.at[2])
-    tiles[c, z] = fin[...]
+    spread(STAGES, lambda core: fin, small_hbm.at[c, d])
     wait_for(zrecv.at[1, pl.ds(0, DEPTH - 1)], z_r.at[1])
     total(1, lambda j: zrecv[1, j], DEPTH)
     finish(1)
-    wait_for(tiles.at[0, pl.ds(0, DEPTH - 1)], fs_r.at[2])
-    s_t = send(tiles.at[c], small_hbm.at[c], sib_s.at[4], sib_r.at[4], sibling)
-    kept.append(pltpu.make_async_copy(tiles.at[c], small_hbm.at[c], lsem.at[4]))
-    kept[-1].start()
-    for n in range(STAGES):
+    for n in range(STAGES + 1):
         wait_for(srecv15, g_r.at[n])
-    s_t.wait_recv()
-
-    for cp in [s_w, s_v, s_x, s_c, s_g, s_t]:
+
+    for cp in [s_w, s_v, s_x, s_c, s_g]:
         cp.wait_send()
     s_g.wait_recv()
     for finish_one in pending:
@@ -689,7 +675,7 @@
         out_shape=(
             jax.ShapeDtypeStruct((ROWS, WIDTH), BF16),
             jax.ShapeDtypeStruct((REPL, 2, 8, BW), F32),
-            jax.ShapeDtypeStruct((2, DEPTH, 8, 128), F32),
+            jax.ShapeDtypeStruct((2, REPL, 8, 128), F32),
         ),
         in_specs=[hbm] * 7,
         out_specs=(hbm,) * 3,
@@ -732,17 +718,16 @@
             pltpu.VMEM((STAGES, DEPTH, 16, 128), BF16),
             pltpu.VMEM((STAGES, DEPTH, 16, 128), BF16),
             pltpu.VMEM((8, 8, 128), F32),
+            pltpu.VMEM((PLANE, 8, 128), F32),
+            pltpu.VMEM((8, 128), F32),
             pltpu.VMEM((DEPTH, 8, 128), F32),
             pltpu.VMEM((8, 128), F32),
-            pltpu.VMEM((PLANE, 8, 128), F32),
-            pltpu.VMEM((8, 128), F32),
-            pltpu.VMEM((2, DEPTH, 8, 128), F32),
             pltpu.VMEM((SPAN, HALF), BF16),
-            dma((11,)), dma((7,)), dma((7,)),
+            dma((12,)), dma((7,)), dma((7,)),
             dma, dma, dma, dma, dma((2,)), dma((6,)), dma, dma,
             dma((STAGES,)), dma((STAGES,)), dma, dma, dma((STAGES,)), dma((STAGES,)),
-            dma((2,)), dma((2,)), dma((3,)), dma((3,)),
-            dma((STAGES,)), dma((STAGES,)), dma((STAGES,)), dma((STAGES,)),
+            dma((2,)), dma((2,)), dma((2,)), dma((2,)),
+            dma((STAGES,)), dma((STAGES,)), dma((STAGES + 1,)), dma((STAGES + 1,)),
         ],
         compiler_params=pltpu.CompilerParams(
             collective_id=0, has_side_effects=True, vmem_limit_bytes=60 * 2**20
@@ -766,7 +751,7 @@
         out_specs=(hbm,) * 6,
         scratch_shapes=[
             pltpu.VMEM((REPL, 2, 8, BW), F32),
-            pltpu.VMEM((2, DEPTH, 8, 128), F32),
+            pltpu.VMEM((2, REPL, 8, 128), F32),
             pltpu.VMEM((2, 128, 128), F32),
             pltpu.VMEM((8, 2, 8, BW), F32),
             pltpu.VMEM((1, WIDTH), F32),

time: 63.7 us -> 60.9 us (0.956)
  Pallas kernels: 63 us -> 60.1 us
    pallas_call x1, Pallas kernels: 60.9 us -> 58.1 us  [per_device(): pl.pallas_call(main_kernel, name='main', out_shape=(jax.ShapeDtypeStruct(...]
where the time goes in v8:
time: 60.9 us; the launch traced here: 60.8 us
  Pallas kernels  60.1 us (99%)
  between operations  0.64 us (1%)
    pallas_call x1, Pallas kernels, per_device(): pl.pallas_call(main_kernel, name='main', out_shape=(jax.ShapeDtypeStruct(...  58.1 us
    pallas_call x1, Pallas kernels, per_device(): pl.pallas_call(last_kernel, name='last', out_shape=(jax.ShapeDtypeStruct(...  2.03 us

profile of v8, /device:TPU:1, one launch (start us, length us, event | category | flops | bytes accessed | tf_op | source)
XLA Modules:
  0.0 60.8 jit_solution(719129724814762468)
XLA Ops:
  0.6 58.1 %main.1 = (bf16[128,2048]{1,0:T(8,128)(2,1)}, f32[8,2,8,256]{3,2,1,0:T(8,128)}, f32[2,8,8,128]{3,2,1,0:T(8,128)}) custom-call(bf16[1,128,2048]{2,1,0:T(8,128)(2,1)} %x_hbm.1, bf16[8,2,8,256]{3,2,1,0:T(8,128)(2,1)} %w_hbm.1, f32[2,2048]{1,0:T(2,128)} %gb_hbm.1, f32[1,2048]{1,0:T(1,128)} %bitcast.4, f32[4,2048]{1,0:T(4,128)} %cw_hbm.1, f32[1,2048]{1,0:T(1,128)} %bitcast.5, ...), custom_call_target="tpu_custom_call" | custom-call | tf_op jit(solution)/shard_map/main/pallas_call | solution.py:672
  58.7 2.0 %last.1 = (bf16[1,128,2048]{2,1,0:T(8,128)(2,1)}, f32[8,2,8,256]{3,2,1,0:T(8,128)}, f32[1,2048]{1,0:T(1,128)}, f32[2,2048]{1,0:T(2,128)}, f32[4,2048]{1,0:T(4,128)}, /*index=5*/f32[1,2048]{1,0:T(1,128)}) custom-call(bf16[128,2048]{1,0:T(8,128)(2,1)} %get-tuple-element.15.gi_in, f32[8,2,8,256]{3,2,1,0:T(8,128)} %get-tuple-element.16.all_in, ...), custom_call_target="tpu_custom_call" | custom-call | tf_op jit(solution)/shard_map/last/pallas_call | solution.py:739

commit v9 on v8

--- a/solution.py
+++ b/solution.py
@@ -55,10 +55,10 @@
 
 def main_kernel(
     x_hbm, w_hbm, gb_hbm, lam_hbm, cw_hbm, cb_hbm, cot_hbm,
-    gi_hbm, all_hbm, small_hbm,
+    gi_hbm, done_hbm,
     gb_ref, lam_ref, cw_ref, cb_ref, xb, cotb, wsh, wf, wu, wpair, W0, W1, xhalo, nat, natc, xs, cs, mb, mt, pre,
-    dec, drv, qq, m1, m2, m3, oma, hp, gp, gm, dsend, drecv, sin, ghs, ghr,
-    wsend, wz, frecv, brecv, bsum, bz, own, fsum, zrecv, ssend, srecv, ssum, szrecv, fin, gib,
+    dec, pp, qq, m1, m2, m3, oma, hp, gp, gm, dsend, drecv, sin, ghs, ghr,
+    wsend, wz, frecv, brecv, bsum, bz, own, fsum, zrecv, ssend, srecv, ssum, szrecv, fin, done, gib,
     lsem, sib_s, sib_r, c1_s, c1_r, hal_s, hal_r, za_s, za_r, c2_s, c2_r, d_s, d_r, e_s, e_r,
     f_s, f_r, b_s, b_r, fs_s, fs_r, z_s, z_r, g_s, g_r,
 ):
@@ -100,17 +100,17 @@
     bar = pltpu.get_barrier_semaphore()
     pl.semaphore_signal(bar, inc=1, device_id=sibling, device_id_type=MESH)
 
-    @pl.loop(1, CHIPS)
+    @pl.loop(1, CHIPS, unroll=True)
     def _(j):
         pl.semaphore_signal(bar, inc=1, device_id=chip(rem(p + j, CHIPS)), device_id_type=MESH)
 
-    @pl.loop(1, PLANE)
+    @pl.loop(1, PLANE, unroll=True)
     def _(j):
         @pl.when(j != PLANE // 2)
         def _():
             pl.semaphore_signal(bar, inc=1, device_id=plane(j)[0], device_id_type=MESH)
 
-    @pl.loop(1, REPL)
+    @pl.loop(1, REPL, unroll=True)
     def _(j):
         dev = {"ctx": 2 * p + 1 - c, "dp": rem(d + j, REPL)}
         pl.semaphore_signal(bar, inc=1, device_id=dev, device_id_type=MESH)
@@ -153,14 +153,14 @@
     pl.semaphore_wait(bar, 1 + (CHIPS - 1) + (PLANE - 2) + (REPL - 1))
 
     part = pl.ds(pl.multiple_of(8 * c, 8), 8)
-    s_w = send(wu.at[1 - c, 0, d], wpair.at[0, part], sib_s.at[0], sib_r.at[0], sibling)
-    s_v = send(wu.at[1 - c, 1], wpair.at[pl.ds(1, REPL), part], sib_s.at[5], sib_r.at[5], sibling)
-    wpair[0, part, :] = wu[c, 0, d]
+    s_w = send(wu.at[1 - c, 1, d], wpair.at[0, part], sib_s.at[0], sib_r.at[0], sibling)
+    s_v = send(wu.at[1 - c, 0], wpair.at[pl.ds(1, REPL), part], sib_s.at[5], sib_r.at[5], sibling)
+    wpair[0, part, :] = wu[c, 1, d]
     s_w.wait_recv()
     mine_w = W0.at[d, y_hi, rows16(z)]
     mine_w[...] = wpair[0].astype(BF16)
 
-    @pl.loop(1, DEPTH)
+    @pl.loop(1, DEPTH, unroll=True)
     def _(j):
         send(mine_w, mine_w, c1_s, c1_r, deep(rem(z + j, DEPTH)))
 
@@ -168,7 +168,7 @@
     s_c = send(cot_hbm.at[0, :, theirs], cotb.at[my_rows], sib_s.at[2], sib_r.at[2], sibling)
     seven = W1.at[0, pl.ds(0, DEPTH - 1)]
     later(seven, c1_s)
-    wpair[1:, part, :] = wu[c, 1]
+    wpair[1:, part, :] = wu[c, 0]
     s_v.wait_recv()
     for u in range(REPL):
         W1[p, u] = wpair[1 + u].astype(BF16)
@@ -219,7 +219,7 @@
     fifteen = frecv.at[0, pl.ds(0, PLANE - 1)]
     mine_s = W0.at[d, y_hi]
 
-    @pl.loop(1, PLANE)
+    @pl.loop(1, PLANE, unroll=True)
     def _(j):
         send(mine_s, mine_s, c2_s, c2_r, plane(j)[0])
 
@@ -272,7 +272,7 @@
 
     def weights(b, g):
         u = 4 * (b % 2) + 2 * g
-        two = (W0[u + lh] if b < 2 else W1[:, u + lh] for lh in range(2))
+        two = (W1[:, u + lh] if b < 2 else W0[u + lh] for lh in range(2))
         return jnp.concatenate([v.reshape(BW, 128) for v in two], 1)
 
     def gates(b):
@@ -299,12 +299,13 @@
                 gm_ = gx * m
                 drive = mult * gm_
                 dec[r, :, block(b)] = a
-                drv[r, :, block(b)] = drive
                 qq[r, :, block(b)] = gm_ * a * lax.rsqrt(jnp.maximum(sq, 0.05))
                 m1[r, :, block(b)] = a * ga
                 oma[r, :, block(b)] = (1.0 - ga) * nr
                 m2[r, :, block(b)] = drive * (1.0 - gx)
                 m3[r, :, block(b)] = mult * gx
+                hp[r, :, block(b)] = hid
+                pp[r, :, block(b)] = prod
                 hid = a * hid + drive
                 prod = prod * a
                 kk = kk + prod * cs[r, :, block(b)]
@@ -341,11 +342,11 @@
             dsend[st, 1, 4 + k : 5 + k, :] = bk[0:1, lane_tile(lh)]
 
     for st in range(STAGES):
-        wait_for(*((fifteen, c2_r) if st == 0 else (ten, za_r.at[1])))
+        wait_for(*((ten, za_r.at[1]) if st == 0 else (fifteen, c2_r)))
         for b in (2 * st, 2 * st + 1):
             gates(b)
 
-        @pl.loop(1, CHIPS)
+        @pl.loop(1, CHIPS, unroll=True)
         def _(j):
             to = rem(p + j, CHIPS)
             send(dsend.at[st, jnp.where(to > p, 0, 1)], drecv.at[st, p], d_s.at[st], d_r.at[st], chip(to))
@@ -365,12 +366,6 @@
 
         hin = ends[b][1] + ends[b][0] * wide(0)
         kin = ends[b][3] + ends[b][2] * wide(1)
-
-        def up(r, h):
-            hp[r, :, block(b)] = h
-            return dec[r, :, block(b)] * h + drv[r, :, block(b)]
-
-        lax.fori_loop(0, R, up, hin, unroll=4)
 
         def down(n, carry):
             kk, t_sum, a_sum, x_sum = carry
@@ -380,7 +375,8 @@
                 r = 2 * i + o
                 gr = cs[r, :, block(b)] + kk
                 kk = dec[r, :, block(b)] * gr
-                t = (hp[r, :, block(b)] - qq[r, :, block(b)]) * m1[r, :, block(b)] * gr
+                before = hp[r, :, block(b)] + pp[r, :, block(b)] * hin
+                t = (before - qq[r, :, block(b)]) * m1[r, :, block(b)] * gr
                 ga = t * oma[r, :, block(b)]
                 gx = gr * m2[r, :, block(b)]
                 gm[r, :, block(b)] = gr * m3[r, :, block(b)]
@@ -442,7 +438,7 @@
         sin[st, 0] = state
         sin[st, 1] = carry_in
         def to_plane(low):
-            @pl.loop(1, PLANE)
+            @pl.loop(1, PLANE, unroll=True)
             def _(j):
                 dev, to_h, to_d = plane(j)
 
@@ -460,18 +456,22 @@
             def _():
                 frecv[0, spot] = wsend[0, d, y_hi]
 
-            @pl.loop(1, DEPTH)
+            @pl.loop(1, DEPTH, unroll=True)
             def _(j):
                 to = rem(z + j, DEPTH)
                 send(wz.at[to], brecv.at[z], b_s.at[0], b_r.at[0], deep(to))
 
             later(brecv.at[pl.ds(0, DEPTH - 1)], b_s.at[0])
             brecv[z] = wz[z]
+        else:
+            to_plane(False)
+            later(fifteen, f_s.at[1])
+            frecv[1, spot] = wsend[1, d, y_hi]
         for b in (2 * st, 2 * st + 1):
             through(b)
             small_sums(b)
 
-    @pl.loop(1, PLANE)
+    @pl.loop(1, PLANE, unroll=True)
     def _(j):
         dev, _, to_d = plane(j)
         send(ssend.at[to_d], srecv.at[spot], fs_s.at[0], fs_r.at[0], dev)
@@ -481,9 +481,6 @@
         ghs[k : k + 1, :] = gm[k, 0:1, :]
     send(ghs, ghr, e_s, e_r, chip(rem(p + CHIPS - 1, CHIPS)))
     later(ghr, e_s)
-    to_plane(False)
-    later(fifteen, f_s.at[1])
-    frecv[1, spot] = wsend[1, d, y_hi]
     srecv[spot] = ssend[d]
 
     def fold(st):
@@ -497,7 +494,7 @@
                 v = v + frecv[st, u, at, :].astype(F32)
             fsum[st, i] = v.astype(BF16)
 
-        @pl.loop(1, DEPTH)
+        @pl.loop(1, DEPTH, unroll=True)
         def _(j):
             to = rem(z + j, DEPTH)
             send(fsum.at[st, to], zrecv.at[st, z], z_s.at[st], z_r.at[st], deep(to))
@@ -537,7 +534,7 @@
                 v = v + brecv[j, h, t].astype(F32)
             bsum[h, t] = v.astype(BF16)
 
-    @pl.loop(1, PLANE)
+    @pl.loop(1, PLANE, unroll=True)
     def _(j):
         dev, to_h, to_d = plane(j)
 
@@ -549,17 +546,17 @@
     def _():
         bz[spot] = bsum[y_hi, x]
 
+    fold(1)
     wait_for(srecv.at[pl.ds(0, PLANE - 1)], fs_r.at[0])
     ssum[...] = jnp.sum(srecv[...], 0)
 
-    @pl.loop(1, DEPTH)
+    @pl.loop(1, DEPTH, unroll=True)
     def _(j):
         send(ssum, szrecv.at[z], fs_s.at[1], fs_r.at[1], deep(rem(z + j, DEPTH)))
 
     later(szrecv.at[pl.ds(0, DEPTH - 1)], fs_s.at[1])
     szrecv[z] = ssum[...]
 
-    fold(1)
     later(zrecv.at[1, pl.ds(0, DEPTH - 1)], z_s.at[1])
 
     @pl.when(y_odd == 0)
@@ -576,79 +573,65 @@
         wait_for(bz.at[pl.ds(0, 7)], b_s.at[1])
 
 
-    srecv15 = srecv.at[pl.ds(0, 2 * REPL - 1)]
-    kept = []
-
-    def spread(n, tile, out):
-        keep = pltpu.make_async_copy(tile(c), out, lsem.at[9 + n])
-        keep.start()
-        kept.append(keep)
-
-        @pl.loop(1, 2 * REPL)
-        def _(j):
-            to_c = rem(c + div(j, REPL), 2)
-            dev = {"ctx": 2 * p + to_c, "dp": rem(d + j, REPL)}
-            send(tile(to_c), out, g_s.at[n], g_r.at[n], dev)
-
-        later(srecv15, g_s.at[n])
-
     def total(st, parts, count):
         whole = parts(0).astype(F32)
         for j in range(1, count):
             whole = whole + parts(j).astype(F32)
         own[st] = whole
 
-    def finish(st):
-        rows = lambda core: own.at[st, pl.ds(pl.multiple_of(8 * core, 8), 8)]
-        spread(st, rows, all_hbm.at[d, c, :, lane_tile(st)])
-
     pl.when(y_odd == 0)(lambda: total(0, lambda j: zrecv[0, j], DEPTH))
     pl.when(y_odd == 1)(lambda: total(0, lambda j: bz[j], PLANE))
-    finish(0)
     wait_for(szrecv.at[pl.ds(0, DEPTH - 1)], fs_r.at[1])
     fin[...] = jnp.sum(szrecv[...], 0)
-    spread(STAGES, lambda core: fin, small_hbm.at[c, d])
     wait_for(zrecv.at[1, pl.ds(0, DEPTH - 1)], z_r.at[1])
     total(1, lambda j: zrecv[1, j], DEPTH)
-    finish(1)
-    for n in range(STAGES + 1):
-        wait_for(srecv15, g_r.at[n])
-
+    for core in range(2):
+        for st in range(STAGES):
+            done[core, st] = own[st, 8 * core : 8 * core + 8, :]
+        done[core, STAGES] = fin[...]
+    keep = pltpu.make_async_copy(done.at[c], done_hbm.at[c, d], lsem.at[9])
+    keep.start()
+
+    @pl.loop(1, 2 * REPL, unroll=True)
+    def _(j):
+        to_c = rem(c + div(j, REPL), 2)
+        dev = {"ctx": 2 * p + to_c, "dp": rem(d + j, REPL)}
+        send(done.at[to_c], done_hbm.at[c, d], g_s, g_r, dev)
+
+    triples = frecv.at[0, pl.ds(0, 2 * REPL - 1), pl.ds(0, 48)]
+    later(triples, g_s)
+    later(triples, g_r)
     for cp in [s_w, s_v, s_x, s_c, s_g]:
         cp.wait_send()
     s_g.wait_recv()
     for finish_one in pending:
         finish_one()
-    for cp in kept:
-        cp.wait()
+    keep.wait()
 
 
 def last_kernel(
-    gi_in, all_in, small_in, gi_out, gw_out, dec_out, bias_out, taps_out, shift_out,
-    all_ref, small_ref, gws, gw, dec, bias, taps, shift, via, l_sem, s_sem,
+    gi_in, done_in, gi_out, gw_out, dec_out, bias_out, taps_out, shift_out,
+    done, gws, gw, dec, bias, taps, shift, via, l_sem, s_sem,
 ):
-    get = pltpu.make_async_copy(all_in, all_ref, l_sem.at[4])
+    get = pltpu.make_async_copy(done_in, done, l_sem.at[4])
     get.start()
-    get_small = pltpu.make_async_copy(small_in, small_ref, l_sem.at[5])
-    get_small.start()
     parts = [pl.ds(k * (ROWS // 4), ROWS // 4) for k in range(4)]
     loads = [pltpu.make_async_copy(gi_in.at[at], via.at[at], l_sem.at[k]) for k, at in enumerate(parts)]
     stores = [pltpu.make_async_copy(via.at[at], gi_out.at[0, at], s_sem.at[k]) for k, at in enumerate(parts)]
     for cp in loads:
         cp.start()
     get.wait()
-    get_small.wait()
     for h in range(2):
         for u in range(8):
             at = slice(h * HALF + 128 * u, h * HALF + 128 * (u + 1))
-            v = small_ref[h, u]
+            v = done[h, u, STAGES]
             dec[:, at] = v[0:1]
             bias[:, at] = v[1:3]
             taps[:, at] = v[3:7]
             shift[:, at] = v[7:8]
             for st in range(STAGES):
                 first = ((u // 2) % 2) * 8 + 4 * h + 2 * st + u // 4
-                gws[u % 2, pl.ds(first, 8, stride=16), :] = all_ref[u, h, :, lane_tile(st)]
+                gws[u % 2, pl.ds(first, 8, stride=16), :] = done[h, u, st]
     for n, (src, dst) in enumerate(((dec, dec_out), (bias, bias_out), (taps, taps_out), (shift, shift_out))):
         stores.append(pltpu.make_async_copy(src, dst, s_sem.at[4 + n]))
         stores[-1].start()
@@ -669,16 +652,15 @@
     hbm = pl.BlockSpec(memory_space=pltpu.HBM)
     dma = pltpu.SemaphoreType.DMA
     big = pltpu.VMEM((R, 8, HALF), F32)
-    gi, packed, small = pl.pallas_call(
+    gi, done = pl.pallas_call(
         main_kernel,
         name="main",
         out_shape=(
             jax.ShapeDtypeStruct((ROWS, WIDTH), BF16),
-            jax.ShapeDtypeStruct((REPL, 2, 8, BW), F32),
-            jax.ShapeDtypeStruct((2, REPL, 8, 128), F32),
+            jax.ShapeDtypeStruct((2, REPL, STAGES + 1, 8, 128), F32),
         ),
         in_specs=[hbm] * 7,
-        out_specs=(hbm,) * 3,
+        out_specs=(hbm,) * 2,
         scratch_shapes=[
             pltpu.VMEM((2, HALF), F32),
             pltpu.VMEM((1, HALF), F32),
@@ -722,12 +704,13 @@
             pltpu.VMEM((8, 128), F32),
             pltpu.VMEM((DEPTH, 8, 128), F32),
             pltpu.VMEM((8, 128), F32),
+            pltpu.VMEM((2, STAGES + 1, 8, 128), F32),
             pltpu.VMEM((SPAN, HALF), BF16),
-            dma((12,)), dma((7,)), dma((7,)),
+            dma((10,)), dma((7,)), dma((7,)),
             dma, dma, dma, dma, dma((2,)), dma((6,)), dma, dma,
             dma((STAGES,)), dma((STAGES,)), dma, dma, dma((STAGES,)), dma((STAGES,)),
             dma((2,)), dma((2,)), dma((2,)), dma((2,)),
-            dma((STAGES,)), dma((STAGES,)), dma((STAGES + 1,)), dma((STAGES + 1,)),
+            dma((STAGES,)), dma((STAGES,)), dma, dma,
         ],
         compiler_params=pltpu.CompilerParams(
             collective_id=0, has_side_effects=True, vmem_limit_bytes=60 * 2**20
@@ -747,11 +730,10 @@
             jax.ShapeDtypeStruct((4, WIDTH), F32),
             jax.ShapeDtypeStruct((1, WIDTH), F32),
         ),
-        in_specs=[hbm] * 3,
+        in_specs=[hbm] * 2,
         out_specs=(hbm,) * 6,
         scratch_shapes=[
-            pltpu.VMEM((REPL, 2, 8, BW), F32),
-            pltpu.VMEM((2, REPL, 8, 128), F32),
+            pltpu.VMEM((2, REPL, STAGES + 1, 8, 128), F32),
             pltpu.VMEM((2, 128, 128), F32),
             pltpu.VMEM((8, 2, 8, BW), F32),
             pltpu.VMEM((1, WIDTH), F32),
@@ -759,11 +741,11 @@
             pltpu.VMEM((4, WIDTH), F32),
             pltpu.VMEM((1, WIDTH), F32),
             pltpu.VMEM((ROWS, WIDTH), BF16),
-            dma((6,)),
+            dma((5,)),
             dma((9,)),
         ],
         compiler_params=pltpu.CompilerParams(vmem_limit_bytes=60 * 2**20),
-    )(gi, packed, small)
+    )(gi, done)
     return gi, gw, dec.reshape(WIDTH), bias, taps, shift.reshape(WIDTH)
 
 

time: 60.9 us -> 60.2 us (0.989)
    pallas_call x1, Pallas kernels: 58.1 us -> 57.4 us  [per_device(): pl.pallas_call(main_kernel, name='main', out_shape=(jax.ShapeDtypeStruct(...]
where the time goes in v9:
time: 60.2 us; the launch traced here: 60.1 us
  Pallas kernels  59.5 us (99%)
  between operations  0.64 us (1%)
    pallas_call x1, Pallas kernels, per_device(): pl.pallas_call(main_kernel, name='main', out_shape=(jax.ShapeDtypeStruct(...  57.4 us
    pallas_call x1, Pallas kernels, per_device(): pl.pallas_call(last_kernel, name='last', out_shape=(jax.ShapeDtypeStruct(...  2.02 us

profile of v9, /device:TPU:1, one launch (start us, length us, event | category | flops | bytes accessed | tf_op | source)
XLA Modules:
  0.0 60.1 jit_solution(11291528877926647795)
XLA Ops:
  0.6 57.4 %main.1 = (bf16[128,2048]{1,0:T(8,128)(2,1)}, f32[2,8,3,8,128]{4,3,2,1,0:T(8,128)}) custom-call(bf16[1,128,2048]{2,1,0:T(8,128)(2,1)} %x_hbm.1, bf16[8,2,8,256]{3,2,1,0:T(8,128)(2,1)} %w_hbm.1, f32[2,2048]{1,0:T(2,128)} %gb_hbm.1, f32[1,2048]{1,0:T(1,128)} %bitcast.4, f32[4,2048]{1,0:T(4,128)} %cw_hbm.1, f32[1,2048]{1,0:T(1,128)} %bitcast.5, ...), custom_call_target="tpu_custom_call" | custom-call | tf_op jit(solution)/shard_map/main/pallas_call | solution.py:655
  58.1 2.0 %last.1 = (bf16[1,128,2048]{2,1,0:T(8,128)(2,1)}, f32[8,2,8,256]{3,2,1,0:T(8,128)}, f32[1,2048]{1,0:T(1,128)}, f32[2,2048]{1,0:T(2,128)}, f32[4,2048]{1,0:T(4,128)}, /*index=5*/f32[1,2048]{1,0:T(1,128)}) custom-call(bf16[128,2048]{1,0:T(8,128)(2,1)} %get-tuple-element.14.gi_in, f32[2,8,3,8,128]{4,3,2,1,0:T(8,128)} %get-tuple-element.15.done_in), custom_call_target="tpu_custom_call" | custom-call | tf_op jit(solution)/shard_map/last/pallas_call | solution.py:722

commit v10 on v9

--- a/solution.py
+++ b/solution.py
@@ -56,7 +56,7 @@
 def main_kernel(
     x_hbm, w_hbm, gb_hbm, lam_hbm, cw_hbm, cb_hbm, cot_hbm,
     gi_hbm, done_hbm,
-    gb_ref, lam_ref, cw_ref, cb_ref, xb, cotb, wsh, wf, wu, wpair, W0, W1, xhalo, nat, natc, xs, cs, mb, mt, pre,
+    gb_ref, lam_ref, cw_ref, cb_ref, xb, cotb, wsh, wf, wu, column, wpair, W0, W1, xhalo, nat, natc, xs, cs, mb, mt, pre,
     dec, pp, qq, m1, m2, m3, oma, hp, gp, gm, dsend, drecv, sin, ghs, ghr,
     wsend, wz, frecv, brecv, bsum, bz, own, fsum, zrecv, ssend, srecv, ssum, szrecv, fin, done, gib,
     lsem, sib_s, sib_r, c1_s, c1_r, hal_s, hal_r, za_s, za_r, c2_s, c2_r, d_s, d_r, e_s, e_r,
@@ -115,6 +115,11 @@
         dev = {"ctx": 2 * p + 1 - c, "dp": rem(d + j, REPL)}
         pl.semaphore_signal(bar, inc=1, device_id=dev, device_id_type=MESH)
 
+    @pl.loop(1, DEPTH, unroll=True)
+    def _(j):
+        dev = {"ctx": 2 * (p - z + rem(z + j, DEPTH)) + 1 - c, "dp": d}
+        pl.semaphore_signal(bar, inc=1, device_id=dev, device_id_type=MESH)
+
     mine = pl.ds(pl.multiple_of(HALF * c, HALF), HALF)
     theirs = pl.ds(pl.multiple_of(HALF * (1 - c), HALF), HALF)
     my_rows = pl.ds(pl.multiple_of(ROWS * c, ROWS), ROWS)
@@ -150,28 +155,25 @@
                 first = ((u // 2) % 2) * 8 + 4 * h + 2 * st + u // 4
                 wu[h, st, u] = wf[u % 2, pl.ds(first, 8, stride=16), :]
 
-    pl.semaphore_wait(bar, 1 + (CHIPS - 1) + (PLANE - 2) + (REPL - 1))
+    pl.semaphore_wait(bar, 1 + (CHIPS - 1) + (PLANE - 2) + (REPL - 1) + (DEPTH - 1))
 
     part = pl.ds(pl.multiple_of(8 * c, 8), 8)
-    s_w = send(wu.at[1 - c, 1, d], wpair.at[0, part], sib_s.at[0], sib_r.at[0], sibling)
-    s_v = send(wu.at[1 - c, 0], wpair.at[pl.ds(1, REPL), part], sib_s.at[5], sib_r.at[5], sibling)
-    wpair[0, part, :] = wu[c, 1, d]
-    s_w.wait_recv()
-    mine_w = W0.at[d, y_hi, rows16(z)]
-    mine_w[...] = wpair[0].astype(BF16)
-
-    @pl.loop(1, DEPTH, unroll=True)
-    def _(j):
-        send(mine_w, mine_w, c1_s, c1_r, deep(rem(z + j, DEPTH)))
-
+    @pl.loop(1, 2 * DEPTH, unroll=True)
+    def _(j):
+        to_c, to_z = rem(c + div(j, DEPTH), 2), rem(z + j, DEPTH)
+        dev = {"ctx": 2 * (p - z + to_z) + to_c, "dp": d}
+        send(wu.at[to_c, 1, d], column.at[z, c], c1_s, c1_r, dev)
+
+    column[z, c] = wu[c, 1, d]
+    s_v = send(wu.at[1 - c, 0], wpair.at[:, part], sib_s.at[5], sib_r.at[5], sibling)
     s_x = send(x_hbm.at[0, :, theirs], xb.at[my_rows], sib_s.at[1], sib_r.at[1], sibling)
     s_c = send(cot_hbm.at[0, :, theirs], cotb.at[my_rows], sib_s.at[2], sib_r.at[2], sibling)
-    seven = W1.at[0, pl.ds(0, DEPTH - 1)]
-    later(seven, c1_s)
-    wpair[1:, part, :] = wu[c, 0]
+    others = srecv.at[pl.ds(0, 2 * DEPTH - 1)]
+    later(others, c1_s)
+    wpair[:, part, :] = wu[c, 0]
     s_v.wait_recv()
     for u in range(REPL):
-        W1[p, u] = wpair[1 + u].astype(BF16)
+        W1[p, u] = wpair[u].astype(BF16)
     across = rem(p + DEPTH, CHIPS)
     rows_a, rows_b = W1.at[p], W1.at[across]
     send(rows_a, rows_a, za_s.at[0], za_r.at[0], chip(across))
@@ -205,7 +207,7 @@
     for k in range(TILES):
         nat[k] = xb[:, lane_tile(k)].astype(F32)
 
-    @pl.loop(0, R)
+    @pl.loop(0, R, unroll=2)
     def _(r):
         for k in range(TILES):
             xs[3 + r, :, lane_tile(k)] = nat[k, pl.ds(r, 8, stride=R), :]
@@ -215,7 +217,8 @@
     near(1)
     later(W1.at[pl.ds(0, 14)], za_s.at[1])
     ten = W1.at[pl.ds(0, 10)]
-    wait_for(seven, c1_r)
+    wait_for(others, c1_r)
+    W0[d, y_hi] = column[...].reshape(128, 128).astype(BF16)
     fifteen = frecv.at[0, pl.ds(0, PLANE - 1)]
     mine_s = W0.at[d, y_hi]
 
@@ -231,7 +234,7 @@
     for k in range(TILES):
         natc[k] = cotb[:, lane_tile(k)].astype(F32)
 
-    @pl.loop(0, R)
+    @pl.loop(0, R, unroll=2)
     def _(r):
         for k in range(TILES):
             cs[r, :, lane_tile(k)] = natc[k, pl.ds(r, 8, stride=R), :]
@@ -252,7 +255,7 @@
         taps = [jnp.broadcast_to(conv_w[k : k + 1, block(b)], (8, BW)) for k in range(4)]
         shift = jnp.broadcast_to(conv_b[:, block(b)], (8, BW))
 
-        @pl.loop(0, R // 2)
+        @pl.loop(0, R // 2, unroll=2)
         def _(i):
             v = [xs[2 * i + k, :, block(b)] for k in range(5)]
             out = []
@@ -512,7 +515,7 @@
     for b in range(NB):
         taps = [jnp.broadcast_to(conv_w[k : k + 1, block(b)], (8, BW)) for k in range(4)]
 
-        @pl.loop(0, R)
+        @pl.loop(0, R, unroll=4)
         def _(r):
             v = taps[0] * gm[r + 3, :, block(b)]
             for k in range(1, 4):
@@ -601,7 +604,7 @@
     triples = frecv.at[0, pl.ds(0, 2 * REPL - 1), pl.ds(0, 48)]
     later(triples, g_s)
     later(triples, g_r)
-    for cp in [s_w, s_v, s_x, s_c, s_g]:
+    for cp in [s_v, s_x, s_c, s_g]:
         cp.wait_send()
     s_g.wait_recv()
     for finish_one in pending:
@@ -671,7 +674,8 @@
             pltpu.VMEM((8, 2, 8, BW), BF16),
             pltpu.VMEM((2, 128, 128), F32),
             pltpu.VMEM((2, STAGES, REPL, 8, 128), F32),
-            pltpu.VMEM((1 + REPL, 16, 128), F32),
+            pltpu.VMEM((DEPTH, 2, 8, 128), F32),
+            pltpu.VMEM((REPL, 16, 128), F32),
             pltpu.VMEM((REPL, 2, 128, 128), BF16),
             pltpu.VMEM((CHIPS, REPL, 16, 128), BF16),
             pltpu.VMEM((16, HALF), BF16),

time: 60.2 us -> 58.7 us (0.975)
  Pallas kernels: 59.5 us -> 57.9 us
    pallas_call x1, Pallas kernels: 57.4 us -> 55.9 us  [per_device(): pl.pallas_call(main_kernel, name='main', out_shape=(jax.ShapeDtypeStruct(...]
where the time goes in v10:
time: 58.7 us; the launch traced here: 58.6 us
  Pallas kernels  57.9 us (99%)
  between operations  0.64 us (1%)
    pallas_call x1, Pallas kernels, per_device(): pl.pallas_call(main_kernel, name='main', out_shape=(jax.ShapeDtypeStruct(...  55.9 us
    pallas_call x1, Pallas kernels, per_device(): pl.pallas_call(last_kernel, name='last', out_shape=(jax.ShapeDtypeStruct(...  2.02 us

profile of v10, /device:TPU:1, one launch (start us, length us, event | category | flops | bytes accessed | tf_op | source)
XLA Modules:
  0.0 58.6 jit_solution(12243686942794154530)
XLA Ops:
  0.6 55.9 %main.1 = (bf16[128,2048]{1,0:T(8,128)(2,1)}, f32[2,8,3,8,128]{4,3,2,1,0:T(8,128)}) custom-call(bf16[1,128,2048]{2,1,0:T(8,128)(2,1)} %x_hbm.1, bf16[8,2,8,256]{3,2,1,0:T(8,128)(2,1)} %w_hbm.1, f32[2,2048]{1,0:T(2,128)} %gb_hbm.1, f32[1,2048]{1,0:T(1,128)} %bitcast.4, f32[4,2048]{1,0:T(4,128)} %cw_hbm.1, f32[1,2048]{1,0:T(1,128)} %bitcast.5, ...), custom_call_target="tpu_custom_call" | custom-call | tf_op jit(solution)/shard_map/main/pallas_call | solution.py:658
  56.5 2.0 %last.1 = (bf16[1,128,2048]{2,1,0:T(8,128)(2,1)}, f32[8,2,8,256]{3,2,1,0:T(8,128)}, f32[1,2048]{1,0:T(1,128)}, f32[2,2048]{1,0:T(2,128)}, f32[4,2048]{1,0:T(4,128)}, /*index=5*/f32[1,2048]{1,0:T(1,128)}) custom-call(bf16[128,2048]{1,0:T(8,128)(2,1)} %get-tuple-element.14.gi_in, f32[2,8,3,8,128]{4,3,2,1,0:T(8,128)} %get-tuple-element.15.done_in), custom_call_target="tpu_custom_call" | custom-call | tf_op jit(solution)/shard_map/last/pallas_call | solution.py:726

commit v11 on v10

--- a/solution.py
+++ b/solution.py
@@ -505,6 +505,37 @@
         zrecv[st, z] = fsum[st, z]
 
     pl.when(y_odd == 0)(lambda: fold(0))
+    wait_for(brecv.at[pl.ds(0, DEPTH - 1)], b_r.at[0])
+    for h in range(2):
+        for t in range(4):
+            v = brecv[0, h, t].astype(F32)
+            for j in range(1, DEPTH):
+                v = v + brecv[j, h, t].astype(F32)
+            bsum[h, t] = v.astype(BF16)
+
+    @pl.loop(1, PLANE, unroll=True)
+    def _(j):
+        dev, to_h, to_d = plane(j)
+
+        @pl.when(to_d >= 4)
+        def _():
+            send(bsum.at[to_h, rem(to_d, 4)], bz.at[spot], b_s.at[1], b_r.at[1], dev)
+
+    @pl.when(y_odd == 1)
+    def _():
+        bz[spot] = bsum[y_hi, x]
+
+    fold(1)
+    wait_for(srecv.at[pl.ds(0, PLANE - 1)], fs_r.at[0])
+    ssum[...] = jnp.sum(srecv[...], 0)
+
+    @pl.loop(1, DEPTH, unroll=True)
+    def _(j):
+        send(ssum, szrecv.at[z], fs_s.at[1], fs_r.at[1], deep(rem(z + j, DEPTH)))
+
+    later(szrecv.at[pl.ds(0, DEPTH - 1)], fs_s.at[1])
+    szrecv[z] = ssum[...]
+
     wait_for(ghr, e_r)
     halo = ghr[...]
     halo = jnp.where(p == CHIPS - 1, jnp.zeros_like(halo), halo)
@@ -529,37 +560,6 @@
     st_g = pltpu.make_async_copy(gib.at[my_rows], gi_hbm.at[:, mine], lsem.at[3])
     st_g.start()
     later(gib.at[my_rows], lsem.at[3])
-    wait_for(brecv.at[pl.ds(0, DEPTH - 1)], b_r.at[0])
-    for h in range(2):
-        for t in range(4):
-            v = brecv[0, h, t].astype(F32)
-            for j in range(1, DEPTH):
-                v = v + brecv[j, h, t].astype(F32)
-            bsum[h, t] = v.astype(BF16)
-
-    @pl.loop(1, PLANE, unroll=True)
-    def _(j):
-        dev, to_h, to_d = plane(j)
-
-        @pl.when(to_d >= 4)
-        def _():
-            send(bsum.at[to_h, rem(to_d, 4)], bz.at[spot], b_s.at[1], b_r.at[1], dev)
-
-    @pl.when(y_odd == 1)
-    def _():
-        bz[spot] = bsum[y_hi, x]
-
-    fold(1)
-    wait_for(srecv.at[pl.ds(0, PLANE - 1)], fs_r.at[0])
-    ssum[...] = jnp.sum(srecv[...], 0)
-
-    @pl.loop(1, DEPTH, unroll=True)
-    def _(j):
-        send(ssum, szrecv.at[z], fs_s.at[1], fs_r.at[1], deep(rem(z + j, DEPTH)))
-
-    later(szrecv.at[pl.ds(0, DEPTH - 1)], fs_s.at[1])
-    szrecv[z] = ssum[...]
-
     later(zrecv.at[1, pl.ds(0, DEPTH - 1)], z_s.at[1])
 
     @pl.when(y_odd == 0)

time: 58.7 us -> 57.7 us (0.983)
  Pallas kernels: 57.9 us -> 56.9 us
    pallas_call x1, Pallas kernels: 55.9 us -> 54.9 us  [per_device(): pl.pallas_call(main_kernel, name='main', out_shape=(jax.ShapeDtypeStruct(...]
where the time goes in v11:
time: 57.7 us; the launch traced here: 57.6 us
  Pallas kernels  56.9 us (99%)
  between operations  0.64 us (1%)
    pallas_call x1, Pallas kernels, per_device(): pl.pallas_call(main_kernel, name='main', out_shape=(jax.ShapeDtypeStruct(...  54.9 us
    pallas_call x1, Pallas kernels, per_device(): pl.pallas_call(last_kernel, name='last', out_shape=(jax.ShapeDtypeStruct(...  2.02 us

profile of v11, /device:TPU:1, one launch (start us, length us, event | category | flops | bytes accessed | tf_op | source)
XLA Modules:
  0.0 57.6 jit_solution(14919379756605753586)
XLA Ops:
  0.6 54.9 %main.1 = (bf16[128,2048]{1,0:T(8,128)(2,1)}, f32[2,8,3,8,128]{4,3,2,1,0:T(8,128)}) custom-call(bf16[1,128,2048]{2,1,0:T(8,128)(2,1)} %x_hbm.1, bf16[8,2,8,256]{3,2,1,0:T(8,128)(2,1)} %w_hbm.1, f32[2,2048]{1,0:T(2,128)} %gb_hbm.1, f32[1,2048]{1,0:T(1,128)} %bitcast.4, f32[4,2048]{1,0:T(4,128)} %cw_hbm.1, f32[1,2048]{1,0:T(1,128)} %bitcast.5, ...), custom_call_target="tpu_custom_call" | custom-call | tf_op jit(solution)/shard_map/main/pallas_call | solution.py:658
  55.6 2.0 %last.1 = (bf16[1,128,2048]{2,1,0:T(8,128)(2,1)}, f32[8,2,8,256]{3,2,1,0:T(8,128)}, f32[1,2048]{1,0:T(1,128)}, f32[2,2048]{1,0:T(2,128)}, f32[4,2048]{1,0:T(4,128)}, /*index=5*/f32[1,2048]{1,0:T(1,128)}) custom-call(bf16[128,2048]{1,0:T(8,128)(2,1)} %get-tuple-element.14.gi_in, f32[2,8,3,8,128]{4,3,2,1,0:T(8,128)} %get-tuple-element.15.done_in), custom_call_target="tpu_custom_call" | custom-call | tf_op jit(solution)/shard_map/last/pallas_call | solution.py:726

commit v12 on v11

--- a/solution.py
+++ b/solution.py
@@ -470,9 +470,10 @@
             to_plane(False)
             later(fifteen, f_s.at[1])
             frecv[1, spot] = wsend[1, d, y_hi]
-        for b in (2 * st, 2 * st + 1):
-            through(b)
-            small_sums(b)
+
+    for b in range(NB):
+        through(b)
+        small_sums(b)
 
     @pl.loop(1, PLANE, unroll=True)
     def _(j):
@@ -489,7 +490,7 @@
     def fold(st):
         wait_for(fifteen, f_r.at[st])
 
-        @pl.loop(0, DEPTH)
+        @pl.loop(0, DEPTH, unroll=4)
         def _(i):
             at = rows16(i)
             v = frecv[st, 0, at, :].astype(F32)

time: 57.7 us -> 57.7 us (level)
  no operation moved by 1% of the time
where the time goes in v12:
time: 57.7 us; the launch traced here: 57.5 us
  Pallas kernels  56.9 us (99%)
  between operations  0.64 us (1%)
    pallas_call x1, Pallas kernels, per_device(): pl.pallas_call(main_kernel, name='main', out_shape=(jax.ShapeDtypeStruct(...  54.9 us
    pallas_call x1, Pallas kernels, per_device(): pl.pallas_call(last_kernel, name='last', out_shape=(jax.ShapeDtypeStruct(...  2.02 us

profile of v12, /device:TPU:1, one launch (start us, length us, event | category | flops | bytes accessed | tf_op | source)
XLA Modules:
  0.0 57.5 jit_solution(12247171729055441754)
XLA Ops:
  0.6 54.9 %main.1 = (bf16[128,2048]{1,0:T(8,128)(2,1)}, f32[2,8,3,8,128]{4,3,2,1,0:T(8,128)}) custom-call(bf16[1,128,2048]{2,1,0:T(8,128)(2,1)} %x_hbm.1, bf16[8,2,8,256]{3,2,1,0:T(8,128)(2,1)} %w_hbm.1, f32[2,2048]{1,0:T(2,128)} %gb_hbm.1, f32[1,2048]{1,0:T(1,128)} %bitcast.4, f32[4,2048]{1,0:T(4,128)} %cw_hbm.1, f32[1,2048]{1,0:T(1,128)} %bitcast.5, ...), custom_call_target="tpu_custom_call" | custom-call | tf_op jit(solution)/shard_map/main/pallas_call | solution.py:659
  55.5 2.0 %last.1 = (bf16[1,128,2048]{2,1,0:T(8,128)(2,1)}, f32[8,2,8,256]{3,2,1,0:T(8,128)}, f32[1,2048]{1,0:T(1,128)}, f32[2,2048]{1,0:T(2,128)}, f32[4,2048]{1,0:T(4,128)}, /*index=5*/f32[1,2048]{1,0:T(1,128)}) custom-call(bf16[128,2048]{1,0:T(8,128)(2,1)} %get-tuple-element.14.gi_in, f32[2,8,3,8,128]{4,3,2,1,0:T(8,128)} %get-tuple-element.15.done_in), custom_call_target="tpu_custom_call" | custom-call | tf_op jit(solution)/shard_map/last/pallas_call | solution.py:727
